TPU v7x, 32 devices: a whole 2x2x4 slice. The times are simulated.
32 devices in a mesh: chan: 4 (over y, x), tm: 8 (over z, core).
Axes of the slice: x: 2, y: 2, z: 4, core: 2. Of those that a mesh axis runs over, the one named last changes fastest.
Arguments:
- records: bfloat16 [352, 512, 1024], P('tm', 'chan'), may hold values from -2000 to 2000, as said below
Outputs:
- cross_near: float32 [32, 2, 2, 512, 2, 128], P('tm', None, None, 'chan')
- cross_far: float32 [32, 512, 2, 128], P('tm', 'chan')
Inputs may be any that keep to these rules, and one draw needn't show every extreme that they name: Raw strain-rate records.
All inputs are finite; a program needn't handle non-finite values.
Results may differ from a plain program's by a relative error of at most 0.009.
Values may be sent and summed in bfloat16 or wider, within the bound.
No kernel may reach another device: no remote copies, remote signals or barrier semaphores. Data moves between devices by JAX's collectives and lax.ppermute only.
A program may use at most 128 MiB of HBM per device.

v0:
```python
import math

import jax
import jax.numpy as jnp
from jax import lax
from jax.sharding import PartitionSpec as P

FREQS = 64
FIRST_BIN = 32


EPSILON = 1e-06


def shifted(value, axis, steps):
    count = lax.axis_size(axis)
    pairs = [(source, (source + steps) % count) for source in range(count)]
    return lax.ppermute(value, axis, pairs)


def dft_table(sample_count, frequency_count, first_bin):
    positions = jnp.arange(sample_count, dtype=jnp.int32)
    bin_numbers = jnp.arange(frequency_count, dtype=jnp.int32) + first_bin
    phase_index = bin_numbers[:, None] * positions[None, :] % sample_count
    phase_angle = 2.0 * math.pi / sample_count * phase_index.astype(jnp.float32)
    hann_taper = 0.5 - 0.5 * jnp.cos(2.0 * math.pi / sample_count * positions.astype(jnp.float32))
    cosine = hann_taper[None, :] * jnp.cos(phase_angle)
    sine_part = -hann_taper[None, :] * jnp.sin(phase_angle)
    return (
        jnp.stack([cosine, sine_part], axis=1)
        .reshape(2 * frequency_count, sample_count)
        .astype(jnp.bfloat16)
    )


def whiten(records, taper_table, overall_scale):
    spectra = jnp.einsum("ks,wcs->kwc", taper_table, records, preferred_element_type=jnp.float32)
    mean_square = jnp.mean(spectra * spectra, axis=0)
    factor = overall_scale / jnp.sqrt(mean_square + EPSILON)
    return (spectra * factor[None]).astype(jnp.bfloat16)


def pair_stack(own_blocks, mate_blocks, window_count):
    halves, freq_rows, complex_parts, windows, block_width = own_blocks.shape
    rounds = mate_blocks.shape[0]
    groups = windows // window_count
    negated = jnp.stack([own_blocks[:, :, 1], -own_blocks[:, :, 0]], axis=2)
    row_side = jnp.stack([own_blocks, negated], axis=-1).reshape(
        halves, freq_rows, complex_parts, groups, window_count, 2 * block_width
    )
    column_side = mate_blocks.reshape(
        rounds, halves, freq_rows, complex_parts, groups, window_count, block_width
    )
    partial_value = jnp.einsum(
        "hgpnwi,rhgpnwj->ghrnij", row_side, column_side, preferred_element_type=jnp.float32
    )
    rounded = lax.optimization_barrier(partial_value.astype(jnp.bfloat16)).astype(jnp.float32)
    summed = jnp.sum(rounded, axis=3)
    return summed.reshape(freq_rows, halves, rounds, block_width, 2, block_width)


def find_partners(blocks):
    chan_count = lax.axis_size("chan")
    half_count = chan_count // 2
    picked = []
    for offset in range(1, half_count + 1):
        picked.append(shifted(blocks, "chan", chan_count - offset))
    near_mates = jnp.stack([blocks] + picked[: half_count - 1], axis=0)
    return (near_mates, picked[half_count - 1])


def far_stack(own_blocks, far_partner, window_count):
    lower_half = lax.axis_index("chan") < lax.axis_size("chan") // 2
    first_block = jnp.where(lower_half, own_blocks, far_partner)
    second_block = jnp.where(lower_half, far_partner, own_blocks)
    half_pick = jnp.where(lower_half, 0, 1).astype(jnp.int32)
    first_block = lax.dynamic_slice_in_dim(first_block, half_pick, 1, 0)
    second_block = lax.dynamic_slice_in_dim(second_block, half_pick, 1, 0)
    result = pair_stack(first_block, second_block[None], window_count)
    return result.reshape(result.shape[0], result.shape[3], 2, result.shape[5])


def body(records):
    window_count = records.shape[0]
    time_count = lax.axis_size("tm")
    taper_table = dft_table(records.shape[2], FREQS, FIRST_BIN)
    whitened = whiten(records, taper_table, float(window_count * time_count) ** (-0.25))
    half_freq = FREQS // 2
    blocks = whitened.reshape(2, half_freq, 2, window_count, records.shape[1])
    blocks = lax.all_to_all(blocks, "tm", split_axis=1, concat_axis=3, tiled=True)
    near_mates, far_mate = find_partners(blocks)
    cross_near = pair_stack(blocks, near_mates, window_count)
    cross_far = far_stack(blocks, far_mate, window_count)
    return (cross_near, cross_far)


def solution(mesh):
    return jax.shard_map(
        body,
        mesh=mesh,
        in_specs=(P("tm", "chan", None),),
        out_specs=(P("tm", None, None, "chan", None, None), P("tm", "chan", None, None)),
        check_vma=False,
    )
```

profile of v0, /device:TPU:6, one launch (start us, length us, event | category | flops | bytes accessed | tf_op | source)
XLA Modules:
  0.0 170.2 jit_solution(9552204374903059683)
XLA Ops:
  0.7 1.2 multiply_convert_fusion.2
  2.4 6.8 %multiply_reduce_fusion = (f32[44,128]{1,0:T(8,128)S(1)}, f32[128,44,128]{2,0,1:T(8,128)S(1)}) fusion(bf16[128,1024,1]{1,0,2:T(8,128)(2,1)S(1)} %reshape.200, bf16[44,128,1024]{2,1,0:T(8,128)(2,1)} %param.1), kind=kOutput, calls=%fused_computation.13 | convolution fusion | flops 1477831168 | bytes 14702592 | tf_op jit(solution)/shard_map/ks,wcs->kwc/dot_general | solution.py:37
  9.6 1.0 copy.66
  10.6 39.7 %all_to_all.18 = bf16[2,32,2,44,128]{4,2,3,0,1:T(2,128)(2,1)S(1)} all-to-all(bf16[2,32,2,44,128]{4,2,3,0,1:T(2,128)(2,1)S(1)} %copy.66), channel_id=1, replica_groups=mesh['chan'=4,'tm'=8] {'tm'}, dimensions={1} | all-to-all | bytes 2883584 | tf_op jit(solution)/shard_map/all_to_all | solution.py:90
  50.6 1.1 copy.69
  52.8 2.7 %fusion.21 = (bf16[2,4,1,352,128]{4,2,3,1,0:T(2,128)(2,1)S(1)}, bf16[2,4,1,352,128]{4,2,3,1,0:T(2,128)(2,1)S(1)}) fusion(bf16[2,4,2,352,128]{4,2,3,1,0:T(2,128)(2,1)S(1)} %bitcast.45), kind=kLoop, calls=%fused_computation.42 | loop fusion | flops 360448 | bytes 2883584 | tf_op jit(solution)/shard_map/slice | solution.py:47
  55.5 3.3 %maximum_bitcast_fusion = bf16[2,4,2,352,128,1]{4,2,3,1,0,5:T(2,128)(2,1)S(1)} fusion(bf16[2,4,1,352,128]{4,2,3,1,0:T(2,128)(2,1)S(1)} %get-tuple-element.9, bf16[2,4,1,352,128]{4,2,3,1,0:T(2,128)(2,1)S(1)} %get-tuple-element.8), kind=kLoop, calls=%fused_computation.18 | loop fusion | flops 2883584 | bytes 2883584 | tf_op jit(solution)/shard_map/stack | solution.py:48
  58.8 5.8 %pad_maximum_fusion = bf16[2,4,2,352,128,2]{4,2,3,1,0,5:T(2,128)(2,1)} fusion(bf16[2,4,2,352,128,1]{4,2,3,1,0,5:T(2,128)(2,1)S(1)} %maximum_bitcast_fusion, bf16[2,4,2,352,128,1]{4,2,3,1,0,5:T(2,128)(2,1)S(1)} %bitcast.46), kind=kLoop, calls=%fused_computation.11 | loop fusion | flops 1441792 | bytes 5767168 | tf_op jit(solution)/shard_map/stack | solution.py:48
  64.5 15.2 %copy.72 = bf16[2,4,2,352,128,2]{3,5,4,2,1,0:T(2,128)(2,1)} copy(bf16[2,4,2,352,128,2]{4,2,3,1,0,5:T(2,128)(2,1)} %pad_maximum_fusion) | data formatting | bytes 5767168 | tf_op jit(solution)/shard_map/stack | solution.py:48
  79.8 13.7 %reshape.196 = bf16[2,4,2,8,44,256]{4,3,5,2,1,0:T(8,128)(2,1)} reshape(bf16[2,4,2,352,128,2]{3,5,4,2,1,0:T(2,128)(2,1)} %copy.72) | data formatting | bytes 5767168 | tf_op jit(solution)/shard_map/reshape | solution.py:48
  93.5 22.5 %collective-permute-done.1 = bf16[2,4,2,352,128]{4,2,3,1,0:T(2,128)(2,1)} collective-permute-done((bf16[2,4,2,352,128]{4,2,3,1,0:T(2,128)(2,1)S(1)}, bf16[2,4,2,352,128]{4,2,3,1,0:T(2,128)(2,1)}, u32[]{:S(2)}, u32[]{:S(2)}) %collective-permute-start.1) | collective-permute-done | bytes 1441824 | tf_op jit(solution)/shard_map/ppermute | solution.py:18
  115.9 3.2 %broadcast_select_fusion.1 = (bf16[1,4,2,352,128]{4,2,3,1,0:T(2,128)(2,1)}, bf16[1,4,2,352,128]{4,2,3,1,0:T(2,128)(2,1)S(1)}) fusion(pred[]{:T(512)S(6)} %lt.14, bf16[2,4,2,352,128]{4,2,3,1,0:T(2,128)(2,1)S(1)} %bitcast.47, s32[]{:T(128)S(6)} %select_n.41, bf16[2,4,2,352,128]{4,2,3,1,0:T(2,128)(2,1)} %collective-permute-done.1), kind=kLoop, calls=%fused_computation.21 | loop fusion | flops 720896 | bytes 2883589 | tf_op jit(solution)/shard_map/jit(_where)/select_n | solution.py:75
  119.1 1.3 fusion.22
  120.4 1.5 maximum_bitcast_fusion.1
  121.9 3.3 %pad_maximum_fusion.1 = bf16[1,4,2,352,128,2]{4,2,3,1,5,0:T(2,128)(2,1)} fusion(bf16[1,4,2,352,128,1]{4,2,3,1,5,0:T(2,128)(2,1)S(1)} %maximum_bitcast_fusion.1, bf16[1,4,2,352,128,1]{4,2,3,1,5,0:T(2,128)(2,1)S(1)} %bitcast.50), kind=kLoop, calls=%fused_computation.19 | loop fusion | flops 720896 | bytes 2883584 | tf_op jit(solution)/shard_map/stack | solution.py:48
  125.2 8.1 %copy.75 = bf16[1,4,2,352,128,2]{3,5,4,2,1,0:T(2,128)(2,1)} copy(bf16[1,4,2,352,128,2]{4,2,3,1,5,0:T(2,128)(2,1)} %pad_maximum_fusion.1) | data formatting | bytes 2883584 | tf_op jit(solution)/shard_map/stack | solution.py:48
  133.3 1.6 copy.70
  135.0 7.6 %reshape.199 = bf16[4,2,8,44,256]{3,2,4,1,0:T(8,128)(2,1)} reshape(bf16[1,4,2,352,128,2]{3,5,4,2,1,0:T(2,128)(2,1)} %copy.75) | data formatting | bytes 2883584 | tf_op jit(solution)/shard_map/reshape.3
  142.5 3.9 %fusion.9 = bf16[4,1,1,8,256,128]{4,5,3,0,2,1:T(8,128)(2,1)S(1)} fusion(bf16[4,2,8,44,256]{3,2,4,1,0:T(8,128)(2,1)} %reshape.199, bf16[4,2,8,44,128]{4,1,3,2,0:T(2,128)(2,1)} %bitcast.53), kind=kOutput, calls=%fused_computation.14 | convolution fusion | flops 185597952 | bytes 4259840 | tf_op jit(solution)/shard_map/hgpnwi,rhgpnwj->ghrnij/dot_general | solution.py:54
  146.5 1.1 convert_reduce_fusion.1
  147.6 2.0 %copy.78 = f32[4,256,128]{2,1,0:T(8,128)} copy(f32[4,256,128]{1,2,0:T(8,128)} %convert_reduce_fusion.1) | data formatting | bytes 1048576 | tf_op jit(solution)/shard_map/reduce_sum | solution.py:58
  149.6 11.2 %fusion.1 = bf16[4,2,2,8,256,128]{4,5,2,3,1,0:T(8,128)(2,1)} fusion(bf16[2,4,2,8,44,256,1]{4,3,5,2,1,0,6:T(8,128)(2,1)} %bitcast.42, bf16[1,2,4,2,8,44,128]{6,5,3,0,4,1,2:T(8,128)(2,1)S(1)} %copy.70, bf16[1,2,4,2,8,44,128]{6,5,3,0,4,1,2:T(8,128)(2,1)S(1)} %bitcast.49), kind=kOutput, calls=%fused_computation.3 | convolution fusion | flops 743833600 | bytes 14155776 | tf_op jit(solution)/shard_map/hgpnwi,rhgpnwj->ghrnij/dot_general | solution.py:54
  160.8 6.4 %convert_reduce_fusion = f32[4,2,2,256,128]{3,4,2,1,0:T(8,128)} fusion(bf16[4,2,2,8,256,128]{4,5,2,3,1,0:T(8,128)(2,1)} %fusion.1), kind=kLoop, calls=%fused_computation.1 | loop fusion | flops 7864320 | bytes 10485760 | tf_op jit(solution)/shard_map/reduce_sum | solution.py:58
  167.3 2.9 %copy.74 = f32[4,2,2,256,128]{4,3,2,1,0:T(8,128)} copy(f32[4,2,2,256,128]{3,4,2,1,0:T(8,128)} %convert_reduce_fusion) | data formatting | bytes 4194304 | tf_op jit(solution)/shard_map/reduce_sum | solution.py:58
  (11 shorter events, 2.3 us)
Async XLA Ops:
  51.7 64.2 %collective-permute-start.1 = (bf16[2,4,2,352,128]{4,2,3,1,0:T(2,128)(2,1)S(1)}, bf16[2,4,2,352,128]{4,2,3,1,0:T(2,128)(2,1)}, u32[]{:S(2)}, u32[]{:S(2)}) collective-permute-start(bf16[2,4,2,352,128]{4,2,3,1,0:T(2,128)(2,1)S(1)} %bitcast.43), channel_id=1, source_target_pairs={{0,16},{8,24},{16,0},{24,8},{1,17},{9,25},{17,1},{25,9},{2,18},{10... | collective-permute-start | bytes 4325384 | tf_op jit(solution)/shard_map/ppermute | solution.py:18
  52.3 81.0 %collective-permute-start = (bf16[2,4,2,352,128]{4,2,3,1,0:T(2,128)(2,1)S(1)}, bf16[2,4,2,352,128]{4,2,3,1,0:T(2,128)(2,1)}, u32[]{:S(2)}, u32[]{:S(2)}) collective-permute-start(bf16[2,4,2,352,128]{4,2,3,1,0:T(2,128)(2,1)S(1)} %bitcast.44), channel_id=1, source_target_pairs={{0,24},{8,0},{16,8},{24,16},{1,25},{9,1},{17,9},{25,17},{2,26},{10... | collective-permute-start | bytes 4325384 | tf_op jit(solution)/shard_map/ppermute | solution.py:18
where the time goes:
time: 172 us; the launch traced here: 170 us
  local copies, waits for them, and re-layouts  53.9 us (31%)
  blocking collectives  39.7 us (23%)
  other arithmetic  30.3 us (18%)
  waiting for transfers between devices  22.5 us (13%)
  matrix products  21.9 us (13%)
    all_to_all x1, blocking collectives, body(): lax.all_to_all(blocks, 'tm', split_axis=1, concat_axis=3, tiled=True)  39.7 us
    another operation x2, local copies, waits for them, and re-layouts, pair_stack(): jnp.stack([own_blocks, negated], axis=-1)  23.4 us
    ppermute x2, waiting for transfers between devices, shifted(): return lax.ppermute(value, axis, pairs)  22.5 us
    dot_general x2, matrix products, pair_stack(): jnp.einsum('hgpnwi,rhgpnwj->ghrnij', row_side, column_side, preferred_ele...  15.2 us
    another operation x4, other arithmetic, pair_stack(): jnp.stack([own_blocks, negated], axis=-1)  13.8 us
    reshape x1, local copies, waits for them, and re-layouts, pair_stack(): jnp.stack([own_blocks, negated], axis=-1)  13.7 us
    another operation x1, local copies, waits for them, and re-layouts  7.56 us
    reduce_sum x2, other arithmetic, pair_stack(): summed = jnp.sum(rounded, axis=3)  7.54 us
  transfers between devices with their start and end apart: 2, of which 1 were waited for; matrix products, arithmetic and copies ran while one was open for 34% of the time, Pallas kernels for 0%

commit v1 on v0

v1 whole, which is shorter than its diff:
```python
import functools
import math

import jax
import jax.numpy as jnp
import ml_dtypes
import numpy as np
from jax import lax
from jax.experimental import pallas as pl
from jax.experimental.pallas import tpu as pltpu
from jax.sharding import PartitionSpec as P

FREQS = 64
FIRST_BIN = 32
EPSILON = 1e-06
VMEM_LIMIT = 48 * 1024 * 1024


def dft_table(sample_count, time_count):
    half_freq = FREQS // 2
    per_device = half_freq // time_count
    positions = np.arange(sample_count)
    taper = 0.5 - 0.5 * np.cos(2.0 * math.pi / sample_count * positions)
    bins = np.arange(FREQS) + FIRST_BIN
    angle = 2.0 * math.pi / sample_count * (bins[:, None] * positions[None, :] % sample_count)
    parts = np.stack([taper * np.cos(angle), -taper * np.sin(angle)], axis=0)
    ordered = parts.reshape(2, 2, time_count, per_device, sample_count).transpose(2, 3, 0, 1, 4)
    return ordered.reshape(2 * FREQS, sample_count).astype(ml_dtypes.bfloat16)


def whiten_kernel(scale, step_windows, window_count, table_ref, records_ref, out_ref, rows_ref):
    step = pl.program_id(0)
    bins = table_ref.shape[0]
    for local in range(step_windows):
        spectra = lax.dot_general(
            table_ref[...], records_ref[local], (((1,), (1,)), ((), ())), preferred_element_type=jnp.float32
        )
        mean_square = jnp.sum(spectra * spectra, axis=0, keepdims=True) * (1.0 / bins)
        whitened = spectra * (scale / jnp.sqrt(mean_square + EPSILON))
        window = step * step_windows + local
        for row in range(0, bins, 8):
            rows_ref[pl.ds(row * window_count + window, 8, stride=window_count), :] = whitened[row : row + 8]

    @pl.when(step == pl.num_programs(0) - 1)
    def _():
        rows = out_ref.shape[1]
        for target in range(out_ref.shape[0]):
            out_ref[target] = rows_ref[target * rows : (target + 1) * rows].astype(jnp.bfloat16)


def whiten(records, time_count):
    window_count, channels, samples = records.shape
    step_windows = 4 if window_count % 4 == 0 else 1
    bins = 2 * FREQS
    rows = bins * window_count // time_count
    scale = float(window_count * time_count) ** (-0.25)
    return pl.pallas_call(
        functools.partial(whiten_kernel, scale, step_windows, window_count),
        grid=(window_count // step_windows,),
        in_specs=[
            pl.BlockSpec((bins, samples), lambda i: (0, 0)),
            pl.BlockSpec((step_windows, channels, samples), lambda i: (i, 0, 0)),
        ],
        out_specs=pl.BlockSpec((time_count, rows, channels), lambda i: (0, 0, 0)),
        out_shape=jax.ShapeDtypeStruct((time_count, rows, channels), jnp.bfloat16),
        scratch_shapes=[pltpu.VMEM((bins * window_count, channels), jnp.float32)],
        compiler_params=pltpu.CompilerParams(vmem_limit_bytes=VMEM_LIMIT),
        name="whiten",
    )(jnp.asarray(dft_table(samples, time_count)), records)


def pair_kernel(window_count, lower_ref, masks_ref, *refs):
    near_out, far_out, near_sum, far_sum = refs[-4:]
    own_ref, far_ref = refs[0], refs[-5]
    near_refs = refs[1:-5]
    groups = own_ref.shape[0]
    width = own_ref.shape[2]
    lower = lower_ref[0] > 0
    half = jnp.where(lower, 0, 1)

    def rotated(block):
        middle = block.shape[0] // 2
        return jnp.concatenate([block[middle:], block[:middle]], axis=0)

    def product(left, right):
        value = lax.dot_general(left, right, (((0,), (0,)), ((), ())), preferred_element_type=jnp.float32)
        return value.astype(jnp.bfloat16).astype(jnp.float32)

    near_total = None
    far_total = None
    for group in range(groups):
        own = own_ref[group]
        turned = rotated(own)
        left = jnp.concatenate(
            [own * masks_ref[0], turned * masks_ref[1], own * masks_ref[2], turned * masks_ref[3]], axis=1
        )
        right = jnp.concatenate([own] + [ref[group] for ref in near_refs], axis=1)
        near = product(left, right)
        far = far_ref[group]
        first = jnp.where(lower, own, far)
        second = jnp.where(lower, far, own)
        far_left = jnp.concatenate(
            [first * masks_ref[2 * half], rotated(first) * masks_ref[2 * half + 1]], axis=1
        )
        far = product(far_left, second)
        if group == 0:
            near_sum[...] = near
            far_sum[...] = far
        else:
            near_sum[...] += near
            far_sum[...] += far
    for h in range(2):
        for r in range(1 + len(near_refs)):
            for p in range(2):
                start = (2 * h + p) * width
                near_out[0, h, r, pl.ds(p, width, stride=2), :] = near_sum[
                    start : start + width, r * width : (r + 1) * width
                ]
    for p in range(2):
        far_out[0, pl.ds(p, width, stride=2), :] = far_sum[p * width : (p + 1) * width, :]


def pair_stack(own, near_mates, far_mate, window_count):
    groups, all_rows, width = own.shape
    rows = 4 * window_count
    per_device = all_rows // rows
    rounds = 1 + len(near_mates)
    lower = (lax.axis_index("chan") < lax.axis_size("chan") // 2).astype(jnp.int32).reshape(1)
    index = np.arange(rows)
    part, half = index // (2 * window_count), index // window_count % 2
    sign = np.where(part == 0, 1.0, -1.0)
    masks = np.stack([half == 0, (half == 0) * sign, half == 1, (half == 1) * sign])
    masks = np.broadcast_to(masks[:, :, None], (4, rows, width)).astype(ml_dtypes.bfloat16)
    block = pl.BlockSpec((groups, rows, width), lambda g, *_: (0, g, 0))
    return pl.pallas_call(
        functools.partial(pair_kernel, window_count),
        grid_spec=pltpu.PrefetchScalarGridSpec(
            num_scalar_prefetch=1,
            grid=(per_device,),
            in_specs=[pl.BlockSpec((4, rows, width), lambda g, *_: (0, 0, 0))] + [block] * (rounds + 1),
            out_specs=[
                pl.BlockSpec((1, 2, rounds, 2 * width, width), lambda g, *_: (g, 0, 0, 0, 0)),
                pl.BlockSpec((1, 2 * width, width), lambda g, *_: (g, 0, 0)),
            ],
            scratch_shapes=[
                pltpu.VMEM((4 * width, rounds * width), jnp.float32),
                pltpu.VMEM((2 * width, width), jnp.float32),
            ],
        ),
        out_shape=[
            jax.ShapeDtypeStruct((per_device, 2, rounds, 2 * width, width), jnp.float32),
            jax.ShapeDtypeStruct((per_device, 2 * width, width), jnp.float32),
        ],
        compiler_params=pltpu.CompilerParams(vmem_limit_bytes=VMEM_LIMIT),
        name="pair_stack",
    )(lower, jnp.asarray(masks), own, *near_mates, far_mate)


def shifted(value, steps):
    count = lax.axis_size("chan")
    return lax.ppermute(value, "chan", [(source, (source + steps) % count) for source in range(count)])


def body(records):
    window_count, width = records.shape[:2]
    time_count, chan_count = lax.axis_size("tm"), lax.axis_size("chan")
    whitened = whiten(records, time_count)
    own = lax.all_to_all(whitened, "tm", split_axis=0, concat_axis=0, tiled=True)
    mates = [shifted(own, -offset) for offset in range(1, chan_count // 2 + 1)]
    near, far = pair_stack(own, mates[:-1], mates[-1], window_count)
    near = near.reshape(near.shape[:3] + (width, 2, width))
    return near, far.reshape(far.shape[0], width, 2, width)


def solution(mesh):
    return jax.shard_map(
        body,
        mesh=mesh,
        in_specs=(P("tm", "chan", None),),
        out_specs=(P("tm", None, None, "chan", None, None), P("tm", "chan", None, None)),
        check_vma=False,
    )
```

time: 172 us -> 123 us (0.72)
  local copies, waits for them, and re-layouts: 53.9 us -> 0.95 us
  waiting for transfers between devices: 22.5 us -> 63 us
  other arithmetic: 30.3 us -> 0 us
  matrix products: 21.9 us -> 0 us
  Pallas kernels: 0 us -> 17.2 us
    ppermute x2, waiting for transfers between devices: 22.5 us -> 63 us  [shifted(): lax.ppermute(value, 'chan', [(source, (source + steps) % count) for sourc...]
    another operation x5 -> x0, local copies, waits for them, and re-layouts: 32.8 us -> none  [the longest x2 23.4 us: pair_stack(): jnp.stack([own_blocks, negated], axis=-1)]
    dot_general x3 -> x0, matrix products: 21.9 us -> none  [the longest x2 15.2 us: pair_stack(): jnp.einsum('hgpnwi,rhgpnwj->ghrnij', row_side, column_side, preferred_ele...]
    pallas_call x0 -> x2, Pallas kernels: none -> 17.2 us  [the longest x1 10.5 us: whiten(): pl.pallas_call(functools.partial(whiten_kernel, scale, step_windows, wind...]
    another operation x6 -> x0, other arithmetic: 15.1 us -> none  [the longest x4 13.8 us: pair_stack(): jnp.stack([own_blocks, negated], axis=-1)]
    reshape x2 -> x0, local copies, waits for them, and re-layouts: 14.7 us -> none  [the longest x1 13.7 us: pair_stack(): jnp.stack([own_blocks, negated], axis=-1)]
    reduce_sum x2 -> x0, other arithmetic: 7.54 us -> none  [pair_stack(): summed = jnp.sum(rounded, axis=3)]
    reduce_sum x2 -> x0, local copies, waits for them, and re-layouts: 4.91 us -> none  [pair_stack(): summed = jnp.sum(rounded, axis=3)]
  transfers between devices with their start and end apart: 2 -> 2, of which waited for: 1 -> 1; matrix products, arithmetic and copies ran while one was open for 34% -> 0% of each run, Pallas kernels for 0% -> 0%
where the time goes in v1:
time: 123 us
  waiting for transfers between devices  63 us (51%)
  blocking collectives  39.8 us (32%)
  Pallas kernels  17.2 us (14%)
    ppermute x2, waiting for transfers between devices, shifted(): lax.ppermute(value, 'chan', [(source, (source + steps) % count) for sourc...  63 us
    all_to_all x1, blocking collectives, body(): lax.all_to_all(whitened, 'tm', split_axis=0, concat_axis=0, tiled=True)  39.8 us
    pallas_call x1, Pallas kernels, whiten(): pl.pallas_call(functools.partial(whiten_kernel, scale, step_windows, wind...  10.5 us
    pallas_call x1, Pallas kernels, pair_stack(): pl.pallas_call(functools.partial(pair_kernel, window_count), grid_spec=pl...  6.69 us
  transfers between devices with their start and end apart: 2, of which 1 were waited for; matrix products, arithmetic and copies ran while one was open for 0% of the time, Pallas kernels for 0%

profile of v1, /device:TPU:6, one launch (start us, length us, event | category | flops | bytes accessed | tf_op | source)
XLA Modules:
  0.0 122.7 jit_solution(14121426577872897976)
XLA Ops:
  0.6 0.0 copy-start
  0.6 0.9 copy-done
  1.6 10.5 %whiten.1 = bf16[8,704,128]{2,1,0:T(8,128)(2,1)S(1)} custom-call(bf16[128,1024]{1,0:T(8,128)(2,1)S(1)} %copy-done, bf16[44,128,1024]{2,1,0:T(8,128)(2,1)} %records_ref.1), custom_call_target="tpu_custom_call" | custom-call | tf_op jit(solution)/shard_map/whiten/pallas_call | solution.py:57
  12.1 0.0 copy-start.1
  12.1 39.8 %all_to_all.5.refs_0_ = bf16[8,704,128]{2,1,0:T(8,128)(2,1)S(1)} all-to-all(bf16[8,704,128]{2,1,0:T(8,128)(2,1)S(1)} %whiten.1), channel_id=1, replica_groups=mesh['chan'=4,'tm'=8] {'tm'}, dimensions={0} | all-to-all | bytes 2883584 | tf_op jit(solution)/shard_map/all_to_all | solution.py:168
  51.9 0.5 collective-permute-start.1
  52.5 0.5 collective-permute-start
  53.0 63.0 %collective-permute-done.1.refs_2_ = bf16[8,704,128]{2,1,0:T(8,128)(2,1)S(1)} collective-permute-done((bf16[8,704,128]{2,1,0:T(8,128)(2,1)S(1)}, bf16[8,704,128]{2,1,0:T(8,128)(2,1)S(1)}, u32[]{:S(2)}, u32[]{:S(2)}) %collective-permute-start.1) | collective-permute-done | bytes 1441824 | tf_op jit(solution)/shard_map/ppermute | solution.py:161
  116.0 0.0 collective-permute-done.refs_1_
  116.0 0.0 copy-done.1
  116.0 6.7 %pair_stack.1 = (f32[4,2,2,256,128]{4,3,2,1,0:T(8,128)}, f32[4,256,128]{2,1,0:T(8,128)}) custom-call(s32[1]{0:T(128)} %bitcast.lower_ref, bf16[4,176,128]{2,1,0:T(8,128)(2,1)S(1)} %copy-done.1, bf16[8,704,128]{2,1,0:T(8,128)(2,1)S(1)} %all_to_all.5.refs_0_, bf16[8,704,128]{2,1,0:T(8,128)(2,1)} %collective-permute-done.refs_1_, ...), custom_call_target="tpu_custom_call" | custom-call | tf_op jit(solution)/shard_map/pair_stack/pallas_call | solution.py:135
Async XLA Ops:
  0.6 1.0 copy-start
  12.1 103.9 %copy-start.1 = (bf16[4,176,128]{2,1,0:T(8,128)(2,1)S(1)}, bf16[4,176,128]{2,1,0:T(8,128)(2,1)}, u32[]{:S(2)}) copy-start(bf16[4,176,128]{2,1,0:T(8,128)(2,1)} %constant.12.clone.masks_ref) | copy-start | bytes 540676
  51.9 64.0 %collective-permute-start.1 = (bf16[8,704,128]{2,1,0:T(8,128)(2,1)S(1)}, bf16[8,704,128]{2,1,0:T(8,128)(2,1)S(1)}, u32[]{:S(2)}, u32[]{:S(2)}) collective-permute-start(bf16[8,704,128]{2,1,0:T(8,128)(2,1)S(1)} %all_to_all.5.refs_0_), channel_id=1, source_target_pairs={{0,16},{8,24},{16,0},{24,8},{1,17},{9,25},{17,1},{25,9},{2,18},{10... | collective-permute-start | bytes 4325384 | tf_op jit(solution)/shard_map/ppermute | solution.py:161
  52.5 63.5 %collective-permute-start = (bf16[8,704,128]{2,1,0:T(8,128)(2,1)S(1)}, bf16[8,704,128]{2,1,0:T(8,128)(2,1)}, u32[]{:S(2)}, u32[]{:S(2)}) collective-permute-start(bf16[8,704,128]{2,1,0:T(8,128)(2,1)S(1)} %all_to_all.5.refs_0_), channel_id=1, source_target_pairs={{0,24},{8,0},{16,8},{24,16},{1,25},{9,1},{17,9},{25,17},{2,26},{10... | collective-permute-start | bytes 4325384 | tf_op jit(solution)/shard_map/ppermute | solution.py:161

commit v2 on v1

v2 whole, which is shorter than its diff:
```python
import functools
import math

import jax
import jax.numpy as jnp
import ml_dtypes
import numpy as np
from jax import lax
from jax.experimental import pallas as pl
from jax.experimental.pallas import tpu as pltpu
from jax.sharding import PartitionSpec as P

FREQS = 64
FIRST_BIN = 32
EPSILON = 1e-06
VMEM_LIMIT = 48 * 1024 * 1024


def dft_table(sample_count, time_count):
    half_freq = FREQS // 2
    per_device = half_freq // time_count
    positions = np.arange(sample_count)
    taper = 0.5 - 0.5 * np.cos(2.0 * math.pi / sample_count * positions)
    bins = np.arange(FREQS) + FIRST_BIN
    angle = 2.0 * math.pi / sample_count * (bins[:, None] * positions[None, :] % sample_count)
    parts = np.stack([taper * np.cos(angle), -taper * np.sin(angle)], axis=0)
    ordered = parts.reshape(2, 2, time_count, per_device, sample_count).transpose(2, 3, 0, 1, 4)
    return ordered.reshape(2 * FREQS, sample_count).astype(ml_dtypes.bfloat16)


def whiten_kernel(scale, step_windows, counts, target_of, table_hbm, records_hbm, *refs):
    out_refs = refs[: len(counts)]
    table_ref, records_ref, rows_ref, table_sem, record_sems = refs[len(counts) :]
    window_count, channels, samples = records_ref.shape
    bins = table_ref.shape[1]
    table_copy = pltpu.make_async_copy(table_hbm, table_ref, table_sem)
    table_copy.start()
    copies = []
    for step in range(window_count // step_windows):
        span = pl.ds(step * step_windows, step_windows)
        copies.append(pltpu.make_async_copy(records_hbm.at[span], records_ref.at[span], record_sems.at[step]))
        copies[-1].start()
    table_copy.wait()
    for step, copy in enumerate(copies):
        copy.wait()
        windows = records_ref[step * step_windows : (step + 1) * step_windows]
        spectra = jnp.dot(
            windows.reshape(step_windows * channels, samples), table_ref[...], preferred_element_type=jnp.float32
        )
        for local in range(step_windows):
            block = spectra[local * channels : (local + 1) * channels].T
            mean_square = jnp.sum(block * block, axis=0, keepdims=True) * (1.0 / bins)
            whitened = block * (scale / jnp.sqrt(mean_square + EPSILON))
            window = step * step_windows + local
            for row in range(0, bins, 8):
                rows_ref[pl.ds(row * window_count + window, 8, stride=window_count), :] = whitened[row : row + 8]
    place = 0
    for out_ref, count in zip(out_refs, counts):
        rows = out_ref.shape[1]
        for index in range(count):
            start = pl.multiple_of(target_of(place) * rows, 16)
            out_ref[index] = rows_ref[pl.ds(start, rows), :].astype(jnp.bfloat16)
            place += 1


def whiten(records, time_count, target_of, counts, sizes):
    window_count, channels, samples = records.shape
    step_windows = 4 if window_count % 4 == 0 else 1
    bins = 2 * FREQS
    rows = bins * window_count // time_count
    scale = float(window_count * time_count) ** (-0.25)
    return pl.pallas_call(
        functools.partial(whiten_kernel, scale, step_windows, counts, target_of),
        in_specs=[pl.BlockSpec(memory_space=pltpu.HBM)] * 2,
        out_specs=[pl.BlockSpec(memory_space=pltpu.VMEM)] * len(sizes),
        out_shape=[jax.ShapeDtypeStruct((size, rows, channels), jnp.bfloat16) for size in sizes],
        scratch_shapes=[
            pltpu.VMEM((samples, bins), jnp.bfloat16),
            pltpu.VMEM(records.shape, jnp.bfloat16),
            pltpu.VMEM((bins * window_count, channels), jnp.float32),
            pltpu.SemaphoreType.DMA,
            pltpu.SemaphoreType.DMA((window_count // step_windows,)),
        ],
        compiler_params=pltpu.CompilerParams(vmem_limit_bytes=VMEM_LIMIT),
        name="whiten",
    )(jnp.asarray(dft_table(samples, time_count).T.copy()), records)


def pair_kernel(chunk_count, operand_count, lower_ref, masks_ref, *refs):
    near_out, far_out, near_sum, far_sum = refs[-4:]
    near_before, far_before = refs[operand_count:-4] or (None, None)
    arrays = [refs[start : start + chunk_count] for start in range(0, operand_count, chunk_count)]
    own_refs, near_refs, far_refs = arrays[0], arrays[1:-1], arrays[-1]
    width = own_refs[0].shape[2]
    lower = lower_ref[0] > 0
    half = jnp.where(lower, 0, 1)

    def rotated(block):
        middle = block.shape[0] // 2
        return jnp.concatenate([block[middle:], block[:middle]], axis=0)

    def product(left, right):
        value = lax.dot_general(left, right, (((0,), (0,)), ((), ())), preferred_element_type=jnp.float32)
        return value.astype(jnp.bfloat16).astype(jnp.float32)

    first_group = True
    for chunk in range(chunk_count):
        for group in range(own_refs[chunk].shape[0]):
            own = own_refs[chunk][group]
            turned = rotated(own)
            left = jnp.concatenate(
                [own * masks_ref[0], turned * masks_ref[1], own * masks_ref[2], turned * masks_ref[3]], axis=1
            )
            right = jnp.concatenate([own] + [near[chunk][group] for near in near_refs], axis=1)
            near = product(left, right)
            far = far_refs[chunk][group]
            first = jnp.where(lower, own, far)
            second = jnp.where(lower, far, own)
            far_left = jnp.concatenate(
                [first * masks_ref[2 * half], rotated(first) * masks_ref[2 * half + 1]], axis=1
            )
            far = product(far_left, second)
            if first_group:
                near_sum[...] = near
                far_sum[...] = far
            else:
                near_sum[...] += near
                far_sum[...] += far
            first_group = False
    for h in range(2):
        for r in range(1 + len(near_refs)):
            for p in range(2):
                start = (2 * h + p) * width
                place = (0, h, r, pl.ds(p, width, stride=2), slice(None))
                total = near_sum[start : start + width, r * width : (r + 1) * width]
                near_out[place] = total if near_before is None else total + near_before[place]
    for p in range(2):
        place = (0, pl.ds(p, width, stride=2), slice(None))
        total = far_sum[p * width : (p + 1) * width, :]
        far_out[place] = total if far_before is None else total + far_before[place]


def pair_stack(own, near, far, window_count, before=()):
    all_rows, width = own[0].shape[1:]
    rows = 4 * window_count
    per_device = all_rows // rows
    rounds = 1 + len(near)
    lower = (lax.axis_index("chan") < lax.axis_size("chan") // 2).astype(jnp.int32).reshape(1)
    index = np.arange(rows)
    part, half = index // (2 * window_count), index // window_count % 2
    sign = np.where(part == 0, 1.0, -1.0)
    masks = np.stack([half == 0, (half == 0) * sign, half == 1, (half == 1) * sign])
    masks = np.broadcast_to(masks[:, :, None], (4, rows, width)).astype(ml_dtypes.bfloat16)
    operands = [chunk for chunks in [own] + near + [far] for chunk in chunks]
    sums = [
        pl.BlockSpec((1, 2, rounds, 2 * width, width), lambda g, *_: (g, 0, 0, 0, 0)),
        pl.BlockSpec((1, 2 * width, width), lambda g, *_: (g, 0, 0)),
    ]
    return pl.pallas_call(
        functools.partial(pair_kernel, len(own), len(operands)),
        grid_spec=pltpu.PrefetchScalarGridSpec(
            num_scalar_prefetch=1,
            grid=(per_device,),
            in_specs=[pl.BlockSpec((4, rows, width), lambda g, *_: (0, 0, 0))]
            + [pl.BlockSpec((chunk.shape[0], rows, width), lambda g, *_: (0, g, 0)) for chunk in operands]
            + (sums if before else []),
            out_specs=sums,
            scratch_shapes=[
                pltpu.VMEM((4 * width, rounds * width), jnp.float32),
                pltpu.VMEM((2 * width, width), jnp.float32),
            ],
        ),
        out_shape=[
            jax.ShapeDtypeStruct((per_device, 2, rounds, 2 * width, width), jnp.float32),
            jax.ShapeDtypeStruct((per_device, 2 * width, width), jnp.float32),
        ],
        input_output_aliases={2 + len(operands) + i: i for i in range(len(before))},
        compiler_params=pltpu.CompilerParams(vmem_limit_bytes=VMEM_LIMIT),
        name="pair_stack",
    )(lower, jnp.asarray(masks), *operands, *before)


def shifted(value, steps):
    count = lax.axis_size("chan")
    return lax.ppermute(value, "chan", [(source, (source + steps) % count) for source in range(count)])


def swapped(value, axis, bit):
    return lax.ppermute(value, axis, [(source, source ^ bit) for source in range(lax.axis_size(axis))])


def moved(value, steps):
    count = lax.axis_size("tm")
    return lax.ppermute(value, "tm", [(source, (source + 2 * steps) % count) for source in range(count)])


def phase_kernel(kept, copies, *refs):
    semaphores = refs[-1]
    outs = refs[kept:-1]
    odd = lax.rem(lax.axis_index("chan"), 2) == 1

    def run(chosen):
        started = []
        for place, (when, source, source_index, target, target_index) in enumerate(copies):
            if when == chosen:
                from_ref = outs[source] if source_index is None else outs[source].at[source_index]
                to_ref = outs[target] if target_index is None else outs[target].at[target_index]
                started.append(pltpu.make_async_copy(from_ref, to_ref, semaphores.at[place]))
                started[-1].start()
        for copy in started:
            copy.wait()

    run("always")
    if any(copy[0] != "always" for copy in copies):
        pl.when(odd)(functools.partial(run, "odd"))
        pl.when(jnp.logical_not(odd))(functools.partial(run, "even"))


def phase(operands, copies, like=()):
    shapes = [jax.ShapeDtypeStruct(x.shape, x.dtype) for x in list(operands) + [operands[i] for i in like]]
    anywhere = pl.BlockSpec(memory_space=pl.ANY)
    return pl.pallas_call(
        functools.partial(phase_kernel, len(operands), copies),
        in_specs=[anywhere] * len(operands),
        out_specs=[anywhere] * len(shapes),
        out_shape=shapes,
        input_output_aliases={i: i for i in range(len(operands))},
        scratch_shapes=[pltpu.SemaphoreType.DMA((max(1, len(copies)),))],
        compiler_params=pltpu.CompilerParams(vmem_limit_bytes=VMEM_LIMIT),
        cost_estimate=pl.CostEstimate(flops=0, bytes_accessed=0, transcendentals=0),
        name="phase",
    )(*operands)


def choose(own, far, target):
    return [("odd", own, None, target, None), ("even", far, None, target, None)]


def square_stack(records):
    window_count = records.shape[0]
    count = lax.axis_size("tm")

    def target_of(place):
        me = lax.axis_index("tm")
        core = me % 2 if place < 4 else 1 - me % 2
        return (me // 2 + (2, 0, 1, 3)[place % 4]) % (count // 2) * 2 + core

    opposite, here, after, before, other_core = whiten(records, count, target_of, (1, 1, 1, 1, 4), (1, 2, 2, 2, 4))
    far_swap = functools.partial(swapped, axis="chan", bit=2)
    near_swap = functools.partial(swapped, axis="chan", bit=1)
    stack = functools.partial(pair_stack, window_count=window_count)

    core = swapped(other_core, "tm", 1)
    last = core[:1]
    here, after, before, core = phase(
        [here, after, before, core],
        [("always", 3, 1, 0, 1), ("always", 3, 2, 1, 1), ("always", 3, 3, 2, 1)],
    )
    after = moved(after, 1)
    here_far = far_swap(here)

    here, here_far, after, before, here_send = phase([here, here_far, after, before], choose(0, 1, 4), like=(0,))
    before = moved(before, 3)
    after_far = far_swap(after)
    here_near = near_swap(here_send)

    after, after_far, before, opposite, here_near, after_send = phase(
        [after, after_far, before, opposite, here_near], choose(0, 1, 5), like=(0,)
    )
    two = moved(opposite, 2)
    before_far = far_swap(before)
    after_near = near_swap(after_send)
    near_sum, far_sum = stack([here], [[here_near]], [here_far])

    before, before_far, two, last, after_near, far_sum, before_send = phase(
        [before, before_far, two, last, after_near, far_sum], choose(0, 1, 6), like=(0,)
    )
    last = moved(last, 2)
    two_far = far_swap(two)
    before_near = near_swap(before_send)
    near_sum, far_sum = stack([after], [[after_near]], [after_far], before=(near_sum, far_sum))

    two, two_far, last, before_near, far_sum, two_send = phase(
        [two, two_far, last, before_near, far_sum], choose(0, 1, 5), like=(0,)
    )
    last_far = far_swap(last)
    last_near = shifted(last, -1)
    two_near = near_swap(two_send)
    near_sum, far_sum = stack([before], [[before_near]], [before_far], before=(near_sum, far_sum))
    return stack([two, last], [[two_near, last_near]], [two_far, last_far], before=(near_sum, far_sum))


def plain_stack(records):
    count, chan_count = lax.axis_size("tm"), lax.axis_size("chan")
    whitened = whiten(records, count, lambda place: place, (count,), (count,))[0]
    own = lax.all_to_all(whitened, "tm", split_axis=0, concat_axis=0, tiled=True)
    mates = [shifted(own, -offset) for offset in range(1, chan_count // 2 + 1)]
    return pair_stack([own], [[mate] for mate in mates[:-1]], [mates[-1]], records.shape[0])


def body(records):
    width = records.shape[1]
    square = lax.axis_size("tm") == 8 and lax.axis_size("chan") == 4
    near, far = (square_stack if square else plain_stack)(records)
    near = near.reshape(near.shape[:3] + (width, 2, width))
    return near, far.reshape(far.shape[0], width, 2, width)


def solution(mesh):
    return jax.shard_map(
        body,
        mesh=mesh,
        in_specs=(P("tm", "chan", None),),
        out_specs=(P("tm", None, None, "chan", None, None), P("tm", "chan", None, None)),
        check_vma=False,
    )
```

time: 123 us -> 76.8 us (0.62)
  the two profiles are of different devices: /device:TPU:6 before, /device:TPU:0 now
where the time goes in v2:
time: 76.8 us; the launch traced here: 76.4 us
  Pallas kernels  30 us (39%)
  waiting for transfers between devices  27.2 us (35%)
  starting transfers between devices  17.5 us (23%)
  local copies, waits for them, and re-layouts  0.97 us (1%)
    ppermute x4, waiting for transfers between devices, moved(): lax.ppermute(value, 'tm', [(source, (source + 2 * steps) % count) for sou...  23 us
    pallas_call x4, Pallas kernels, pair_stack(): pl.pallas_call(functools.partial(pair_kernel, len(own), len(operands)), g...  17.3 us
    pallas_call x1, Pallas kernels, whiten(): pl.pallas_call(functools.partial(whiten_kernel, scale, step_windows, coun...  10.7 us
    ppermute x10, starting transfers between devices, swapped(): lax.ppermute(value, axis, [(source, source ^ bit) for source in range(lax...  10.4 us
    ppermute x4, starting transfers between devices, moved(): lax.ppermute(value, 'tm', [(source, (source + 2 * steps) % count) for sou...  5.28 us
    ppermute x10, waiting for transfers between devices, swapped(): lax.ppermute(value, axis, [(source, source ^ bit) for source in range(lax...  4.2 us
    pallas_call x5, Pallas kernels, phase(): pl.pallas_call(functools.partial(phase_kernel, len(operands), copies), in...  2.05 us
    ppermute x1, starting transfers between devices, shifted(): lax.ppermute(value, 'chan', [(source, (source + steps) % count) for sourc...  1.85 us
  transfers between devices with their start and end apart: 15, of which 7 were waited for; matrix products, arithmetic and copies ran while one was open for 0% of the time, Pallas kernels for 16%

profile of v2, /device:TPU:0, one launch (start us, length us, event | category | flops | bytes accessed | tf_op | source)
XLA Modules:
  0.0 76.4 jit_solution(11651908527429441052)
XLA Ops:
  0.6 0.9 %copy-done.1 = bf16[1024,128]{1,0:T(8,128)(2,1)S(1)} copy-done((bf16[1024,128]{1,0:T(8,128)(2,1)S(1)}, bf16[1024,128]{1,0:T(8,128)(2,1)}, u32[]{:S(2)}) %copy-start.1) | copy-done | bytes 262168
  1.6 10.7 %whiten.1 = (bf16[1,704,128]{2,1,0:T(8,128)(2,1)}, bf16[2,704,128]{2,1,0:T(8,128)(2,1)S(1)}, bf16[2,704,128]{2,1,0:T(8,128)(2,1)S(1)}, bf16[2,704,128]{2,1,0:T(8,128)(2,1)S(1)}, bf16[4,704,128]{2,1,0:T(8,128)(2,1)S(1)}) custom-call(bf16[1024,128]{1,0:T(8,128)(2,1)S(1)} %copy-done.1, bf16[44,128,1024]{2,1,0:T(8,128)(2,1)} %records_hbm.1), custom_call_target="tpu_custom_call" | custom-call | tf_op jit(solution)/shard_map/whiten/pallas_call | solution.py:72
  12.8 1.8 %collective-permute-done.refs_3_ = bf16[4,704,128]{2,1,0:T(8,128)(2,1)S(1)} collective-permute-done((bf16[4,704,128]{2,1,0:T(8,128)(2,1)S(1)}, bf16[4,704,128]{2,1,0:T(8,128)(2,1)S(1)}, u32[]{:S(2)}, u32[]{:S(2)}) %collective-permute-start) | collective-permute-done | bytes 720928 | tf_op jit(solution)/shard_map/ppermute | solution.py:189
  14.7 0.7 phase.5
  15.4 3.0 %collective-permute-start.2 = (bf16[2,704,128]{2,1,0:T(8,128)(2,1)S(1)}, bf16[2,704,128]{2,1,0:T(8,128)(2,1)S(1)}, u32[]{:S(2)}, u32[]{:S(2)}) collective-permute-start(bf16[2,704,128]{2,1,0:T(8,128)(2,1)S(1)} %get-tuple-element.47), channel_id=1, source_target_pairs={{0,2},{1,3},{2,4},{3,5},{4,6},{5,7},{6,0},{7,1},{8,10},{9,11},{10,... | collective-permute-start | bytes 1081352 | tf_op jit(solution)/shard_map/ppermute | solution.py:194
  18.4 1.5 %collective-permute-start.1 = (bf16[2,704,128]{2,1,0:T(8,128)(2,1)S(1)}, bf16[2,704,128]{2,1,0:T(8,128)(2,1)S(1)}, u32[]{:S(2)}, u32[]{:S(2)}) collective-permute-start(bf16[2,704,128]{2,1,0:T(8,128)(2,1)S(1)} %get-tuple-element.46.refs_0_), channel_id=1, source_target_pairs={{0,16},{8,24},{16,0},{24,8},{1,17},{9,25},{17,1},{25,9},{2,18},{10... | collective-permute-start | bytes 1081352 | tf_op jit(solution)/shard_map/ppermute | solution.py:189
  19.9 9.2 %collective-permute-done.2.refs_2_ = bf16[2,704,128]{2,1,0:T(8,128)(2,1)S(1)} collective-permute-done((bf16[2,704,128]{2,1,0:T(8,128)(2,1)S(1)}, bf16[2,704,128]{2,1,0:T(8,128)(2,1)S(1)}, u32[]{:S(2)}, u32[]{:S(2)}) %collective-permute-start.2) | collective-permute-done | bytes 360480 | tf_op jit(solution)/shard_map/ppermute | solution.py:194
  29.3 1.9 %collective-permute-start.4 = (bf16[2,704,128]{2,1,0:T(8,128)(2,1)S(1)}, bf16[2,704,128]{2,1,0:T(8,128)(2,1)S(1)}, u32[]{:S(2)}, u32[]{:S(2)}) collective-permute-start(bf16[2,704,128]{2,1,0:T(8,128)(2,1)S(1)} %get-tuple-element.50), channel_id=1, source_target_pairs={{0,6},{1,7},{2,0},{3,1},{4,2},{5,3},{6,4},{7,5},{8,14},{9,15},{10,... | collective-permute-start | bytes 1081352 | tf_op jit(solution)/shard_map/ppermute | solution.py:194
  31.2 1.5 %collective-permute-start.5 = (bf16[2,704,128]{2,1,0:T(8,128)(2,1)S(1)}, bf16[2,704,128]{2,1,0:T(8,128)(2,1)S(1)}, u32[]{:S(2)}, u32[]{:S(2)}) collective-permute-start(bf16[2,704,128]{2,1,0:T(8,128)(2,1)S(1)} %get-tuple-element.52), channel_id=1, source_target_pairs={{0,8},{8,0},{16,24},{24,16},{1,9},{9,1},{17,25},{25,17},{2,10},{10... | collective-permute-start | bytes 1081352 | tf_op jit(solution)/shard_map/ppermute | solution.py:189
  32.7 1.5 %collective-permute-start.3 = (bf16[2,704,128]{2,1,0:T(8,128)(2,1)S(1)}, bf16[2,704,128]{2,1,0:T(8,128)(2,1)S(1)}, u32[]{:S(2)}, u32[]{:S(2)}) collective-permute-start(bf16[2,704,128]{2,1,0:T(8,128)(2,1)S(1)} %get-tuple-element.49.refs_0_), channel_id=1, source_target_pairs={{0,16},{8,24},{16,0},{24,8},{1,17},{9,25},{17,1},{25,9},{2,18},{10... | collective-permute-start | bytes 1081352 | tf_op jit(solution)/shard_map/ppermute | solution.py:189
  34.2 5.1 %collective-permute-done.4.refs_2_ = bf16[2,704,128]{2,1,0:T(8,128)(2,1)S(1)} collective-permute-done((bf16[2,704,128]{2,1,0:T(8,128)(2,1)S(1)}, bf16[2,704,128]{2,1,0:T(8,128)(2,1)S(1)}, u32[]{:S(2)}, u32[]{:S(2)}) %collective-permute-start.4) | collective-permute-done | bytes 360480 | tf_op jit(solution)/shard_map/ppermute | solution.py:194
  39.3 1.2 %collective-permute-done.5.refs_4_ = bf16[2,704,128]{2,1,0:T(8,128)(2,1)S(1)} collective-permute-done((bf16[2,704,128]{2,1,0:T(8,128)(2,1)S(1)}, bf16[2,704,128]{2,1,0:T(8,128)(2,1)S(1)}, u32[]{:S(2)}, u32[]{:S(2)}) %collective-permute-start.5) | collective-permute-done | bytes 360480 | tf_op jit(solution)/shard_map/ppermute | solution.py:189
  40.5 1.1 %collective-permute-done.3.refs_1_ = bf16[2,704,128]{2,1,0:T(8,128)(2,1)S(1)} collective-permute-done((bf16[2,704,128]{2,1,0:T(8,128)(2,1)S(1)}, bf16[2,704,128]{2,1,0:T(8,128)(2,1)S(1)}, u32[]{:S(2)}, u32[]{:S(2)}) %collective-permute-start.3) | collective-permute-done | bytes 360480 | tf_op jit(solution)/shard_map/ppermute | solution.py:189
  41.7 0.7 phase.7
  43.1 1.4 %collective-permute-start.6 = (bf16[2,704,128]{2,1,0:T(8,128)(2,1)S(1)}, bf16[2,704,128]{2,1,0:T(8,128)(2,1)S(1)}, u32[]{:S(2)}, u32[]{:S(2)}) collective-permute-start(bf16[2,704,128]{2,1,0:T(8,128)(2,1)S(1)} %get-tuple-element.53.refs_0_), channel_id=1, source_target_pairs={{0,16},{8,24},{16,0},{24,8},{1,17},{9,25},{17,1},{25,9},{2,18},{10... | collective-permute-start | bytes 1081352 | tf_op jit(solution)/shard_map/ppermute | solution.py:189
  44.9 3.1 %pair_stack.4 = (f32[4,2,2,256,128]{4,3,2,1,0:T(8,128)}, f32[4,256,128]{2,1,0:T(8,128)}) custom-call(s32[1]{0:T(128)} %bitcast.lower_ref, bf16[4,176,128]{2,1,0:T(8,128)(2,1)S(1)} %copy-done, bf16[2,704,128]{2,1,0:T(8,128)(2,1)S(1)} %get-tuple-element.56.refs_0_, bf16[2,704,128]{2,1,0:T(8,128)(2,1)S(1)} %get-tuple-element.57.refs_1_, ...), custom_call_target="tpu_custom_call" | custom-call | tf_op jit(solution)/shard_map/pair_stack/pallas_call | solution.py:159
  48.0 7.0 %collective-permute-done.7.refs_2_ = bf16[1,704,128]{2,1,0:T(8,128)(2,1)S(1)} collective-permute-done((bf16[1,704,128]{2,1,0:T(8,128)(2,1)}, bf16[1,704,128]{2,1,0:T(8,128)(2,1)S(1)}, u32[]{:S(2)}, u32[]{:S(2)}) %collective-permute-start.7) | collective-permute-done | bytes 180256 | tf_op jit(solution)/shard_map/ppermute | solution.py:194
  55.2 1.5 %collective-permute-start.11 = (bf16[2,704,128]{2,1,0:T(8,128)(2,1)S(1)}, bf16[2,704,128]{2,1,0:T(8,128)(2,1)S(1)}, u32[]{:S(2)}, u32[]{:S(2)}) collective-permute-start(bf16[2,704,128]{2,1,0:T(8,128)(2,1)S(1)} %get-tuple-element.62), channel_id=1, source_target_pairs={{0,8},{8,0},{16,24},{24,16},{1,9},{9,1},{17,25},{25,17},{2,10},{10... | collective-permute-start | bytes 1081352 | tf_op jit(solution)/shard_map/ppermute | solution.py:189
  56.8 4.8 %pair_stack.5 = (f32[4,2,2,256,128]{4,3,2,1,0:T(8,128)}, f32[4,256,128]{2,1,0:T(8,128)}) custom-call(s32[1]{0:T(128)} %bitcast.lower_ref, bf16[4,176,128]{2,1,0:T(8,128)(2,1)S(1)} %copy-done, bf16[2,704,128]{2,1,0:T(8,128)(2,1)S(1)} %get-tuple-element.63.refs_0_, ...), custom_call_target="tpu_custom_call", output_to_operand_aliasing={{0}: (5, {}), {1}: (6, {})} | custom-call | tf_op jit(solution)/shard_map/pair_stack/pallas_call | solution.py:159
  61.5 1.6 %collective-permute-done.10.refs_2_ = bf16[1,704,128]{2,1,0:T(8,128)(2,1)S(1)} collective-permute-done((bf16[1,704,128]{2,1,0:T(8,128)(2,1)S(1)}, bf16[1,704,128]{2,1,0:T(8,128)(2,1)S(1)}, u32[]{:S(2)}, u32[]{:S(2)}) %collective-permute-start.10) | collective-permute-done | bytes 180256 | tf_op jit(solution)/shard_map/ppermute | solution.py:194
  63.4 1.7 %collective-permute-start.12 = (bf16[1,704,128]{2,1,0:T(8,128)(2,1)S(1)}, bf16[1,704,128]{2,1,0:T(8,128)(2,1)S(1)}, u32[]{:S(2)}, u32[]{:S(2)}) collective-permute-start(bf16[1,704,128]{2,1,0:T(8,128)(2,1)S(1)} %get-tuple-element.71), channel_id=1, source_target_pairs={{0,8},{8,0},{16,24},{24,16},{1,9},{9,1},{17,25},{25,17},{2,10},{10... | collective-permute-start | bytes 540680 | tf_op jit(solution)/shard_map/ppermute | solution.py:189
  65.1 1.9 %collective-permute-start.13 = (bf16[1,704,128]{2,1,0:T(8,128)(2,1)S(1)}, bf16[1,704,128]{2,1,0:T(8,128)(2,1)S(1)}, u32[]{:S(2)}, u32[]{:S(2)}) collective-permute-start(bf16[1,704,128]{2,1,0:T(8,128)(2,1)S(1)} %get-tuple-element.70.refs_1_), channel_id=1, source_target_pairs={{0,24},{8,0},{16,8},{24,16},{1,25},{9,1},{17,9},{25,17},{2,26},{10... | collective-permute-start | bytes 540680 | tf_op jit(solution)/shard_map/ppermute | solution.py:185
  67.0 4.7 %pair_stack.6 = (f32[4,2,2,256,128]{4,3,2,1,0:T(8,128)}, f32[4,256,128]{2,1,0:T(8,128)}) custom-call(s32[1]{0:T(128)} %bitcast.lower_ref, bf16[4,176,128]{2,1,0:T(8,128)(2,1)S(1)} %copy-done, bf16[2,704,128]{2,1,0:T(8,128)(2,1)S(1)} %get-tuple-element.73.refs_0_, ...), custom_call_target="tpu_custom_call", output_to_operand_aliasing={{0}: (5, {}), {1}: (6, {})} | custom-call | tf_op jit(solution)/shard_map/pair_stack/pallas_call | solution.py:159
  71.7 4.7 %pair_stack.7 = (f32[4,2,2,256,128]{4,3,2,1,0:T(8,128)}, f32[4,256,128]{2,1,0:T(8,128)}) custom-call(s32[1]{0:T(128)} %bitcast.lower_ref, bf16[4,176,128]{2,1,0:T(8,128)(2,1)S(1)} %copy-done, bf16[1,704,128]{2,1,0:T(8,128)(2,1)S(1)} %get-tuple-element.69.refs_0_, ...), custom_call_target="tpu_custom_call", output_to_operand_aliasing={{0}: (8, {}), {1}: (9, {})} | custom-call | tf_op jit(solution)/shard_map/pair_stack/pallas_call | solution.py:159
  (21 shorter events, 2.2 us)
Async XLA Ops:
  0.6 1.0 %copy-start.1 = (bf16[1024,128]{1,0:T(8,128)(2,1)S(1)}, bf16[1024,128]{1,0:T(8,128)(2,1)}, u32[]{:S(2)}) copy-start(bf16[1024,128]{1,0:T(8,128)(2,1)} %constant.11.clone.table_hbm) | copy-start | bytes 786436
  12.3 2.3 %collective-permute-start = (bf16[4,704,128]{2,1,0:T(8,128)(2,1)S(1)}, bf16[4,704,128]{2,1,0:T(8,128)(2,1)S(1)}, u32[]{:S(2)}, u32[]{:S(2)}) collective-permute-start(bf16[4,704,128]{2,1,0:T(8,128)(2,1)S(1)} %get-tuple-element.45), channel_id=1, source_target_pairs={{0,1},{1,0},{2,3},{3,2},{4,5},{5,4},{6,7},{7,6},{8,9},{9,8},{10,11... | collective-permute-start | bytes 2162696 | tf_op jit(solution)/shard_map/ppermute | solution.py:189
  14.6 30.3 %copy-start = (bf16[4,176,128]{2,1,0:T(8,128)(2,1)S(1)}, bf16[4,176,128]{2,1,0:T(8,128)(2,1)}, u32[]{:S(2)}) copy-start(bf16[4,176,128]{2,1,0:T(8,128)(2,1)} %constant.12.clone.masks_ref) | copy-start | bytes 540676
  15.4 13.7 %collective-permute-start.2 = (bf16[2,704,128]{2,1,0:T(8,128)(2,1)S(1)}, bf16[2,704,128]{2,1,0:T(8,128)(2,1)S(1)}, u32[]{:S(2)}, u32[]{:S(2)}) collective-permute-start(bf16[2,704,128]{2,1,0:T(8,128)(2,1)S(1)} %get-tuple-element.47), channel_id=1, source_target_pairs={{0,2},{1,3},{2,4},{3,5},{4,6},{5,7},{6,0},{7,1},{8,10},{9,11},{10,... | collective-permute-start | bytes 1081352 | tf_op jit(solution)/shard_map/ppermute | solution.py:194
  18.4 10.7 %collective-permute-start.1 = (bf16[2,704,128]{2,1,0:T(8,128)(2,1)S(1)}, bf16[2,704,128]{2,1,0:T(8,128)(2,1)S(1)}, u32[]{:S(2)}, u32[]{:S(2)}) collective-permute-start(bf16[2,704,128]{2,1,0:T(8,128)(2,1)S(1)} %get-tuple-element.46.refs_0_), channel_id=1, source_target_pairs={{0,16},{8,24},{16,0},{24,8},{1,17},{9,25},{17,1},{25,9},{2,18},{10... | collective-permute-start | bytes 1081352 | tf_op jit(solution)/shard_map/ppermute | solution.py:189
  29.3 10.0 %collective-permute-start.4 = (bf16[2,704,128]{2,1,0:T(8,128)(2,1)S(1)}, bf16[2,704,128]{2,1,0:T(8,128)(2,1)S(1)}, u32[]{:S(2)}, u32[]{:S(2)}) collective-permute-start(bf16[2,704,128]{2,1,0:T(8,128)(2,1)S(1)} %get-tuple-element.50), channel_id=1, source_target_pairs={{0,6},{1,7},{2,0},{3,1},{4,2},{5,3},{6,4},{7,5},{8,14},{9,15},{10,... | collective-permute-start | bytes 1081352 | tf_op jit(solution)/shard_map/ppermute | solution.py:194
  31.2 9.3 %collective-permute-start.5 = (bf16[2,704,128]{2,1,0:T(8,128)(2,1)S(1)}, bf16[2,704,128]{2,1,0:T(8,128)(2,1)S(1)}, u32[]{:S(2)}, u32[]{:S(2)}) collective-permute-start(bf16[2,704,128]{2,1,0:T(8,128)(2,1)S(1)} %get-tuple-element.52), channel_id=1, source_target_pairs={{0,8},{8,0},{16,24},{24,16},{1,9},{9,1},{17,25},{25,17},{2,10},{10... | collective-permute-start | bytes 1081352 | tf_op jit(solution)/shard_map/ppermute | solution.py:189
  32.7 9.0 %collective-permute-start.3 = (bf16[2,704,128]{2,1,0:T(8,128)(2,1)S(1)}, bf16[2,704,128]{2,1,0:T(8,128)(2,1)S(1)}, u32[]{:S(2)}, u32[]{:S(2)}) collective-permute-start(bf16[2,704,128]{2,1,0:T(8,128)(2,1)S(1)} %get-tuple-element.49.refs_0_), channel_id=1, source_target_pairs={{0,16},{8,24},{16,0},{24,8},{1,17},{9,25},{17,1},{25,9},{2,18},{10... | collective-permute-start | bytes 1081352 | tf_op jit(solution)/shard_map/ppermute | solution.py:189
  42.4 12.6 %collective-permute-start.8 = (bf16[2,704,128]{2,1,0:T(8,128)(2,1)}, bf16[2,704,128]{2,1,0:T(8,128)(2,1)S(1)}, u32[]{:S(2)}, u32[]{:S(2)}) collective-permute-start(bf16[2,704,128]{2,1,0:T(8,128)(2,1)} %get-tuple-element.55), channel_id=1, source_target_pairs={{0,8},{8,0},{16,24},{24,16},{1,9},{9,1},{17,25},{25,17},{2,10},{10... | collective-permute-start | bytes 1081352 | tf_op jit(solution)/shard_map/ppermute | solution.py:189
  43.1 12.0 %collective-permute-start.6 = (bf16[2,704,128]{2,1,0:T(8,128)(2,1)S(1)}, bf16[2,704,128]{2,1,0:T(8,128)(2,1)S(1)}, u32[]{:S(2)}, u32[]{:S(2)}) collective-permute-start(bf16[2,704,128]{2,1,0:T(8,128)(2,1)S(1)} %get-tuple-element.53.refs_0_), channel_id=1, source_target_pairs={{0,16},{8,24},{16,0},{24,8},{1,17},{9,25},{17,1},{25,9},{2,18},{10... | collective-permute-start | bytes 1081352 | tf_op jit(solution)/shard_map/ppermute | solution.py:189
  44.5 10.5 %collective-permute-start.7 = (bf16[1,704,128]{2,1,0:T(8,128)(2,1)}, bf16[1,704,128]{2,1,0:T(8,128)(2,1)S(1)}, u32[]{:S(2)}, u32[]{:S(2)}) collective-permute-start(bf16[1,704,128]{2,1,0:T(8,128)(2,1)} %get-tuple-element.54), channel_id=1, source_target_pairs={{0,4},{1,5},{2,6},{3,7},{4,0},{5,1},{6,2},{7,3},{8,12},{9,13},{10,... | collective-permute-start | bytes 540680 | tf_op jit(solution)/shard_map/ppermute | solution.py:194
  55.2 7.9 %collective-permute-start.11 = (bf16[2,704,128]{2,1,0:T(8,128)(2,1)S(1)}, bf16[2,704,128]{2,1,0:T(8,128)(2,1)S(1)}, u32[]{:S(2)}, u32[]{:S(2)}) collective-permute-start(bf16[2,704,128]{2,1,0:T(8,128)(2,1)S(1)} %get-tuple-element.62), channel_id=1, source_target_pairs={{0,8},{8,0},{16,24},{24,16},{1,9},{9,1},{17,25},{25,17},{2,10},{10... | collective-permute-start | bytes 1081352 | tf_op jit(solution)/shard_map/ppermute | solution.py:189
  56.7 6.4 %collective-permute-start.10 = (bf16[1,704,128]{2,1,0:T(8,128)(2,1)S(1)}, bf16[1,704,128]{2,1,0:T(8,128)(2,1)S(1)}, u32[]{:S(2)}, u32[]{:S(2)}) collective-permute-start(bf16[1,704,128]{2,1,0:T(8,128)(2,1)S(1)} %get-tuple-element.61), channel_id=1, source_target_pairs={{0,4},{1,5},{2,6},{3,7},{4,0},{5,1},{6,2},{7,3},{8,12},{9,13},{10,... | collective-permute-start | bytes 540680 | tf_op jit(solution)/shard_map/ppermute | solution.py:194
  56.8 6.4 %collective-permute-start.9 = (bf16[1,704,128]{2,1,0:T(8,128)(2,1)S(1)}, bf16[1,704,128]{2,1,0:T(8,128)(2,1)S(1)}, u32[]{:S(2)}, u32[]{:S(2)}) collective-permute-start(bf16[1,704,128]{2,1,0:T(8,128)(2,1)S(1)} %get-tuple-element.60.refs_0_), channel_id=1, source_target_pairs={{0,16},{8,24},{16,0},{24,8},{1,17},{9,25},{17,1},{25,9},{2,18},{10... | collective-permute-start | bytes 540680 | tf_op jit(solution)/shard_map/ppermute | solution.py:189
  63.4 8.3 %collective-permute-start.12 = (bf16[1,704,128]{2,1,0:T(8,128)(2,1)S(1)}, bf16[1,704,128]{2,1,0:T(8,128)(2,1)S(1)}, u32[]{:S(2)}, u32[]{:S(2)}) collective-permute-start(bf16[1,704,128]{2,1,0:T(8,128)(2,1)S(1)} %get-tuple-element.71), channel_id=1, source_target_pairs={{0,8},{8,0},{16,24},{24,16},{1,9},{9,1},{17,25},{25,17},{2,10},{10... | collective-permute-start | bytes 540680 | tf_op jit(solution)/shard_map/ppermute | solution.py:189
  65.1 6.6 %collective-permute-start.14 = (bf16[1,704,128]{2,1,0:T(8,128)(2,1)S(1)}, bf16[1,704,128]{2,1,0:T(8,128)(2,1)S(1)}, u32[]{:S(2)}, u32[]{:S(2)}) collective-permute-start(bf16[1,704,128]{2,1,0:T(8,128)(2,1)S(1)} %get-tuple-element.70.refs_1_), channel_id=1, source_target_pairs={{0,16},{8,24},{16,0},{24,8},{1,17},{9,25},{17,1},{25,9},{2,18},{10... | collective-permute-start | bytes 540680 | tf_op jit(solution)/shard_map/ppermute | solution.py:189
  65.1 6.6 %collective-permute-start.13 = (bf16[1,704,128]{2,1,0:T(8,128)(2,1)S(1)}, bf16[1,704,128]{2,1,0:T(8,128)(2,1)S(1)}, u32[]{:S(2)}, u32[]{:S(2)}) collective-permute-start(bf16[1,704,128]{2,1,0:T(8,128)(2,1)S(1)} %get-tuple-element.70.refs_1_), channel_id=1, source_target_pairs={{0,24},{8,0},{16,8},{24,16},{1,25},{9,1},{17,9},{25,17},{2,26},{10... | collective-permute-start | bytes 540680 | tf_op jit(solution)/shard_map/ppermute | solution.py:185

commit v3 on v2

--- a/solution.py
+++ b/solution.py
@@ -13,47 +13,53 @@
 FREQS = 64
 FIRST_BIN = 32
 EPSILON = 1e-06
-VMEM_LIMIT = 48 * 1024 * 1024
-
-
-def dft_table(sample_count, time_count):
-    half_freq = FREQS // 2
-    per_device = half_freq // time_count
-    positions = np.arange(sample_count)
-    taper = 0.5 - 0.5 * np.cos(2.0 * math.pi / sample_count * positions)
-    bins = np.arange(FREQS) + FIRST_BIN
-    angle = 2.0 * math.pi / sample_count * (bins[:, None] * positions[None, :] % sample_count)
-    parts = np.stack([taper * np.cos(angle), -taper * np.sin(angle)], axis=0)
-    ordered = parts.reshape(2, 2, time_count, per_device, sample_count).transpose(2, 3, 0, 1, 4)
-    return ordered.reshape(2 * FREQS, sample_count).astype(ml_dtypes.bfloat16)
-
-
-def whiten_kernel(scale, step_windows, counts, target_of, table_hbm, records_hbm, *refs):
+WHITEN_VMEM = 52 * 1024 * 1024
+VMEM_LIMIT = 16 * 1024 * 1024
+
+
+def dft_table(bins, samples):
+    row = lax.broadcasted_iota(jnp.int32, (bins, samples), 0)
+    position = lax.broadcasted_iota(jnp.int32, (bins, samples), 1)
+    frequency = FIRST_BIN + FREQS // 2 * (row % 2) + row // 4
+    phase_index = (frequency * position + samples // 4 * (row // 2 % 2)) % samples
+    scale = 2.0 * math.pi / samples
+    taper = 0.5 - 0.5 * jnp.cos(scale * lax.broadcasted_iota(jnp.int32, (1, samples), 1).astype(jnp.float32))
+    return (taper * jnp.cos(scale * phase_index.astype(jnp.float32))).astype(jnp.bfloat16)
+
+
+def whiten_kernel(scale, step_windows, counts, target_of, records_hbm, *refs):
     out_refs = refs[: len(counts)]
-    table_ref, records_ref, rows_ref, table_sem, record_sems = refs[len(counts) :]
+    table_ref, records_ref, rows_ref, record_sems = refs[len(counts) :]
     window_count, channels, samples = records_ref.shape
-    bins = table_ref.shape[1]
-    table_copy = pltpu.make_async_copy(table_hbm, table_ref, table_sem)
-    table_copy.start()
-    copies = []
-    for step in range(window_count // step_windows):
+    bins = table_ref.shape[0]
+    steps = window_count // step_windows
+
+    def record_copy(step):
         span = pl.ds(step * step_windows, step_windows)
-        copies.append(pltpu.make_async_copy(records_hbm.at[span], records_ref.at[span], record_sems.at[step]))
-        copies[-1].start()
-    table_copy.wait()
-    for step, copy in enumerate(copies):
-        copy.wait()
+        return pltpu.make_async_copy(records_hbm.at[span], records_ref.at[span], record_sems.at[step])
+
+    for step in range(min(2, steps)):
+        record_copy(step).start()
+    table_ref[...] = dft_table(bins, samples)
+    for step in range(steps):
+        record_copy(step).wait()
+        if step + 2 < steps:
+            record_copy(step + 2).start()
         windows = records_ref[step * step_windows : (step + 1) * step_windows]
-        spectra = jnp.dot(
-            windows.reshape(step_windows * channels, samples), table_ref[...], preferred_element_type=jnp.float32
+        spectra = lax.dot_general(
+            table_ref[...],
+            windows.reshape(step_windows * channels, samples),
+            (((1,), (1,)), ((), ())),
+            preferred_element_type=jnp.float32,
         )
+        mean_square = jnp.sum(spectra * spectra, axis=0, keepdims=True) * (1.0 / bins)
+        whitened = spectra * (scale / jnp.sqrt(mean_square + EPSILON))
         for local in range(step_windows):
-            block = spectra[local * channels : (local + 1) * channels].T
-            mean_square = jnp.sum(block * block, axis=0, keepdims=True) * (1.0 / bins)
-            whitened = block * (scale / jnp.sqrt(mean_square + EPSILON))
             window = step * step_windows + local
             for row in range(0, bins, 8):
-                rows_ref[pl.ds(row * window_count + window, 8, stride=window_count), :] = whitened[row : row + 8]
+                rows_ref[pl.ds(row * window_count + window, 8, stride=window_count), :] = whitened[
+                    row : row + 8, local * channels : (local + 1) * channels
+                ]
     place = 0
     for out_ref, count in zip(out_refs, counts):
         rows = out_ref.shape[1]
@@ -65,25 +71,24 @@
 
 def whiten(records, time_count, target_of, counts, sizes):
     window_count, channels, samples = records.shape
-    step_windows = 4 if window_count % 4 == 0 else 1
+    step_windows = window_count // 4 if window_count % 4 == 0 else window_count
     bins = 2 * FREQS
     rows = bins * window_count // time_count
     scale = float(window_count * time_count) ** (-0.25)
     return pl.pallas_call(
         functools.partial(whiten_kernel, scale, step_windows, counts, target_of),
-        in_specs=[pl.BlockSpec(memory_space=pltpu.HBM)] * 2,
+        in_specs=[pl.BlockSpec(memory_space=pltpu.HBM)],
         out_specs=[pl.BlockSpec(memory_space=pltpu.VMEM)] * len(sizes),
         out_shape=[jax.ShapeDtypeStruct((size, rows, channels), jnp.bfloat16) for size in sizes],
         scratch_shapes=[
-            pltpu.VMEM((samples, bins), jnp.bfloat16),
+            pltpu.VMEM((bins, samples), jnp.bfloat16),
             pltpu.VMEM(records.shape, jnp.bfloat16),
             pltpu.VMEM((bins * window_count, channels), jnp.float32),
-            pltpu.SemaphoreType.DMA,
             pltpu.SemaphoreType.DMA((window_count // step_windows,)),
         ],
-        compiler_params=pltpu.CompilerParams(vmem_limit_bytes=VMEM_LIMIT),
+        compiler_params=pltpu.CompilerParams(vmem_limit_bytes=WHITEN_VMEM),
         name="whiten",
-    )(jnp.asarray(dft_table(samples, time_count).T.copy()), records)
+    )(records)
 
 
 def pair_kernel(chunk_count, operand_count, lower_ref, masks_ref, *refs):
@@ -140,7 +145,7 @@
         far_out[place] = total if far_before is None else total + far_before[place]
 
 
-def pair_stack(own, near, far, window_count, before=()):
+def pair_stack(own, near, far, window_count, before=(), in_place=False):
     all_rows, width = own[0].shape[1:]
     rows = 4 * window_count
     per_device = all_rows // rows
@@ -174,7 +179,7 @@
             jax.ShapeDtypeStruct((per_device, 2, rounds, 2 * width, width), jnp.float32),
             jax.ShapeDtypeStruct((per_device, 2 * width, width), jnp.float32),
         ],
-        input_output_aliases={2 + len(operands) + i: i for i in range(len(before))},
+        input_output_aliases={2 + len(operands) + i: i for i in range(len(before) if in_place else 0)},
         compiler_params=pltpu.CompilerParams(vmem_limit_bytes=VMEM_LIMIT),
         name="pair_stack",
     )(lower, jnp.asarray(masks), *operands, *before)
@@ -194,21 +199,14 @@
     return lax.ppermute(value, "tm", [(source, (source + 2 * steps) % count) for source in range(count)])
 
 
-def phase_kernel(kept, copies, *refs):
-    semaphores = refs[-1]
-    outs = refs[kept:-1]
+def phase_kernel(kept, made, copies, *refs):
+    sources, outs = refs[kept : len(refs) - kept - made], refs[len(refs) - made :]
     odd = lax.rem(lax.axis_index("chan"), 2) == 1
 
     def run(chosen):
-        started = []
-        for place, (when, source, source_index, target, target_index) in enumerate(copies):
+        for when, source, target, first in copies:
             if when == chosen:
-                from_ref = outs[source] if source_index is None else outs[source].at[source_index]
-                to_ref = outs[target] if target_index is None else outs[target].at[target_index]
-                started.append(pltpu.make_async_copy(from_ref, to_ref, semaphores.at[place]))
-                started[-1].start()
-        for copy in started:
-            copy.wait()
+                outs[target][first : first + sources[source].shape[0]] = sources[source][...]
 
     run("always")
     if any(copy[0] != "always" for copy in copies):
@@ -216,24 +214,22 @@
         pl.when(jnp.logical_not(odd))(functools.partial(run, "even"))
 
 
-def phase(operands, copies, like=()):
-    shapes = [jax.ShapeDtypeStruct(x.shape, x.dtype) for x in list(operands) + [operands[i] for i in like]]
-    anywhere = pl.BlockSpec(memory_space=pl.ANY)
+def phase(kept, sources=(), counts=(), copies=()):
+    made = [jax.ShapeDtypeStruct((count,) + sources[0].shape[1:], sources[0].dtype) for count in counts]
+    anywhere, vmem = pl.BlockSpec(memory_space=pl.ANY), pl.BlockSpec(memory_space=pltpu.VMEM)
     return pl.pallas_call(
-        functools.partial(phase_kernel, len(operands), copies),
-        in_specs=[anywhere] * len(operands),
-        out_specs=[anywhere] * len(shapes),
-        out_shape=shapes,
-        input_output_aliases={i: i for i in range(len(operands))},
-        scratch_shapes=[pltpu.SemaphoreType.DMA((max(1, len(copies)),))],
+        functools.partial(phase_kernel, len(kept), len(made), tuple(copies)),
+        in_specs=[anywhere] * len(kept) + [vmem] * len(sources),
+        out_specs=[anywhere] * len(kept) + [vmem] * len(made),
+        out_shape=[jax.ShapeDtypeStruct(x.shape, x.dtype) for x in kept] + made,
+        input_output_aliases={i: i for i in range(len(kept))},
         compiler_params=pltpu.CompilerParams(vmem_limit_bytes=VMEM_LIMIT),
-        cost_estimate=pl.CostEstimate(flops=0, bytes_accessed=0, transcendentals=0),
         name="phase",
-    )(*operands)
-
-
-def choose(own, far, target):
-    return [("odd", own, None, target, None), ("even", far, None, target, None)]
+    )(*kept, *sources)
+
+
+def near_payload(kept, own, far):
+    return phase(kept, [own, far], [own.shape[0]], [("odd", 0, 0, 0), ("even", 1, 0, 0)])
 
 
 def square_stack(records):
@@ -243,50 +239,61 @@
     def target_of(place):
         me = lax.axis_index("tm")
         core = me % 2 if place < 4 else 1 - me % 2
-        return (me // 2 + (2, 0, 1, 3)[place % 4]) % (count // 2) * 2 + core
-
-    opposite, here, after, before, other_core = whiten(records, count, target_of, (1, 1, 1, 1, 4), (1, 2, 2, 2, 4))
+        return (me // 2 + (1, 2, 3, 0)[place % 4]) % (count // 2) * 2 + core
+
+    after_one, opposite, before, here, core = whiten(records, count, target_of, (1, 1, 1, 1, 4), (1, 1, 1, 1, 4))
     far_swap = functools.partial(swapped, axis="chan", bit=2)
     near_swap = functools.partial(swapped, axis="chan", bit=1)
     stack = functools.partial(pair_stack, window_count=window_count)
-
-    core = swapped(other_core, "tm", 1)
-    last = core[:1]
-    here, after, before, core = phase(
-        [here, after, before, core],
-        [("always", 3, 1, 0, 1), ("always", 3, 2, 1, 1), ("always", 3, 3, 2, 1)],
+    grow = functools.partial(stack, in_place=True)
+    token = jnp.zeros((8, 128), jnp.float32)
+
+    after_one = moved(after_one, 1)
+    core = swapped(core, "tm", 1)
+    core_after, core_last, core_before, core_here = (core[i : i + 1] for i in range(4))
+    token, here, after_two, last, before_two = phase(
+        [token],
+        [here, core_here, core_after, core_last, core_before],
+        [2, 1, 1, 1],
+        [("always", 0, 0, 0), ("always", 1, 0, 1), ("always", 2, 1, 0), ("always", 3, 2, 0), ("always", 4, 3, 0)],
     )
-    after = moved(after, 1)
+    after_two = moved(after_two, 1)
     here_far = far_swap(here)
 
-    here, here_far, after, before, here_send = phase([here, here_far, after, before], choose(0, 1, 4), like=(0,))
-    before = moved(before, 3)
+    token, after_one, before = phase([token, after_one, before])
+    before_one = moved(before, 3)
+
+    token, before_two, after = phase([token, before_two], [after_one, after_two], [2], [("always", 0, 0, 0), ("always", 1, 0, 1)])
+    before_two = moved(before_two, 3)
     after_far = far_swap(after)
+
+    token, here_send = near_payload([token], here, here_far)
     here_near = near_swap(here_send)
 
-    after, after_far, before, opposite, here_near, after_send = phase(
-        [after, after_far, before, opposite, here_near], choose(0, 1, 5), like=(0,)
-    )
+    token, before_one, opposite = phase([token, before_one, opposite])
     two = moved(opposite, 2)
+
+    token, last, before = phase([token, last], [before_one, before_two], [2], [("always", 0, 0, 0), ("always", 1, 0, 1)])
+    last = moved(last, 2)
     before_far = far_swap(before)
+
+    token, after_send = near_payload([token], after, after_far)
     after_near = near_swap(after_send)
     near_sum, far_sum = stack([here], [[here_near]], [here_far])
 
-    before, before_far, two, last, after_near, far_sum, before_send = phase(
-        [before, before_far, two, last, after_near, far_sum], choose(0, 1, 6), like=(0,)
-    )
-    last = moved(last, 2)
+    token, far_sum, before_send = near_payload([token, far_sum], before, before_far)
+    before_near = near_swap(before_send)
+
+    token, two = phase([token, two])
     two_far = far_swap(two)
-    before_near = near_swap(before_send)
-    near_sum, far_sum = stack([after], [[after_near]], [after_far], before=(near_sum, far_sum))
-
-    two, two_far, last, before_near, far_sum, two_send = phase(
-        [two, two_far, last, before_near, far_sum], choose(0, 1, 5), like=(0,)
-    )
+    near_sum, far_sum = grow([after], [[after_near]], [after_far], before=(near_sum, far_sum))
+
+    token, far_sum, two_send = near_payload([token, far_sum], two, two_far)
+    two_near = near_swap(two_send)
+
+    last_near = shifted(last, -1)
     last_far = far_swap(last)
-    last_near = shifted(last, -1)
-    two_near = near_swap(two_send)
-    near_sum, far_sum = stack([before], [[before_near]], [before_far], before=(near_sum, far_sum))
+    near_sum, far_sum = grow([before], [[before_near]], [before_far], before=(near_sum, far_sum))
     return stack([two, last], [[two_near, last_near]], [two_far, last_far], before=(near_sum, far_sum))
 
 

time: 76.8 us -> 64.5 us (0.84)
  Pallas kernels: 30 us -> 17.4 us
  starting transfers between devices: 17.5 us -> 22.8 us
  waiting for transfers between devices: 27.2 us -> 22.7 us
    pallas_call x4, Pallas kernels: 17.3 us -> 8.71 us  [pair_stack(): pl.pallas_call(functools.partial(pair_kernel, len(own), len(operands)), g...]
    ppermute x4 -> x6, waiting for transfers between devices: 23 us -> 15.4 us  [moved(): lax.ppermute(value, 'tm', [(source, (source + 2 * steps) % count) for sou...]
    pallas_call x1, Pallas kernels: 10.7 us -> 6.98 us  [whiten(): pl.pallas_call(functools.partial(whiten_kernel, scale, step_windows, coun...]
    ppermute x4 -> x6, starting transfers between devices: 5.28 us -> 8.99 us  [moved(): lax.ppermute(value, 'tm', [(source, (source + 2 * steps) % count) for sou...]
    ppermute x10, waiting for transfers between devices: 4.2 us -> 7.25 us  [swapped(): lax.ppermute(value, axis, [(source, source ^ bit) for source in range(lax...]
    ppermute x10, starting transfers between devices: 10.4 us -> 12.5 us  [swapped(): lax.ppermute(value, axis, [(source, source ^ bit) for source in range(lax...]
    pallas_call x5 -> x10, Pallas kernels: 2.05 us -> 1.69 us  [phase(): pl.pallas_call(functools.partial(phase_kernel, len(kept), len(made), tupl...]
  transfers between devices with their start and end apart: 15 -> 17, of which waited for: 7 -> 9; matrix products, arithmetic and copies ran while one was open for 0% -> 0% of each run, Pallas kernels for 16% -> 12%
where the time goes in v3:
time: 64.5 us; the launch traced here: 64.3 us
  starting transfers between devices  22.8 us (35%)
  waiting for transfers between devices  22.7 us (35%)
  Pallas kernels  17.4 us (27%)
  between operations  0.77 us (1%)
  local copies, waits for them, and re-layouts  0.71 us (1%)
    ppermute x6, waiting for transfers between devices, moved(): lax.ppermute(value, 'tm', [(source, (source + 2 * steps) % count) for sou...  15.4 us
    ppermute x10, starting transfers between devices, swapped(): lax.ppermute(value, axis, [(source, source ^ bit) for source in range(lax...  12.5 us
    ppermute x6, starting transfers between devices, moved(): lax.ppermute(value, 'tm', [(source, (source + 2 * steps) % count) for sou...  8.99 us
    pallas_call x4, Pallas kernels, pair_stack(): pl.pallas_call(functools.partial(pair_kernel, len(own), len(operands)), g...  8.71 us
    ppermute x10, waiting for transfers between devices, swapped(): lax.ppermute(value, axis, [(source, source ^ bit) for source in range(lax...  7.25 us
    pallas_call x1, Pallas kernels, whiten(): pl.pallas_call(functools.partial(whiten_kernel, scale, step_windows, coun...  6.98 us
    pallas_call x10, Pallas kernels, phase(): pl.pallas_call(functools.partial(phase_kernel, len(kept), len(made), tupl...  1.69 us
  transfers between devices with their start and end apart: 17, of which 9 were waited for; matrix products, arithmetic and copies ran while one was open for 0% of the time, Pallas kernels for 12%

profile of v3, /device:TPU:0, one launch (start us, length us, event | category | flops | bytes accessed | tf_op | source)
XLA Modules:
  0.0 64.3 jit_solution(993750196651018818)
XLA Ops:
  0.6 7.0 %whiten.1 = (bf16[1,704,128]{2,1,0:T(8,128)(2,1)S(1)}, bf16[1,704,128]{2,1,0:T(8,128)(2,1)S(1)}, bf16[1,704,128]{2,1,0:T(8,128)(2,1)S(1)}, bf16[1,704,128]{2,1,0:T(8,128)(2,1)S(1)}, bf16[4,704,128]{2,1,0:T(8,128)(2,1)S(1)}) custom-call(bf16[44,128,1024]{2,1,0:T(8,128)(2,1)} %records_hbm.1), custom_call_target="tpu_custom_call" | custom-call | tf_op jit(solution)/shard_map/whiten/pallas_call | solution.py:78
  8.1 2.6 %collective-permute-start.1 = (bf16[1,704,128]{2,1,0:T(8,128)(2,1)S(1)}, bf16[1,704,128]{2,1,0:T(8,128)(2,1)S(1)}, u32[]{:S(2)}, u32[]{:S(2)}) collective-permute-start(bf16[1,704,128]{2,1,0:T(8,128)(2,1)S(1)} %get-tuple-element.46), channel_id=1, source_target_pairs={{0,2},{1,3},{2,4},{3,5},{4,6},{5,7},{6,0},{7,1},{8,10},{9,11},{10,... | collective-permute-start | bytes 540680 | tf_op jit(solution)/shard_map/ppermute | solution.py:199
  10.9 2.1 %collective-permute-start.3 = (bf16[2,704,128]{2,1,0:T(8,128)(2,1)S(1)}, bf16[2,704,128]{2,1,0:T(8,128)(2,1)S(1)}, u32[]{:S(2)}, u32[]{:S(2)}) collective-permute-start(bf16[2,704,128]{2,1,0:T(8,128)(2,1)S(1)} %get-tuple-element.53.refs_1_.refs_0_), channel_id=1, source_target_pairs={{0,16},{8,24},{16,0},{24,8},{1,17},{9,25},{17,1},{25,9},{2,18},{10... | collective-permute-start | bytes 1081352 | tf_op jit(solution)/shard_map/ppermute | solution.py:194
  13.0 1.6 %collective-permute-start.2 = (bf16[1,704,128]{2,1,0:T(8,128)(2,1)S(1)}, bf16[1,704,128]{2,1,0:T(8,128)(2,1)S(1)}, u32[]{:S(2)}, u32[]{:S(2)}) collective-permute-start(bf16[1,704,128]{2,1,0:T(8,128)(2,1)S(1)} %get-tuple-element.51), channel_id=1, source_target_pairs={{0,2},{1,3},{2,4},{3,5},{4,6},{5,7},{6,0},{7,1},{8,10},{9,11},{10,... | collective-permute-start | bytes 540680 | tf_op jit(solution)/shard_map/ppermute | solution.py:199
  14.6 3.6 %collective-permute-done.1.refs_1_ = bf16[1,704,128]{2,1,0:T(8,128)(2,1)S(1)} collective-permute-done((bf16[1,704,128]{2,1,0:T(8,128)(2,1)S(1)}, bf16[1,704,128]{2,1,0:T(8,128)(2,1)S(1)}, u32[]{:S(2)}, u32[]{:S(2)}) %collective-permute-start.1) | collective-permute-done | bytes 180256 | tf_op jit(solution)/shard_map/ppermute | solution.py:199
  18.2 1.9 %collective-permute-start.4 = (bf16[1,704,128]{2,1,0:T(8,128)(2,1)S(1)}, bf16[1,704,128]{2,1,0:T(8,128)(2,1)S(1)}, u32[]{:S(2)}, u32[]{:S(2)}) collective-permute-start(bf16[1,704,128]{2,1,0:T(8,128)(2,1)S(1)} %get-tuple-element.55), channel_id=1, source_target_pairs={{0,6},{1,7},{2,0},{3,1},{4,2},{5,3},{6,4},{7,5},{8,14},{9,15},{10,... | collective-permute-start | bytes 540680 | tf_op jit(solution)/shard_map/ppermute | solution.py:199
  20.1 2.2 %collective-permute-done.2.refs_3_ = bf16[1,704,128]{2,1,0:T(8,128)(2,1)S(1)} collective-permute-done((bf16[1,704,128]{2,1,0:T(8,128)(2,1)S(1)}, bf16[1,704,128]{2,1,0:T(8,128)(2,1)S(1)}, u32[]{:S(2)}, u32[]{:S(2)}) %collective-permute-start.2) | collective-permute-done | bytes 180256 | tf_op jit(solution)/shard_map/ppermute | solution.py:199
  23.6 1.5 %collective-permute-start.6 = (bf16[2,704,128]{2,1,0:T(8,128)(2,1)S(1)}, bf16[2,704,128]{2,1,0:T(8,128)(2,1)S(1)}, u32[]{:S(2)}, u32[]{:S(2)}) collective-permute-start(bf16[2,704,128]{2,1,0:T(8,128)(2,1)S(1)} %get-tuple-element.62.refs_1_.refs_0_), channel_id=1, source_target_pairs={{0,16},{8,24},{16,0},{24,8},{1,17},{9,25},{17,1},{25,9},{2,18},{10... | collective-permute-start | bytes 1081352 | tf_op jit(solution)/shard_map/ppermute | solution.py:194
  25.9 1.5 %collective-permute-start.7 = (bf16[2,704,128]{2,1,0:T(8,128)(2,1)}, bf16[2,704,128]{2,1,0:T(8,128)(2,1)S(1)}, u32[]{:S(2)}, u32[]{:S(2)}) collective-permute-start(bf16[2,704,128]{2,1,0:T(8,128)(2,1)} %get-tuple-element.64), channel_id=1, source_target_pairs={{0,8},{8,0},{16,24},{24,16},{1,9},{9,1},{17,25},{25,17},{2,10},{10... | collective-permute-start | bytes 1081352 | tf_op jit(solution)/shard_map/ppermute | solution.py:194
  27.4 2.2 %collective-permute-done.5.refs_3_ = bf16[1,704,128]{2,1,0:T(8,128)(2,1)S(1)} collective-permute-done((bf16[1,704,128]{2,1,0:T(8,128)(2,1)S(1)}, bf16[1,704,128]{2,1,0:T(8,128)(2,1)S(1)}, u32[]{:S(2)}, u32[]{:S(2)}) %collective-permute-start.5) | collective-permute-done | bytes 180256 | tf_op jit(solution)/shard_map/ppermute | solution.py:199
  30.3 1.5 %collective-permute-start.8 = (bf16[2,704,128]{2,1,0:T(8,128)(2,1)S(1)}, bf16[2,704,128]{2,1,0:T(8,128)(2,1)S(1)}, u32[]{:S(2)}, u32[]{:S(2)}) collective-permute-start(bf16[2,704,128]{2,1,0:T(8,128)(2,1)S(1)} %get-tuple-element.66.refs_2_.refs_0_), channel_id=1, source_target_pairs={{0,16},{8,24},{16,0},{24,8},{1,17},{9,25},{17,1},{25,9},{2,18},{10... | collective-permute-start | bytes 1081352 | tf_op jit(solution)/shard_map/ppermute | solution.py:194
  32.3 1.3 %collective-permute-done.6.refs_2_ = bf16[2,704,128]{2,1,0:T(8,128)(2,1)S(1)} collective-permute-done((bf16[2,704,128]{2,1,0:T(8,128)(2,1)S(1)}, bf16[2,704,128]{2,1,0:T(8,128)(2,1)S(1)}, u32[]{:S(2)}, u32[]{:S(2)}) %collective-permute-start.6) | collective-permute-done | bytes 360480 | tf_op jit(solution)/shard_map/ppermute | solution.py:194
  34.4 1.5 %collective-permute-start.11 = (bf16[2,704,128]{2,1,0:T(8,128)(2,1)}, bf16[2,704,128]{2,1,0:T(8,128)(2,1)S(1)}, u32[]{:S(2)}, u32[]{:S(2)}) collective-permute-start(bf16[2,704,128]{2,1,0:T(8,128)(2,1)} %get-tuple-element.72), channel_id=1, source_target_pairs={{0,8},{8,0},{16,24},{24,16},{1,9},{9,1},{17,25},{25,17},{2,10},{10... | collective-permute-start | bytes 1081352 | tf_op jit(solution)/shard_map/ppermute | solution.py:194
  37.0 1.9 %pair_stack.4 = (f32[4,2,2,256,128]{4,3,2,1,0:T(8,128)S(1)}, f32[4,256,128]{2,1,0:T(8,128)S(1)}) custom-call(s32[1]{0:T(128)} %bitcast.lower_ref, bf16[4,176,128]{2,1,0:T(8,128)(2,1)S(1)} %copy-done, bf16[2,704,128]{2,1,0:T(8,128)(2,1)S(1)} %get-tuple-element.53.refs_1_.refs_0_, bf16[2,704,128]{2,1,0:T(8,128)(2,1)S(1)} %collective-permute-done.7.refs_1_, ...), custom_call_target="tpu_custom_call" | custom-call | tf_op jit(solution)/shard_map/pair_stack/pallas_call | solution.py:164
  38.9 2.0 %collective-permute-done.8.refs_3_.refs_2_ = bf16[2,704,128]{2,1,0:T(8,128)(2,1)S(1)} collective-permute-done((bf16[2,704,128]{2,1,0:T(8,128)(2,1)S(1)}, bf16[2,704,128]{2,1,0:T(8,128)(2,1)S(1)}, u32[]{:S(2)}, u32[]{:S(2)}) %collective-permute-start.8) | collective-permute-done | bytes 360480 | tf_op jit(solution)/shard_map/ppermute | solution.py:194
  40.9 1.6 %collective-permute-start.16 = (bf16[2,704,128]{2,1,0:T(8,128)(2,1)S(1)}, bf16[2,704,128]{2,1,0:T(8,128)(2,1)S(1)}, u32[]{:S(2)}, u32[]{:S(2)}) collective-permute-start(bf16[2,704,128]{2,1,0:T(8,128)(2,1)S(1)} %get-tuple-element.77), channel_id=1, source_target_pairs={{0,8},{8,0},{16,24},{24,16},{1,9},{9,1},{17,25},{25,17},{2,10},{10... | collective-permute-start | bytes 1081352 | tf_op jit(solution)/shard_map/ppermute | solution.py:194
  42.5 4.1 %collective-permute-done.9.refs_1_ = bf16[1,704,128]{2,1,0:T(8,128)(2,1)S(1)} collective-permute-done((bf16[1,704,128]{2,1,0:T(8,128)(2,1)S(1)}, bf16[1,704,128]{2,1,0:T(8,128)(2,1)S(1)}, u32[]{:S(2)}, u32[]{:S(2)}) %collective-permute-start.9) | collective-permute-done | bytes 180256 | tf_op jit(solution)/shard_map/ppermute | solution.py:199
  47.2 3.3 %collective-permute-done.10.refs_1_ = bf16[1,704,128]{2,1,0:T(8,128)(2,1)S(1)} collective-permute-done((bf16[1,704,128]{2,1,0:T(8,128)(2,1)}, bf16[1,704,128]{2,1,0:T(8,128)(2,1)S(1)}, u32[]{:S(2)}, u32[]{:S(2)}) %collective-permute-start.10) | collective-permute-done | bytes 180256 | tf_op jit(solution)/shard_map/ppermute | solution.py:199
  50.4 1.3 %collective-permute-start.14 = (bf16[1,704,128]{2,1,0:T(8,128)(2,1)S(1)}, bf16[1,704,128]{2,1,0:T(8,128)(2,1)S(1)}, u32[]{:S(2)}, u32[]{:S(2)}) collective-permute-start(bf16[1,704,128]{2,1,0:T(8,128)(2,1)S(1)} %collective-permute-done.10.refs_1_), channel_id=1, source_target_pairs={{0,24},{8,0},{16,8},{24,16},{1,25},{9,1},{17,9},{25,17},{2,26},{10... | collective-permute-start | bytes 540680 | tf_op jit(solution)/shard_map/ppermute | solution.py:190
  51.7 1.7 %collective-permute-start.15 = (bf16[1,704,128]{2,1,0:T(8,128)(2,1)S(1)}, bf16[1,704,128]{2,1,0:T(8,128)(2,1)S(1)}, u32[]{:S(2)}, u32[]{:S(2)}) collective-permute-start(bf16[1,704,128]{2,1,0:T(8,128)(2,1)S(1)} %collective-permute-done.10.refs_1_), channel_id=1, source_target_pairs={{0,16},{8,24},{16,0},{24,8},{1,17},{9,25},{17,1},{25,9},{2,18},{10... | collective-permute-start | bytes 540680 | tf_op jit(solution)/shard_map/ppermute | solution.py:194
  53.4 1.9 %pair_stack.5 = (f32[4,2,2,256,128]{4,3,2,1,0:T(8,128)S(1)}, f32[4,256,128]{2,1,0:T(8,128)S(1)}) custom-call(s32[1]{0:T(128)} %bitcast.lower_ref, bf16[4,176,128]{2,1,0:T(8,128)(2,1)S(1)} %copy-done, bf16[2,704,128]{2,1,0:T(8,128)(2,1)S(1)} %get-tuple-element.62.refs_1_.refs_0_, ...), custom_call_target="tpu_custom_call", output_to_operand_aliasing={{0}: (5, {}), {1}: (6, {})} | custom-call | tf_op jit(solution)/shard_map/pair_stack/pallas_call | solution.py:164
  55.4 1.9 %pair_stack.6 = (f32[4,2,2,256,128]{4,3,2,1,0:T(8,128)S(1)}, f32[4,256,128]{2,1,0:T(8,128)S(1)}) custom-call(s32[1]{0:T(128)} %bitcast.lower_ref, bf16[4,176,128]{2,1,0:T(8,128)(2,1)S(1)} %copy-done, bf16[2,704,128]{2,1,0:T(8,128)(2,1)S(1)} %get-tuple-element.66.refs_2_.refs_0_, ...), custom_call_target="tpu_custom_call", output_to_operand_aliasing={{0}: (5, {}), {1}: (6, {})} | custom-call | tf_op jit(solution)/shard_map/pair_stack/pallas_call | solution.py:164
  57.8 3.5 %collective-permute-done.13.refs_2_ = bf16[1,704,128]{2,1,0:T(8,128)(2,1)S(1)} collective-permute-done((bf16[1,704,128]{2,1,0:T(8,128)(2,1)S(1)}, bf16[1,704,128]{2,1,0:T(8,128)(2,1)S(1)}, u32[]{:S(2)}, u32[]{:S(2)}) %collective-permute-start.13) | collective-permute-done | bytes 180256 | tf_op jit(solution)/shard_map/ppermute | solution.py:194
  61.3 3.0 %pair_stack.7 = (f32[4,2,2,256,128]{4,3,2,1,0:T(8,128)}, f32[4,256,128]{2,1,0:T(8,128)}) custom-call(s32[1]{0:T(128)} %bitcast.lower_ref, bf16[4,176,128]{2,1,0:T(8,128)(2,1)S(1)} %copy-done, bf16[1,704,128]{2,1,0:T(8,128)(2,1)S(1)} %get-tuple-element.69.refs_2_.refs_0_, bf16[1,704,128]{2,1,0:T(8,128)(2,1)S(1)} %collective-permute-done.10.refs_1_, ...), custom_call_target="tpu_custom_call" | custom-call | tf_op jit(solution)/shard_map/pair_stack/pallas_call | solution.py:164
  (31 shorter events, 6.8 us)
Async XLA Ops:
  7.6 3.1 %collective-permute-start = (bf16[4,704,128]{2,1,0:T(8,128)(2,1)S(1)}, bf16[4,704,128]{2,1,0:T(8,128)(2,1)S(1)}, u32[]{:S(2)}, u32[]{:S(2)}) collective-permute-start(bf16[4,704,128]{2,1,0:T(8,128)(2,1)S(1)} %get-tuple-element.44), channel_id=1, source_target_pairs={{0,1},{1,0},{2,3},{3,2},{4,5},{5,4},{6,7},{7,6},{8,9},{9,8},{10,11... | collective-permute-start | bytes 2162696 | tf_op jit(solution)/shard_map/ppermute | solution.py:194
  8.1 10.1 %collective-permute-start.1 = (bf16[1,704,128]{2,1,0:T(8,128)(2,1)S(1)}, bf16[1,704,128]{2,1,0:T(8,128)(2,1)S(1)}, u32[]{:S(2)}, u32[]{:S(2)}) collective-permute-start(bf16[1,704,128]{2,1,0:T(8,128)(2,1)S(1)} %get-tuple-element.46), channel_id=1, source_target_pairs={{0,2},{1,3},{2,4},{3,5},{4,6},{5,7},{6,0},{7,1},{8,10},{9,11},{10,... | collective-permute-start | bytes 540680 | tf_op jit(solution)/shard_map/ppermute | solution.py:199
  10.8 26.2 %copy-start = (bf16[4,176,128]{2,1,0:T(8,128)(2,1)S(1)}, bf16[4,176,128]{2,1,0:T(8,128)(2,1)}, u32[]{:S(2)}) copy-start(bf16[4,176,128]{2,1,0:T(8,128)(2,1)} %constant.11.clone.masks_ref) | copy-start | bytes 540676
  10.9 14.2 %collective-permute-start.3 = (bf16[2,704,128]{2,1,0:T(8,128)(2,1)S(1)}, bf16[2,704,128]{2,1,0:T(8,128)(2,1)S(1)}, u32[]{:S(2)}, u32[]{:S(2)}) collective-permute-start(bf16[2,704,128]{2,1,0:T(8,128)(2,1)S(1)} %get-tuple-element.53.refs_1_.refs_0_), channel_id=1, source_target_pairs={{0,16},{8,24},{16,0},{24,8},{1,17},{9,25},{17,1},{25,9},{2,18},{10... | collective-permute-start | bytes 1081352 | tf_op jit(solution)/shard_map/ppermute | solution.py:194
  13.0 9.3 %collective-permute-start.2 = (bf16[1,704,128]{2,1,0:T(8,128)(2,1)S(1)}, bf16[1,704,128]{2,1,0:T(8,128)(2,1)S(1)}, u32[]{:S(2)}, u32[]{:S(2)}) collective-permute-start(bf16[1,704,128]{2,1,0:T(8,128)(2,1)S(1)} %get-tuple-element.51), channel_id=1, source_target_pairs={{0,2},{1,3},{2,4},{3,5},{4,6},{5,7},{6,0},{7,1},{8,10},{9,11},{10,... | collective-permute-start | bytes 540680 | tf_op jit(solution)/shard_map/ppermute | solution.py:199
  18.2 9.2 %collective-permute-start.4 = (bf16[1,704,128]{2,1,0:T(8,128)(2,1)S(1)}, bf16[1,704,128]{2,1,0:T(8,128)(2,1)S(1)}, u32[]{:S(2)}, u32[]{:S(2)}) collective-permute-start(bf16[1,704,128]{2,1,0:T(8,128)(2,1)S(1)} %get-tuple-element.55), channel_id=1, source_target_pairs={{0,6},{1,7},{2,0},{3,1},{4,2},{5,3},{6,4},{7,5},{8,14},{9,15},{10,... | collective-permute-start | bytes 540680 | tf_op jit(solution)/shard_map/ppermute | solution.py:199
  22.4 7.2 %collective-permute-start.5 = (bf16[1,704,128]{2,1,0:T(8,128)(2,1)S(1)}, bf16[1,704,128]{2,1,0:T(8,128)(2,1)S(1)}, u32[]{:S(2)}, u32[]{:S(2)}) collective-permute-start(bf16[1,704,128]{2,1,0:T(8,128)(2,1)S(1)} %get-tuple-element.60), channel_id=1, source_target_pairs={{0,6},{1,7},{2,0},{3,1},{4,2},{5,3},{6,4},{7,5},{8,14},{9,15},{10,... | collective-permute-start | bytes 540680 | tf_op jit(solution)/shard_map/ppermute | solution.py:199
  23.6 10.0 %collective-permute-start.6 = (bf16[2,704,128]{2,1,0:T(8,128)(2,1)S(1)}, bf16[2,704,128]{2,1,0:T(8,128)(2,1)S(1)}, u32[]{:S(2)}, u32[]{:S(2)}) collective-permute-start(bf16[2,704,128]{2,1,0:T(8,128)(2,1)S(1)} %get-tuple-element.62.refs_1_.refs_0_), channel_id=1, source_target_pairs={{0,16},{8,24},{16,0},{24,8},{1,17},{9,25},{17,1},{25,9},{2,18},{10... | collective-permute-start | bytes 1081352 | tf_op jit(solution)/shard_map/ppermute | solution.py:194
  25.9 11.1 %collective-permute-start.7 = (bf16[2,704,128]{2,1,0:T(8,128)(2,1)}, bf16[2,704,128]{2,1,0:T(8,128)(2,1)S(1)}, u32[]{:S(2)}, u32[]{:S(2)}) collective-permute-start(bf16[2,704,128]{2,1,0:T(8,128)(2,1)} %get-tuple-element.64), channel_id=1, source_target_pairs={{0,8},{8,0},{16,24},{24,16},{1,9},{9,1},{17,25},{25,17},{2,10},{10... | collective-permute-start | bytes 1081352 | tf_op jit(solution)/shard_map/ppermute | solution.py:194
  29.7 0.7 %copy-start.1 = (bf16[1,704,128]{2,1,0:T(8,128)(2,1)}, bf16[1,704,128]{2,1,0:T(8,128)(2,1)S(1)}, u32[]{:S(2)}) copy-start(bf16[1,704,128]{2,1,0:T(8,128)(2,1)S(1)} %get-tuple-element.70) | copy-start | bytes 540676
  30.3 10.6 %collective-permute-start.8 = (bf16[2,704,128]{2,1,0:T(8,128)(2,1)S(1)}, bf16[2,704,128]{2,1,0:T(8,128)(2,1)S(1)}, u32[]{:S(2)}, u32[]{:S(2)}) collective-permute-start(bf16[2,704,128]{2,1,0:T(8,128)(2,1)S(1)} %get-tuple-element.66.refs_2_.refs_0_), channel_id=1, source_target_pairs={{0,16},{8,24},{16,0},{24,8},{1,17},{9,25},{17,1},{25,9},{2,18},{10... | collective-permute-start | bytes 1081352 | tf_op jit(solution)/shard_map/ppermute | solution.py:194
  31.8 14.8 %collective-permute-start.9 = (bf16[1,704,128]{2,1,0:T(8,128)(2,1)S(1)}, bf16[1,704,128]{2,1,0:T(8,128)(2,1)S(1)}, u32[]{:S(2)}, u32[]{:S(2)}) collective-permute-start(bf16[1,704,128]{2,1,0:T(8,128)(2,1)S(1)} %get-tuple-element.68), channel_id=1, source_target_pairs={{0,4},{1,5},{2,6},{3,7},{4,0},{5,1},{6,2},{7,3},{8,12},{9,13},{10,... | collective-permute-start | bytes 540680 | tf_op jit(solution)/shard_map/ppermute | solution.py:199
  34.4 19.0 %collective-permute-start.11 = (bf16[2,704,128]{2,1,0:T(8,128)(2,1)}, bf16[2,704,128]{2,1,0:T(8,128)(2,1)S(1)}, u32[]{:S(2)}, u32[]{:S(2)}) collective-permute-start(bf16[2,704,128]{2,1,0:T(8,128)(2,1)} %get-tuple-element.72), channel_id=1, source_target_pairs={{0,8},{8,0},{16,24},{24,16},{1,9},{9,1},{17,25},{25,17},{2,10},{10... | collective-permute-start | bytes 1081352 | tf_op jit(solution)/shard_map/ppermute | solution.py:194
  35.9 14.5 %collective-permute-start.10 = (bf16[1,704,128]{2,1,0:T(8,128)(2,1)}, bf16[1,704,128]{2,1,0:T(8,128)(2,1)S(1)}, u32[]{:S(2)}, u32[]{:S(2)}) collective-permute-start(bf16[1,704,128]{2,1,0:T(8,128)(2,1)} %copy-done.1), channel_id=1, source_target_pairs={{0,4},{1,5},{2,6},{3,7},{4,0},{5,1},{6,2},{7,3},{8,12},{9,13},{10,... | collective-permute-start | bytes 540680 | tf_op jit(solution)/shard_map/ppermute | solution.py:199
  40.9 14.5 %collective-permute-start.16 = (bf16[2,704,128]{2,1,0:T(8,128)(2,1)S(1)}, bf16[2,704,128]{2,1,0:T(8,128)(2,1)S(1)}, u32[]{:S(2)}, u32[]{:S(2)}) collective-permute-start(bf16[2,704,128]{2,1,0:T(8,128)(2,1)S(1)} %get-tuple-element.77), channel_id=1, source_target_pairs={{0,8},{8,0},{16,24},{24,16},{1,9},{9,1},{17,25},{25,17},{2,10},{10... | collective-permute-start | bytes 1081352 | tf_op jit(solution)/shard_map/ppermute | solution.py:194
  46.6 8.7 %collective-permute-start.12 = (bf16[1,704,128]{2,1,0:T(8,128)(2,1)S(1)}, bf16[1,704,128]{2,1,0:T(8,128)(2,1)S(1)}, u32[]{:S(2)}, u32[]{:S(2)}) collective-permute-start(bf16[1,704,128]{2,1,0:T(8,128)(2,1)S(1)} %get-tuple-element.69.refs_2_.refs_0_), channel_id=1, source_target_pairs={{0,16},{8,24},{16,0},{24,8},{1,17},{9,25},{17,1},{25,9},{2,18},{10... | collective-permute-start | bytes 540680 | tf_op jit(solution)/shard_map/ppermute | solution.py:194
  50.4 7.0 %collective-permute-start.14 = (bf16[1,704,128]{2,1,0:T(8,128)(2,1)S(1)}, bf16[1,704,128]{2,1,0:T(8,128)(2,1)S(1)}, u32[]{:S(2)}, u32[]{:S(2)}) collective-permute-start(bf16[1,704,128]{2,1,0:T(8,128)(2,1)S(1)} %collective-permute-done.10.refs_1_), channel_id=1, source_target_pairs={{0,24},{8,0},{16,8},{24,16},{1,25},{9,1},{17,9},{25,17},{2,26},{10... | collective-permute-start | bytes 540680 | tf_op jit(solution)/shard_map/ppermute | solution.py:190
  51.7 6.1 %collective-permute-start.15 = (bf16[1,704,128]{2,1,0:T(8,128)(2,1)S(1)}, bf16[1,704,128]{2,1,0:T(8,128)(2,1)S(1)}, u32[]{:S(2)}, u32[]{:S(2)}) collective-permute-start(bf16[1,704,128]{2,1,0:T(8,128)(2,1)S(1)} %collective-permute-done.10.refs_1_), channel_id=1, source_target_pairs={{0,16},{8,24},{16,0},{24,8},{1,17},{9,25},{17,1},{25,9},{2,18},{10... | collective-permute-start | bytes 540680 | tf_op jit(solution)/shard_map/ppermute | solution.py:194
  55.4 6.0 %collective-permute-start.13 = (bf16[1,704,128]{2,1,0:T(8,128)(2,1)S(1)}, bf16[1,704,128]{2,1,0:T(8,128)(2,1)S(1)}, u32[]{:S(2)}, u32[]{:S(2)}) collective-permute-start(bf16[1,704,128]{2,1,0:T(8,128)(2,1)S(1)} %get-tuple-element.76), channel_id=1, source_target_pairs={{0,8},{8,0},{16,24},{24,16},{1,9},{9,1},{17,25},{25,17},{2,10},{10... | collective-permute-start | bytes 540680 | tf_op jit(solution)/shard_map/ppermute | solution.py:194

commit v4 on v3

--- a/solution.py
+++ b/solution.py
@@ -91,9 +91,15 @@
     )(records)
 
 
-def pair_kernel(chunk_count, operand_count, lower_ref, masks_ref, *refs):
-    near_out, far_out, near_sum, far_sum = refs[-4:]
-    near_before, far_before = refs[operand_count:-4] or (None, None)
+def pair_kernel(chunk_count, operand_count, streamed, lower_ref, masks_ref, *refs):
+    if streamed:
+        near_hbm, far_hbm, near_sum, far_sum, near_out, far_out, sems = refs[-7:]
+        near_before, far_before = refs[operand_count:-7] or (None, None)
+        slot = pl.program_id(0)
+    else:
+        near_out, far_out, near_sum, far_sum = refs[-4:]
+        near_before, far_before = refs[operand_count:-4] or (None, None)
+        slot = 0
     arrays = [refs[start : start + chunk_count] for start in range(0, operand_count, chunk_count)]
     own_refs, near_refs, far_refs = arrays[0], arrays[1:-1], arrays[-1]
     width = own_refs[0].shape[2]
@@ -136,16 +142,33 @@
         for r in range(1 + len(near_refs)):
             for p in range(2):
                 start = (2 * h + p) * width
-                place = (0, h, r, pl.ds(p, width, stride=2), slice(None))
+                place = (h, r, pl.ds(p, width, stride=2), slice(None))
                 total = near_sum[start : start + width, r * width : (r + 1) * width]
-                near_out[place] = total if near_before is None else total + near_before[place]
+                near_out[(slot,) + place] = total if near_before is None else total + near_before[(0,) + place]
     for p in range(2):
-        place = (0, pl.ds(p, width, stride=2), slice(None))
+        place = (pl.ds(p, width, stride=2), slice(None))
         total = far_sum[p * width : (p + 1) * width, :]
-        far_out[place] = total if far_before is None else total + far_before[place]
-
-
-def pair_stack(own, near, far, window_count, before=(), in_place=False):
+        far_out[(slot,) + place] = total if far_before is None else total + far_before[(0,) + place]
+    if streamed:
+
+        def writes(g):
+            return [
+                pltpu.make_async_copy(near_out.at[g, 0], near_hbm.at[g, 0], sems.at[g, 0]),
+                pltpu.make_async_copy(near_out.at[g, 1], near_hbm.at[g, 1], sems.at[g, 1]),
+                pltpu.make_async_copy(far_out.at[g], far_hbm.at[g], sems.at[g, 2]),
+            ]
+
+        for write in writes(slot):
+            write.start()
+
+        @pl.when(slot == pl.num_programs(0) - 1)
+        def _():
+            for g in range(near_out.shape[0]):
+                for write in writes(g):
+                    write.wait()
+
+
+def pair_stack(own, near, far, window_count, before=(), in_place=False, streamed=False):
     all_rows, width = own[0].shape[1:]
     rows = 4 * window_count
     per_device = all_rows // rows
@@ -162,18 +185,27 @@
         pl.BlockSpec((1, 2 * width, width), lambda g, *_: (g, 0, 0)),
     ]
     return pl.pallas_call(
-        functools.partial(pair_kernel, len(own), len(operands)),
+        functools.partial(pair_kernel, len(own), len(operands), streamed),
         grid_spec=pltpu.PrefetchScalarGridSpec(
             num_scalar_prefetch=1,
             grid=(per_device,),
             in_specs=[pl.BlockSpec((4, rows, width), lambda g, *_: (0, 0, 0))]
             + [pl.BlockSpec((chunk.shape[0], rows, width), lambda g, *_: (0, g, 0)) for chunk in operands]
             + (sums if before else []),
-            out_specs=sums,
+            out_specs=[pl.BlockSpec(memory_space=pltpu.HBM)] * 2 if streamed else sums,
             scratch_shapes=[
                 pltpu.VMEM((4 * width, rounds * width), jnp.float32),
                 pltpu.VMEM((2 * width, width), jnp.float32),
-            ],
+            ]
+            + (
+                [
+                    pltpu.VMEM((per_device, 2, rounds, 2 * width, width), jnp.float32),
+                    pltpu.VMEM((per_device, 2 * width, width), jnp.float32),
+                    pltpu.SemaphoreType.DMA((per_device, 3)),
+                ]
+                if streamed
+                else []
+            ),
         ),
         out_shape=[
             jax.ShapeDtypeStruct((per_device, 2, rounds, 2 * width, width), jnp.float32),
@@ -250,51 +282,59 @@
 
     after_one = moved(after_one, 1)
     core = swapped(core, "tm", 1)
+    here_far = far_swap(here)
     core_after, core_last, core_before, core_here = (core[i : i + 1] for i in range(4))
-    token, here, after_two, last, before_two = phase(
+    token, also, after_two, last, before_two = phase(
         [token],
-        [here, core_here, core_after, core_last, core_before],
-        [2, 1, 1, 1],
-        [("always", 0, 0, 0), ("always", 1, 0, 1), ("always", 2, 1, 0), ("always", 3, 2, 0), ("always", 4, 3, 0)],
+        [core_here, core_after, core_last, core_before],
+        [1, 1, 1, 1],
+        [("always", i, i, 0) for i in range(4)],
     )
     after_two = moved(after_two, 1)
-    here_far = far_swap(here)
+    also_far = far_swap(also)
 
     token, after_one, before = phase([token, after_one, before])
     before_one = moved(before, 3)
 
-    token, before_two, after = phase([token, before_two], [after_one, after_two], [2], [("always", 0, 0, 0), ("always", 1, 0, 1)])
-    before_two = moved(before_two, 3)
-    after_far = far_swap(after)
-
     token, here_send = near_payload([token], here, here_far)
     here_near = near_swap(here_send)
 
-    token, before_one, opposite = phase([token, before_one, opposite])
+    token, after = phase([token], [after_one, after_two], [2], [("always", 0, 0, 0), ("always", 1, 0, 1)])
+    after_far = far_swap(after)
+
+    token, before_two, also_send = near_payload([token, before_two], also, also_far)
+    before_two = moved(before_two, 3)
+    also_near = near_swap(also_send)
+
+
+    token, before_one, opposite, here_near = phase([token, before_one, opposite, here_near])
     two = moved(opposite, 2)
 
-    token, last, before = phase([token, last], [before_one, before_two], [2], [("always", 0, 0, 0), ("always", 1, 0, 1)])
+    token, last, also_near, before = phase([token, last, also_near], [before_one, before_two], [2], [("always", 0, 0, 0), ("always", 1, 0, 1)])
     last = moved(last, 2)
     before_far = far_swap(before)
 
-    token, after_send = near_payload([token], after, after_far)
+    token, here, after_send = near_payload([token, here], after, after_far)
     after_near = near_swap(after_send)
-    near_sum, far_sum = stack([here], [[here_near]], [here_far])
+    near_sum, far_sum = stack([here, also], [[here_near, also_near]], [here_far, also_far])
 
     token, far_sum, before_send = near_payload([token, far_sum], before, before_far)
     before_near = near_swap(before_send)
 
     token, two = phase([token, two])
     two_far = far_swap(two)
-    near_sum, far_sum = grow([after], [[after_near]], [after_far], before=(near_sum, far_sum))
-
-    token, far_sum, two_send = near_payload([token, far_sum], two, two_far)
+
+    token, two_send = near_payload([token], two, two_far)
     two_near = near_swap(two_send)
 
     last_near = shifted(last, -1)
     last_far = far_swap(last)
-    near_sum, far_sum = grow([before], [[before_near]], [before_far], before=(near_sum, far_sum))
-    return stack([two, last], [[two_near, last_near]], [two_far, last_far], before=(near_sum, far_sum))
+    near_sum, far_sum = grow(
+        [after, before], [[after_near, before_near]], [after_far, before_far], before=(near_sum, far_sum)
+    )
+    return stack(
+        [two, last], [[two_near, last_near]], [two_far, last_far], before=(near_sum, far_sum), streamed=True
+    )
 
 
 def plain_stack(records):

time: 64.5 us -> 62.3 us (0.966)
  starting transfers between devices: 22.8 us -> 26 us
  Pallas kernels: 17.4 us -> 14.5 us
  waiting for transfers between devices: 22.7 us -> 20.8 us
  local copies, waits for them, and re-layouts: 0.71 us -> 0.06 us
    ppermute x6, waiting for transfers between devices: 15.4 us -> 9.77 us  [moved(): lax.ppermute(value, 'tm', [(source, (source + 2 * steps) % count) for sou...]
    ppermute x10 -> x12, waiting for transfers between devices: 7.25 us -> 10.8 us  [swapped(): lax.ppermute(value, axis, [(source, source ^ bit) for source in range(lax...]
    ppermute x6, starting transfers between devices: 8.99 us -> 10.9 us  [moved(): lax.ppermute(value, 'tm', [(source, (source + 2 * steps) % count) for sou...]
    pallas_call x10 -> x11, Pallas kernels: 1.69 us -> 0.21 us  [phase(): pl.pallas_call(functools.partial(phase_kernel, len(kept), len(made), tupl...]
    pallas_call x4 -> x3, Pallas kernels: 8.71 us -> 7.34 us  [pair_stack(): pl.pallas_call(functools.partial(pair_kernel, len(own), len(operands), st...]
    ppermute x10 -> x12, starting transfers between devices: 12.5 us -> 13.3 us  [swapped(): lax.ppermute(value, axis, [(source, source ^ bit) for source in range(lax...]
    unnamed x4 -> x2, local copies, waits for them, and re-layouts: 0.66 us -> 0.01 us
  transfers between devices with their start and end apart: 17 -> 19, of which waited for: 9 -> 10; matrix products, arithmetic and copies ran while one was open for 0% -> 0% of each run, Pallas kernels for 12% -> 8%
where the time goes in v4:
time: 62.3 us; the launch traced here: 62.2 us
  starting transfers between devices  26 us (42%)
  waiting for transfers between devices  20.8 us (33%)
  Pallas kernels  14.5 us (23%)
  between operations  0.74 us (1%)
    ppermute x12, starting transfers between devices, swapped(): lax.ppermute(value, axis, [(source, source ^ bit) for source in range(lax...  13.3 us
    ppermute x6, starting transfers between devices, moved(): lax.ppermute(value, 'tm', [(source, (source + 2 * steps) % count) for sou...  10.9 us
    ppermute x12, waiting for transfers between devices, swapped(): lax.ppermute(value, axis, [(source, source ^ bit) for source in range(lax...  10.8 us
    ppermute x6, waiting for transfers between devices, moved(): lax.ppermute(value, 'tm', [(source, (source + 2 * steps) % count) for sou...  9.77 us
    pallas_call x3, Pallas kernels, pair_stack(): pl.pallas_call(functools.partial(pair_kernel, len(own), len(operands), st...  7.34 us
    pallas_call x1, Pallas kernels, whiten(): pl.pallas_call(functools.partial(whiten_kernel, scale, step_windows, coun...  6.98 us
    ppermute x1, starting transfers between devices, shifted(): lax.ppermute(value, 'chan', [(source, (source + steps) % count) for sourc...  1.85 us
  transfers between devices with their start and end apart: 19, of which 10 were waited for; matrix products, arithmetic and copies ran while one was open for 0% of the time, Pallas kernels for 8%

profile of v4, /device:TPU:0, one launch (start us, length us, event | category | flops | bytes accessed | tf_op | source)
XLA Modules:
  0.0 62.2 jit_solution(5031613761922147501)
XLA Ops:
  0.6 7.0 %whiten.1 = (bf16[1,704,128]{2,1,0:T(8,128)(2,1)S(1)}, bf16[1,704,128]{2,1,0:T(8,128)(2,1)S(1)}, bf16[1,704,128]{2,1,0:T(8,128)(2,1)S(1)}, bf16[1,704,128]{2,1,0:T(8,128)(2,1)S(1)}, bf16[4,704,128]{2,1,0:T(8,128)(2,1)S(1)}) custom-call(bf16[44,128,1024]{2,1,0:T(8,128)(2,1)} %records_hbm.1), custom_call_target="tpu_custom_call" | custom-call | tf_op jit(solution)/shard_map/whiten/pallas_call | solution.py:78
  8.1 2.6 %collective-permute-start.1 = (bf16[1,704,128]{2,1,0:T(8,128)(2,1)S(1)}, bf16[1,704,128]{2,1,0:T(8,128)(2,1)S(1)}, u32[]{:S(2)}, u32[]{:S(2)}) collective-permute-start(bf16[1,704,128]{2,1,0:T(8,128)(2,1)S(1)} %get-tuple-element.47), channel_id=1, source_target_pairs={{0,2},{1,3},{2,4},{3,5},{4,6},{5,7},{6,0},{7,1},{8,10},{9,11},{10,... | collective-permute-start | bytes 540680 | tf_op jit(solution)/shard_map/ppermute | solution.py:231
  10.8 1.5 %collective-permute-start.2 = (bf16[1,704,128]{2,1,0:T(8,128)(2,1)S(1)}, bf16[1,704,128]{2,1,0:T(8,128)(2,1)S(1)}, u32[]{:S(2)}, u32[]{:S(2)}) collective-permute-start(bf16[1,704,128]{2,1,0:T(8,128)(2,1)S(1)} %get-tuple-element.50.refs_1_), channel_id=1, source_target_pairs={{0,16},{8,24},{16,0},{24,8},{1,17},{9,25},{17,1},{25,9},{2,18},{10... | collective-permute-start | bytes 540680 | tf_op jit(solution)/shard_map/ppermute | solution.py:226
  12.4 1.6 %collective-permute-start.3 = (bf16[1,704,128]{2,1,0:T(8,128)(2,1)S(1)}, bf16[1,704,128]{2,1,0:T(8,128)(2,1)S(1)}, u32[]{:S(2)}, u32[]{:S(2)}) collective-permute-start(bf16[1,704,128]{2,1,0:T(8,128)(2,1)S(1)} %get-tuple-element.53), channel_id=1, source_target_pairs={{0,2},{1,3},{2,4},{3,5},{4,6},{5,7},{6,0},{7,1},{8,10},{9,11},{10,... | collective-permute-start | bytes 540680 | tf_op jit(solution)/shard_map/ppermute | solution.py:231
  14.6 3.6 %collective-permute-done.1.refs_1_ = bf16[1,704,128]{2,1,0:T(8,128)(2,1)S(1)} collective-permute-done((bf16[1,704,128]{2,1,0:T(8,128)(2,1)S(1)}, bf16[1,704,128]{2,1,0:T(8,128)(2,1)S(1)}, u32[]{:S(2)}, u32[]{:S(2)}) %collective-permute-start.1) | collective-permute-done | bytes 180256 | tf_op jit(solution)/shard_map/ppermute | solution.py:231
  18.2 1.7 %collective-permute-start.6 = (bf16[1,704,128]{2,1,0:T(8,128)(2,1)S(1)}, bf16[1,704,128]{2,1,0:T(8,128)(2,1)S(1)}, u32[]{:S(2)}, u32[]{:S(2)}) collective-permute-start(bf16[1,704,128]{2,1,0:T(8,128)(2,1)S(1)} %get-tuple-element.60), channel_id=1, source_target_pairs={{0,8},{8,0},{16,24},{24,16},{1,9},{9,1},{17,25},{25,17},{2,10},{10... | collective-permute-start | bytes 540680 | tf_op jit(solution)/shard_map/ppermute | solution.py:226
  19.9 2.1 %collective-permute-start.5 = (bf16[1,704,128]{2,1,0:T(8,128)(2,1)S(1)}, bf16[1,704,128]{2,1,0:T(8,128)(2,1)S(1)}, u32[]{:S(2)}, u32[]{:S(2)}) collective-permute-start(bf16[1,704,128]{2,1,0:T(8,128)(2,1)S(1)} %get-tuple-element.58), channel_id=1, source_target_pairs={{0,6},{1,7},{2,0},{3,1},{4,2},{5,3},{6,4},{7,5},{8,14},{9,15},{10,... | collective-permute-start | bytes 540680 | tf_op jit(solution)/shard_map/ppermute | solution.py:231
  22.1 1.5 %collective-permute-start.7 = (bf16[1,704,128]{2,1,0:T(8,128)(2,1)S(1)}, bf16[1,704,128]{2,1,0:T(8,128)(2,1)S(1)}, u32[]{:S(2)}, u32[]{:S(2)}) collective-permute-start(bf16[1,704,128]{2,1,0:T(8,128)(2,1)S(1)} %get-tuple-element.63), channel_id=1, source_target_pairs={{0,8},{8,0},{16,24},{24,16},{1,9},{9,1},{17,25},{25,17},{2,10},{10... | collective-permute-start | bytes 540680 | tf_op jit(solution)/shard_map/ppermute | solution.py:226
  23.6 1.6 %collective-permute-start.8 = (bf16[1,704,128]{2,1,0:T(8,128)(2,1)S(1)}, bf16[1,704,128]{2,1,0:T(8,128)(2,1)S(1)}, u32[]{:S(2)}, u32[]{:S(2)}) collective-permute-start(bf16[1,704,128]{2,1,0:T(8,128)(2,1)S(1)} %get-tuple-element.65), channel_id=1, source_target_pairs={{0,6},{1,7},{2,0},{3,1},{4,2},{5,3},{6,4},{7,5},{8,14},{9,15},{10,... | collective-permute-start | bytes 540680 | tf_op jit(solution)/shard_map/ppermute | solution.py:231
  25.2 1.5 %collective-permute-start.9 = (bf16[2,704,128]{2,1,0:T(8,128)(2,1)S(1)}, bf16[2,704,128]{2,1,0:T(8,128)(2,1)S(1)}, u32[]{:S(2)}, u32[]{:S(2)}) collective-permute-start(bf16[2,704,128]{2,1,0:T(8,128)(2,1)S(1)} %get-tuple-element.67.refs_2_.refs_0_), channel_id=1, source_target_pairs={{0,16},{8,24},{16,0},{24,8},{1,17},{9,25},{17,1},{25,9},{2,18},{10... | collective-permute-start | bytes 1081352 | tf_op jit(solution)/shard_map/ppermute | solution.py:226
  26.7 1.6 %collective-permute-done.7.refs_2_ = bf16[1,704,128]{2,1,0:T(8,128)(2,1)S(1)} collective-permute-done((bf16[1,704,128]{2,1,0:T(8,128)(2,1)S(1)}, bf16[1,704,128]{2,1,0:T(8,128)(2,1)S(1)}, u32[]{:S(2)}, u32[]{:S(2)}) %collective-permute-start.7) | collective-permute-done | bytes 180256 | tf_op jit(solution)/shard_map/ppermute | solution.py:226
  28.3 1.3 %collective-permute-done.8.refs_4_ = bf16[1,704,128]{2,1,0:T(8,128)(2,1)S(1)} collective-permute-done((bf16[1,704,128]{2,1,0:T(8,128)(2,1)S(1)}, bf16[1,704,128]{2,1,0:T(8,128)(2,1)S(1)}, u32[]{:S(2)}, u32[]{:S(2)}) %collective-permute-start.8) | collective-permute-done | bytes 180256 | tf_op jit(solution)/shard_map/ppermute | solution.py:231
  29.6 1.6 %collective-permute-start.10 = (bf16[2,704,128]{2,1,0:T(8,128)(2,1)S(1)}, bf16[2,704,128]{2,1,0:T(8,128)(2,1)S(1)}, u32[]{:S(2)}, u32[]{:S(2)}) collective-permute-start(bf16[2,704,128]{2,1,0:T(8,128)(2,1)S(1)} %get-tuple-element.73.refs_2_.refs_1_), channel_id=1, source_target_pairs={{0,16},{8,24},{16,0},{24,8},{1,17},{9,25},{17,1},{25,9},{2,18},{10... | collective-permute-start | bytes 1081352 | tf_op jit(solution)/shard_map/ppermute | solution.py:226
  31.1 2.2 %collective-permute-start.11 = (bf16[1,704,128]{2,1,0:T(8,128)(2,1)S(1)}, bf16[1,704,128]{2,1,0:T(8,128)(2,1)S(1)}, u32[]{:S(2)}, u32[]{:S(2)}) collective-permute-start(bf16[1,704,128]{2,1,0:T(8,128)(2,1)S(1)} %get-tuple-element.75), channel_id=1, source_target_pairs={{0,4},{1,5},{2,6},{3,7},{4,0},{5,1},{6,2},{7,3},{8,12},{9,13},{10,... | collective-permute-start | bytes 540680 | tf_op jit(solution)/shard_map/ppermute | solution.py:231
  34.1 2.5 %collective-permute-done.9.refs_3_.refs_4_ = bf16[2,704,128]{2,1,0:T(8,128)(2,1)S(1)} collective-permute-done((bf16[2,704,128]{2,1,0:T(8,128)(2,1)S(1)}, bf16[2,704,128]{2,1,0:T(8,128)(2,1)S(1)}, u32[]{:S(2)}, u32[]{:S(2)}) %collective-permute-start.9) | collective-permute-done | bytes 360480 | tf_op jit(solution)/shard_map/ppermute | solution.py:226
  37.1 1.8 %pair_stack.3 = (f32[4,2,2,256,128]{4,3,2,1,0:T(8,128)S(1)}, f32[4,256,128]{2,1,0:T(8,128)S(1)}) custom-call(s32[1]{0:T(128)} %bitcast.lower_ref, bf16[4,176,128]{2,1,0:T(8,128)(2,1)S(1)} %copy-done, bf16[1,704,128]{2,1,0:T(8,128)(2,1)S(1)} %get-tuple-element.69.refs_0_, bf16[1,704,128]{2,1,0:T(8,128)(2,1)S(1)} %get-tuple-element.56.refs_2_.refs_1_, ...), custom_call_target="tpu_custom_call" | custom-call | tf_op jit(solution)/shard_map/pair_stack/pallas_call | solution.py:187
  38.9 3.4 %collective-permute-done.10.refs_3_.refs_5_ = bf16[2,704,128]{2,1,0:T(8,128)(2,1)S(1)} collective-permute-done((bf16[2,704,128]{2,1,0:T(8,128)(2,1)S(1)}, bf16[2,704,128]{2,1,0:T(8,128)(2,1)S(1)}, u32[]{:S(2)}, u32[]{:S(2)}) %collective-permute-start.10) | collective-permute-done | bytes 360480 | tf_op jit(solution)/shard_map/ppermute | solution.py:226
  43.0 2.9 %collective-permute-done.11.refs_1_ = bf16[1,704,128]{2,1,0:T(8,128)(2,1)S(1)} collective-permute-done((bf16[1,704,128]{2,1,0:T(8,128)(2,1)S(1)}, bf16[1,704,128]{2,1,0:T(8,128)(2,1)S(1)}, u32[]{:S(2)}, u32[]{:S(2)}) %collective-permute-start.11) | collective-permute-done | bytes 180256 | tf_op jit(solution)/shard_map/ppermute | solution.py:231
  46.4 2.0 %collective-permute-done.12.refs_1_ = bf16[1,704,128]{2,1,0:T(8,128)(2,1)S(1)} collective-permute-done((bf16[1,704,128]{2,1,0:T(8,128)(2,1)S(1)}, bf16[1,704,128]{2,1,0:T(8,128)(2,1)S(1)}, u32[]{:S(2)}, u32[]{:S(2)}) %collective-permute-start.12) | collective-permute-done | bytes 180256 | tf_op jit(solution)/shard_map/ppermute | solution.py:231
  48.4 1.9 %collective-permute-start.15 = (bf16[1,704,128]{2,1,0:T(8,128)(2,1)S(1)}, bf16[1,704,128]{2,1,0:T(8,128)(2,1)S(1)}, u32[]{:S(2)}, u32[]{:S(2)}) collective-permute-start(bf16[1,704,128]{2,1,0:T(8,128)(2,1)S(1)} %collective-permute-done.12.refs_1_), channel_id=1, source_target_pairs={{0,24},{8,0},{16,8},{24,16},{1,25},{9,1},{17,9},{25,17},{2,26},{10... | collective-permute-start | bytes 540680 | tf_op jit(solution)/shard_map/ppermute | solution.py:222
  50.2 1.5 %collective-permute-start.16 = (bf16[1,704,128]{2,1,0:T(8,128)(2,1)S(1)}, bf16[1,704,128]{2,1,0:T(8,128)(2,1)S(1)}, u32[]{:S(2)}, u32[]{:S(2)}) collective-permute-start(bf16[1,704,128]{2,1,0:T(8,128)(2,1)S(1)} %collective-permute-done.12.refs_1_), channel_id=1, source_target_pairs={{0,16},{8,24},{16,0},{24,8},{1,17},{9,25},{17,1},{25,9},{2,18},{10... | collective-permute-start | bytes 540680 | tf_op jit(solution)/shard_map/ppermute | solution.py:226
  53.0 2.9 %pair_stack.4 = (f32[4,2,2,256,128]{4,3,2,1,0:T(8,128)S(1)}, f32[4,256,128]{2,1,0:T(8,128)S(1)}) custom-call(s32[1]{0:T(128)} %bitcast.lower_ref, bf16[4,176,128]{2,1,0:T(8,128)(2,1)S(1)} %copy-done, bf16[2,704,128]{2,1,0:T(8,128)(2,1)S(1)} %get-tuple-element.67.refs_2_.refs_0_, ...), custom_call_target="tpu_custom_call", output_to_operand_aliasing={{0}: (8, {}), {1}: (9, {})} | custom-call | tf_op jit(solution)/shard_map/pair_stack/pallas_call | solution.py:187
  56.4 3.1 %collective-permute-done.14.refs_2_ = bf16[1,704,128]{2,1,0:T(8,128)(2,1)S(1)} collective-permute-done((bf16[1,704,128]{2,1,0:T(8,128)(2,1)S(1)}, bf16[1,704,128]{2,1,0:T(8,128)(2,1)S(1)}, u32[]{:S(2)}, u32[]{:S(2)}) %collective-permute-start.14) | collective-permute-done | bytes 180256 | tf_op jit(solution)/shard_map/ppermute | solution.py:226
  59.5 2.7 %pair_stack.5 = (f32[4,2,2,256,128]{4,3,2,1,0:T(8,128)}, f32[4,256,128]{2,1,0:T(8,128)}) custom-call(s32[1]{0:T(128)} %bitcast.lower_ref, bf16[4,176,128]{2,1,0:T(8,128)(2,1)S(1)} %copy-done, bf16[1,704,128]{2,1,0:T(8,128)(2,1)S(1)} %get-tuple-element.76.refs_1_.refs_0_, bf16[1,704,128]{2,1,0:T(8,128)(2,1)S(1)} %collective-permute-done.12.refs_1_, ...), custom_call_target="tpu_custom_call" | custom-call | tf_op jit(solution)/shard_map/pair_stack/pallas_call | solution.py:187
  (33 shorter events, 5.5 us)
Async XLA Ops:
  7.6 4.7 %collective-permute-start = (bf16[4,704,128]{2,1,0:T(8,128)(2,1)S(1)}, bf16[4,704,128]{2,1,0:T(8,128)(2,1)S(1)}, u32[]{:S(2)}, u32[]{:S(2)}) collective-permute-start(bf16[4,704,128]{2,1,0:T(8,128)(2,1)S(1)} %get-tuple-element.45), channel_id=1, source_target_pairs={{0,1},{1,0},{2,3},{3,2},{4,5},{5,4},{6,7},{7,6},{8,9},{9,8},{10,11... | collective-permute-start | bytes 2162696 | tf_op jit(solution)/shard_map/ppermute | solution.py:226
  8.1 10.1 %collective-permute-start.1 = (bf16[1,704,128]{2,1,0:T(8,128)(2,1)S(1)}, bf16[1,704,128]{2,1,0:T(8,128)(2,1)S(1)}, u32[]{:S(2)}, u32[]{:S(2)}) collective-permute-start(bf16[1,704,128]{2,1,0:T(8,128)(2,1)S(1)} %get-tuple-element.47), channel_id=1, source_target_pairs={{0,2},{1,3},{2,4},{3,5},{4,6},{5,7},{6,0},{7,1},{8,10},{9,11},{10,... | collective-permute-start | bytes 540680 | tf_op jit(solution)/shard_map/ppermute | solution.py:231
  10.8 7.4 %collective-permute-start.2 = (bf16[1,704,128]{2,1,0:T(8,128)(2,1)S(1)}, bf16[1,704,128]{2,1,0:T(8,128)(2,1)S(1)}, u32[]{:S(2)}, u32[]{:S(2)}) collective-permute-start(bf16[1,704,128]{2,1,0:T(8,128)(2,1)S(1)} %get-tuple-element.50.refs_1_), channel_id=1, source_target_pairs={{0,16},{8,24},{16,0},{24,8},{1,17},{9,25},{17,1},{25,9},{2,18},{10... | collective-permute-start | bytes 540680 | tf_op jit(solution)/shard_map/ppermute | solution.py:226
  12.4 24.7 %copy-start = (bf16[4,176,128]{2,1,0:T(8,128)(2,1)S(1)}, bf16[4,176,128]{2,1,0:T(8,128)(2,1)}, u32[]{:S(2)}) copy-start(bf16[4,176,128]{2,1,0:T(8,128)(2,1)} %constant.11.clone.masks_ref) | copy-start | bytes 540676
  12.4 9.6 %collective-permute-start.3 = (bf16[1,704,128]{2,1,0:T(8,128)(2,1)S(1)}, bf16[1,704,128]{2,1,0:T(8,128)(2,1)S(1)}, u32[]{:S(2)}, u32[]{:S(2)}) collective-permute-start(bf16[1,704,128]{2,1,0:T(8,128)(2,1)S(1)} %get-tuple-element.53), channel_id=1, source_target_pairs={{0,2},{1,3},{2,4},{3,5},{4,6},{5,7},{6,0},{7,1},{8,10},{9,11},{10,... | collective-permute-start | bytes 540680 | tf_op jit(solution)/shard_map/ppermute | solution.py:231
  14.0 8.0 %collective-permute-start.4 = (bf16[1,704,128]{2,1,0:T(8,128)(2,1)S(1)}, bf16[1,704,128]{2,1,0:T(8,128)(2,1)S(1)}, u32[]{:S(2)}, u32[]{:S(2)}) collective-permute-start(bf16[1,704,128]{2,1,0:T(8,128)(2,1)S(1)} %get-tuple-element.56.refs_2_.refs_1_), channel_id=1, source_target_pairs={{0,16},{8,24},{16,0},{24,8},{1,17},{9,25},{17,1},{25,9},{2,18},{10... | collective-permute-start | bytes 540680 | tf_op jit(solution)/shard_map/ppermute | solution.py:226
  18.2 8.5 %collective-permute-start.6 = (bf16[1,704,128]{2,1,0:T(8,128)(2,1)S(1)}, bf16[1,704,128]{2,1,0:T(8,128)(2,1)S(1)}, u32[]{:S(2)}, u32[]{:S(2)}) collective-permute-start(bf16[1,704,128]{2,1,0:T(8,128)(2,1)S(1)} %get-tuple-element.60), channel_id=1, source_target_pairs={{0,8},{8,0},{16,24},{24,16},{1,9},{9,1},{17,25},{25,17},{2,10},{10... | collective-permute-start | bytes 540680 | tf_op jit(solution)/shard_map/ppermute | solution.py:226
  19.9 6.8 %collective-permute-start.5 = (bf16[1,704,128]{2,1,0:T(8,128)(2,1)S(1)}, bf16[1,704,128]{2,1,0:T(8,128)(2,1)S(1)}, u32[]{:S(2)}, u32[]{:S(2)}) collective-permute-start(bf16[1,704,128]{2,1,0:T(8,128)(2,1)S(1)} %get-tuple-element.58), channel_id=1, source_target_pairs={{0,6},{1,7},{2,0},{3,1},{4,2},{5,3},{6,4},{7,5},{8,14},{9,15},{10,... | collective-permute-start | bytes 540680 | tf_op jit(solution)/shard_map/ppermute | solution.py:231
  22.1 6.2 %collective-permute-start.7 = (bf16[1,704,128]{2,1,0:T(8,128)(2,1)S(1)}, bf16[1,704,128]{2,1,0:T(8,128)(2,1)S(1)}, u32[]{:S(2)}, u32[]{:S(2)}) collective-permute-start(bf16[1,704,128]{2,1,0:T(8,128)(2,1)S(1)} %get-tuple-element.63), channel_id=1, source_target_pairs={{0,8},{8,0},{16,24},{24,16},{1,9},{9,1},{17,25},{25,17},{2,10},{10... | collective-permute-start | bytes 540680 | tf_op jit(solution)/shard_map/ppermute | solution.py:226
  23.6 6.0 %collective-permute-start.8 = (bf16[1,704,128]{2,1,0:T(8,128)(2,1)S(1)}, bf16[1,704,128]{2,1,0:T(8,128)(2,1)S(1)}, u32[]{:S(2)}, u32[]{:S(2)}) collective-permute-start(bf16[1,704,128]{2,1,0:T(8,128)(2,1)S(1)} %get-tuple-element.65), channel_id=1, source_target_pairs={{0,6},{1,7},{2,0},{3,1},{4,2},{5,3},{6,4},{7,5},{8,14},{9,15},{10,... | collective-permute-start | bytes 540680 | tf_op jit(solution)/shard_map/ppermute | solution.py:231
  25.2 11.3 %collective-permute-start.9 = (bf16[2,704,128]{2,1,0:T(8,128)(2,1)S(1)}, bf16[2,704,128]{2,1,0:T(8,128)(2,1)S(1)}, u32[]{:S(2)}, u32[]{:S(2)}) collective-permute-start(bf16[2,704,128]{2,1,0:T(8,128)(2,1)S(1)} %get-tuple-element.67.refs_2_.refs_0_), channel_id=1, source_target_pairs={{0,16},{8,24},{16,0},{24,8},{1,17},{9,25},{17,1},{25,9},{2,18},{10... | collective-permute-start | bytes 1081352 | tf_op jit(solution)/shard_map/ppermute | solution.py:226
  29.6 12.8 %collective-permute-start.10 = (bf16[2,704,128]{2,1,0:T(8,128)(2,1)S(1)}, bf16[2,704,128]{2,1,0:T(8,128)(2,1)S(1)}, u32[]{:S(2)}, u32[]{:S(2)}) collective-permute-start(bf16[2,704,128]{2,1,0:T(8,128)(2,1)S(1)} %get-tuple-element.73.refs_2_.refs_1_), channel_id=1, source_target_pairs={{0,16},{8,24},{16,0},{24,8},{1,17},{9,25},{17,1},{25,9},{2,18},{10... | collective-permute-start | bytes 1081352 | tf_op jit(solution)/shard_map/ppermute | solution.py:226
  31.1 14.7 %collective-permute-start.11 = (bf16[1,704,128]{2,1,0:T(8,128)(2,1)S(1)}, bf16[1,704,128]{2,1,0:T(8,128)(2,1)S(1)}, u32[]{:S(2)}, u32[]{:S(2)}) collective-permute-start(bf16[1,704,128]{2,1,0:T(8,128)(2,1)S(1)} %get-tuple-element.75), channel_id=1, source_target_pairs={{0,4},{1,5},{2,6},{3,7},{4,0},{5,1},{6,2},{7,3},{8,12},{9,13},{10,... | collective-permute-start | bytes 540680 | tf_op jit(solution)/shard_map/ppermute | solution.py:231
  33.3 15.1 %collective-permute-start.12 = (bf16[1,704,128]{2,1,0:T(8,128)(2,1)S(1)}, bf16[1,704,128]{2,1,0:T(8,128)(2,1)S(1)}, u32[]{:S(2)}, u32[]{:S(2)}) collective-permute-start(bf16[1,704,128]{2,1,0:T(8,128)(2,1)S(1)} %get-tuple-element.77), channel_id=1, source_target_pairs={{0,4},{1,5},{2,6},{3,7},{4,0},{5,1},{6,2},{7,3},{8,12},{9,13},{10,... | collective-permute-start | bytes 540680 | tf_op jit(solution)/shard_map/ppermute | solution.py:231
  36.6 16.4 %collective-permute-start.17 = (bf16[2,704,128]{2,1,0:T(8,128)(2,1)S(1)}, bf16[2,704,128]{2,1,0:T(8,128)(2,1)S(1)}, u32[]{:S(2)}, u32[]{:S(2)}) collective-permute-start(bf16[2,704,128]{2,1,0:T(8,128)(2,1)S(1)} %get-tuple-element.80), channel_id=1, source_target_pairs={{0,8},{8,0},{16,24},{24,16},{1,9},{9,1},{17,25},{25,17},{2,10},{10... | collective-permute-start | bytes 1081352 | tf_op jit(solution)/shard_map/ppermute | solution.py:226
  42.4 10.6 %collective-permute-start.18 = (bf16[2,704,128]{2,1,0:T(8,128)(2,1)S(1)}, bf16[2,704,128]{2,1,0:T(8,128)(2,1)S(1)}, u32[]{:S(2)}, u32[]{:S(2)}) collective-permute-start(bf16[2,704,128]{2,1,0:T(8,128)(2,1)S(1)} %get-tuple-element.81), channel_id=1, source_target_pairs={{0,8},{8,0},{16,24},{24,16},{1,9},{9,1},{17,25},{25,17},{2,10},{10... | collective-permute-start | bytes 1081352 | tf_op jit(solution)/shard_map/ppermute | solution.py:226
  45.8 5.9 %collective-permute-start.13 = (bf16[1,704,128]{2,1,0:T(8,128)(2,1)S(1)}, bf16[1,704,128]{2,1,0:T(8,128)(2,1)S(1)}, u32[]{:S(2)}, u32[]{:S(2)}) collective-permute-start(bf16[1,704,128]{2,1,0:T(8,128)(2,1)S(1)} %get-tuple-element.76.refs_1_.refs_0_), channel_id=1, source_target_pairs={{0,16},{8,24},{16,0},{24,8},{1,17},{9,25},{17,1},{25,9},{2,18},{10... | collective-permute-start | bytes 540680 | tf_op jit(solution)/shard_map/ppermute | solution.py:226
  48.4 7.8 %collective-permute-start.15 = (bf16[1,704,128]{2,1,0:T(8,128)(2,1)S(1)}, bf16[1,704,128]{2,1,0:T(8,128)(2,1)S(1)}, u32[]{:S(2)}, u32[]{:S(2)}) collective-permute-start(bf16[1,704,128]{2,1,0:T(8,128)(2,1)S(1)} %collective-permute-done.12.refs_1_), channel_id=1, source_target_pairs={{0,24},{8,0},{16,8},{24,16},{1,25},{9,1},{17,9},{25,17},{2,26},{10... | collective-permute-start | bytes 540680 | tf_op jit(solution)/shard_map/ppermute | solution.py:222
  50.2 6.2 %collective-permute-start.16 = (bf16[1,704,128]{2,1,0:T(8,128)(2,1)S(1)}, bf16[1,704,128]{2,1,0:T(8,128)(2,1)S(1)}, u32[]{:S(2)}, u32[]{:S(2)}) collective-permute-start(bf16[1,704,128]{2,1,0:T(8,128)(2,1)S(1)} %collective-permute-done.12.refs_1_), channel_id=1, source_target_pairs={{0,16},{8,24},{16,0},{24,8},{1,17},{9,25},{17,1},{25,9},{2,18},{10... | collective-permute-start | bytes 540680 | tf_op jit(solution)/shard_map/ppermute | solution.py:226
  51.8 7.7 %collective-permute-start.14 = (bf16[1,704,128]{2,1,0:T(8,128)(2,1)S(1)}, bf16[1,704,128]{2,1,0:T(8,128)(2,1)S(1)}, u32[]{:S(2)}, u32[]{:S(2)}) collective-permute-start(bf16[1,704,128]{2,1,0:T(8,128)(2,1)S(1)} %get-tuple-element.79), channel_id=1, source_target_pairs={{0,8},{8,0},{16,24},{24,16},{1,9},{9,1},{17,25},{25,17},{2,10},{10... | collective-permute-start | bytes 540680 | tf_op jit(solution)/shard_map/ppermute | solution.py:226

commit v5 on v3

--- a/solution.py
+++ b/solution.py
@@ -91,40 +91,46 @@
     )(records)
 
 
+def rotated(block):
+    middle = block.shape[0] // 2
+    return jnp.concatenate([block[middle:], block[:middle]], axis=0)
+
+
+def product(left, right):
+    value = lax.dot_general(left, right, (((0,), (0,)), ((), ())), preferred_element_type=jnp.float32)
+    return value.astype(jnp.bfloat16).astype(jnp.float32)
+
+
+def both_halves(own, masks_ref):
+    turned = rotated(own)
+    return jnp.concatenate(
+        [own * masks_ref[0], turned * masks_ref[1], own * masks_ref[2], turned * masks_ref[3]], axis=1
+    )
+
+
+def far_product(own, far, lower, masks_ref):
+    half = jnp.where(lower, 0, 1)
+    first = jnp.where(lower, own, far)
+    second = jnp.where(lower, far, own)
+    left = jnp.concatenate([first * masks_ref[2 * half], rotated(first) * masks_ref[2 * half + 1]], axis=1)
+    return product(left, second)
+
+
 def pair_kernel(chunk_count, operand_count, lower_ref, masks_ref, *refs):
     near_out, far_out, near_sum, far_sum = refs[-4:]
     near_before, far_before = refs[operand_count:-4] or (None, None)
     arrays = [refs[start : start + chunk_count] for start in range(0, operand_count, chunk_count)]
     own_refs, near_refs, far_refs = arrays[0], arrays[1:-1], arrays[-1]
-    width = own_refs[0].shape[2]
+    width = masks_ref.shape[2]
     lower = lower_ref[0] > 0
-    half = jnp.where(lower, 0, 1)
-
-    def rotated(block):
-        middle = block.shape[0] // 2
-        return jnp.concatenate([block[middle:], block[:middle]], axis=0)
-
-    def product(left, right):
-        value = lax.dot_general(left, right, (((0,), (0,)), ((), ())), preferred_element_type=jnp.float32)
-        return value.astype(jnp.bfloat16).astype(jnp.float32)
 
     first_group = True
     for chunk in range(chunk_count):
         for group in range(own_refs[chunk].shape[0]):
             own = own_refs[chunk][group]
-            turned = rotated(own)
-            left = jnp.concatenate(
-                [own * masks_ref[0], turned * masks_ref[1], own * masks_ref[2], turned * masks_ref[3]], axis=1
-            )
             right = jnp.concatenate([own] + [near[chunk][group] for near in near_refs], axis=1)
-            near = product(left, right)
-            far = far_refs[chunk][group]
-            first = jnp.where(lower, own, far)
-            second = jnp.where(lower, far, own)
-            far_left = jnp.concatenate(
-                [first * masks_ref[2 * half], rotated(first) * masks_ref[2 * half + 1]], axis=1
-            )
-            far = product(far_left, second)
+            near = product(both_halves(own, masks_ref), right)
+            far = far_product(own, far_refs[chunk][group], lower, masks_ref)
             if first_group:
                 near_sum[...] = near
                 far_sum[...] = far
@@ -145,30 +151,106 @@
         far_out[place] = total if far_before is None else total + far_before[place]
 
 
+def last_kernel(count, finish_far, lower_ref, masks_ref, *refs):
+    own_refs, mate_refs = refs[:count], refs[count : 2 * count]
+    if finish_far:
+        near_before, far_before, near_hbm, far_hbm, near_sum, far_sum, near_stage, far_stage, sems = refs[2 * count :]
+    else:
+        near_before, _, near_hbm, near_sum, near_stage, sems = refs[2 * count :]
+    rows, width = masks_ref.shape[1:]
+    lower = lower_ref[0] > 0
+    r = 0 if finish_far else 1
+    writes = []
+    for g in range(near_stage.shape[0]):
+        span = slice(g * rows, (g + 1) * rows)
+        near_total = near_sum.at[g % 2]
+        groups = [(c, i) for c in range(count) for i in range(own_refs[c].shape[0])]
+        for place, (chunk, group) in enumerate(groups):
+            own, mate = own_refs[chunk][group, span], mate_refs[chunk][group, span]
+            near = product(both_halves(own, masks_ref), own if finish_far else mate)
+            near_total[...] = near if place == 0 else near_total[...] + near
+            if finish_far:
+                far = far_product(own, mate, lower, masks_ref)
+                far_sum[g % 2] = far if place == 0 else far_sum[g % 2] + far
+        for h in range(2):
+            for p in range(2):
+                start = (2 * h + p) * width
+                pair_rows = pl.ds(p, width, stride=2)
+                near_stage[g, h, pair_rows, :] = (
+                    near_total[start : start + width, :] + near_before[g, h, r, pair_rows, :]
+                )
+            writes.append(pltpu.make_async_copy(near_stage.at[g, h], near_hbm.at[g, h, r], sems.at[g, h]))
+            writes[-1].start()
+        if finish_far:
+            for p in range(2):
+                pair_rows = pl.ds(p, width, stride=2)
+                far_stage[g, pair_rows, :] = (
+                    far_sum[g % 2, p * width : (p + 1) * width, :] + far_before[g, pair_rows, :]
+                )
+            writes.append(pltpu.make_async_copy(far_stage.at[g], far_hbm.at[g], sems.at[g, 2]))
+            writes[-1].start()
+    for write in writes:
+        write.wait()
+
+
+def stack_tables(window_count, width):
+    lower = (lax.axis_index("chan") < lax.axis_size("chan") // 2).astype(jnp.int32).reshape(1)
+    index = np.arange(4 * window_count)
+    part, half = index // (2 * window_count), index // window_count % 2
+    sign = np.where(part == 0, 1.0, -1.0)
+    masks = np.stack([half == 0, (half == 0) * sign, half == 1, (half == 1) * sign])
+    masks = np.broadcast_to(masks[:, :, None], masks.shape + (width,)).astype(ml_dtypes.bfloat16)
+    return lower, jnp.asarray(masks)
+
+
+def last_stack(own, mates, window_count, near_before, far_before=None, near_done=None):
+    per_device, _, rounds, _, width = near_before.shape
+    finish_far = near_done is None
+    assert rounds == 2
+    vmem, hbm = pl.BlockSpec(memory_space=pltpu.VMEM), pl.BlockSpec(memory_space=pltpu.HBM)
+    near_shape = jax.ShapeDtypeStruct(near_before.shape, jnp.float32)
+    far_shape = jax.ShapeDtypeStruct((per_device, 2 * width, width), jnp.float32)
+    near_scratch = [pltpu.VMEM((2, 4 * width, width), jnp.float32)]
+    far_scratch = [pltpu.VMEM((2, 2 * width, width), jnp.float32)] if finish_far else []
+    near_stage = [pltpu.VMEM((per_device, 2, 2 * width, width), jnp.float32)]
+    far_stage = [pltpu.VMEM((per_device, 2 * width, width), jnp.float32)] if finish_far else []
+    operands = list(own) + list(mates) + [near_before]
+    return pl.pallas_call(
+        functools.partial(last_kernel, len(own), finish_far),
+        in_specs=[pl.BlockSpec(memory_space=pltpu.SMEM)]
+        + [vmem] * (1 + len(operands))
+        + [vmem if finish_far else hbm],
+        out_specs=[hbm, hbm] if finish_far else hbm,
+        out_shape=[near_shape, far_shape] if finish_far else near_shape,
+        scratch_shapes=near_scratch
+        + far_scratch
+        + near_stage
+        + far_stage
+        + [pltpu.SemaphoreType.DMA((per_device, 3))],
+        input_output_aliases={} if finish_far else {2 + len(operands): 0},
+        compiler_params=pltpu.CompilerParams(vmem_limit_bytes=VMEM_LIMIT),
+        name="last_stack",
+    )(*stack_tables(window_count, width), *operands, far_before if finish_far else near_done)
+
+
 def pair_stack(own, near, far, window_count, before=(), in_place=False):
     all_rows, width = own[0].shape[1:]
     rows = 4 * window_count
     per_device = all_rows // rows
     rounds = 1 + len(near)
-    lower = (lax.axis_index("chan") < lax.axis_size("chan") // 2).astype(jnp.int32).reshape(1)
-    index = np.arange(rows)
-    part, half = index // (2 * window_count), index // window_count % 2
-    sign = np.where(part == 0, 1.0, -1.0)
-    masks = np.stack([half == 0, (half == 0) * sign, half == 1, (half == 1) * sign])
-    masks = np.broadcast_to(masks[:, :, None], (4, rows, width)).astype(ml_dtypes.bfloat16)
+    lower, masks = stack_tables(window_count, width)
     operands = [chunk for chunks in [own] + near + [far] for chunk in chunks]
     sums = [
         pl.BlockSpec((1, 2, rounds, 2 * width, width), lambda g, *_: (g, 0, 0, 0, 0)),
         pl.BlockSpec((1, 2 * width, width), lambda g, *_: (g, 0, 0)),
     ]
+    blocks = [pl.BlockSpec((chunk.shape[0], rows, width), lambda g, *_: (0, g, 0)) for chunk in operands]
     return pl.pallas_call(
         functools.partial(pair_kernel, len(own), len(operands)),
         grid_spec=pltpu.PrefetchScalarGridSpec(
             num_scalar_prefetch=1,
             grid=(per_device,),
-            in_specs=[pl.BlockSpec((4, rows, width), lambda g, *_: (0, 0, 0))]
-            + [pl.BlockSpec((chunk.shape[0], rows, width), lambda g, *_: (0, g, 0)) for chunk in operands]
-            + (sums if before else []),
+            in_specs=[pl.BlockSpec((4, rows, width), lambda g, *_: (0, 0, 0))] + blocks + (sums if before else []),
             out_specs=sums,
             scratch_shapes=[
                 pltpu.VMEM((4 * width, rounds * width), jnp.float32),
@@ -182,7 +264,7 @@
         input_output_aliases={2 + len(operands) + i: i for i in range(len(before) if in_place else 0)},
         compiler_params=pltpu.CompilerParams(vmem_limit_bytes=VMEM_LIMIT),
         name="pair_stack",
-    )(lower, jnp.asarray(masks), *operands, *before)
+    )(lower, masks, *operands, *before)
 
 
 def shifted(value, steps):
@@ -250,51 +332,59 @@
 
     after_one = moved(after_one, 1)
     core = swapped(core, "tm", 1)
+    here_far = far_swap(here)
     core_after, core_last, core_before, core_here = (core[i : i + 1] for i in range(4))
-    token, here, after_two, last, before_two = phase(
+    token, also, after_two, last, before_two = phase(
         [token],
-        [here, core_here, core_after, core_last, core_before],
-        [2, 1, 1, 1],
-        [("always", 0, 0, 0), ("always", 1, 0, 1), ("always", 2, 1, 0), ("always", 3, 2, 0), ("always", 4, 3, 0)],
+        [core_here, core_after, core_last, core_before],
+        [1, 1, 1, 1],
+        [("always", i, i, 0) for i in range(4)],
     )
     after_two = moved(after_two, 1)
-    here_far = far_swap(here)
+    also_far = far_swap(also)
 
     token, after_one, before = phase([token, after_one, before])
     before_one = moved(before, 3)
 
-    token, before_two, after = phase([token, before_two], [after_one, after_two], [2], [("always", 0, 0, 0), ("always", 1, 0, 1)])
-    before_two = moved(before_two, 3)
-    after_far = far_swap(after)
-
     token, here_send = near_payload([token], here, here_far)
     here_near = near_swap(here_send)
 
-    token, before_one, opposite = phase([token, before_one, opposite])
+    token, after = phase([token], [after_one, after_two], [2], [("always", 0, 0, 0), ("always", 1, 0, 1)])
+    after_far = far_swap(after)
+
+    token, before_two, also_send = near_payload([token, before_two], also, also_far)
+    before_two = moved(before_two, 3)
+    also_near = near_swap(also_send)
+
+
+    token, before_one, opposite, here_near = phase([token, before_one, opposite, here_near])
     two = moved(opposite, 2)
 
-    token, last, before = phase([token, last], [before_one, before_two], [2], [("always", 0, 0, 0), ("always", 1, 0, 1)])
+    token, last, also_near, before = phase([token, last, also_near], [before_one, before_two], [2], [("always", 0, 0, 0), ("always", 1, 0, 1)])
     last = moved(last, 2)
     before_far = far_swap(before)
 
-    token, after_send = near_payload([token], after, after_far)
+    token, here, after_send = near_payload([token, here], after, after_far)
     after_near = near_swap(after_send)
-    near_sum, far_sum = stack([here], [[here_near]], [here_far])
+    near_sum, far_sum = stack([here, also], [[here_near, also_near]], [here_far, also_far])
 
     token, far_sum, before_send = near_payload([token, far_sum], before, before_far)
     before_near = near_swap(before_send)
 
     token, two = phase([token, two])
     two_far = far_swap(two)
-    near_sum, far_sum = grow([after], [[after_near]], [after_far], before=(near_sum, far_sum))
-
-    token, far_sum, two_send = near_payload([token, far_sum], two, two_far)
+
+    token, two_send = near_payload([token], two, two_far)
     two_near = near_swap(two_send)
 
     last_near = shifted(last, -1)
     last_far = far_swap(last)
-    near_sum, far_sum = grow([before], [[before_near]], [before_far], before=(near_sum, far_sum))
-    return stack([two, last], [[two_near, last_near]], [two_far, last_far], before=(near_sum, far_sum))
+    near_sum, far_sum = grow(
+        [after, before], [[after_near, before_near]], [after_far, before_far], before=(near_sum, far_sum)
+    )
+    near_done, far_done = last_stack([two, last], [two_far, last_far], window_count, near_sum, far_before=far_sum)
+    near_done = last_stack([two, last], [two_near, last_near], window_count, near_sum, near_done=near_done)
+    return near_done, far_done
 
 
 def plain_stack(records):

time: 64.5 us -> 61.4 us (0.952)
  waiting for transfers between devices: 22.7 us -> 20 us
  starting transfers between devices: 22.8 us -> 24.9 us
  Pallas kernels: 17.4 us -> 15.4 us
  local copies, waits for them, and re-layouts: 0.71 us -> 0.06 us
    ppermute x6, waiting for transfers between devices: 15.4 us -> 9.77 us  [moved(): lax.ppermute(value, 'tm', [(source, (source + 2 * steps) % count) for sou...]
    pallas_call x4 -> x2, Pallas kernels: 8.71 us -> 4.69 us  [pair_stack(): pl.pallas_call(functools.partial(pair_kernel, len(own), len(operands)), g...]
    pallas_call x0 -> x2, Pallas kernels: none -> 3.51 us  [last_stack(): pl.pallas_call(functools.partial(last_kernel, len(own), finish_far), in_s...]
    ppermute x10 -> x12, waiting for transfers between devices: 7.25 us -> 10.2 us  [swapped(): lax.ppermute(value, axis, [(source, source ^ bit) for source in range(lax...]
    ppermute x6, starting transfers between devices: 8.99 us -> 10.9 us  [moved(): lax.ppermute(value, 'tm', [(source, (source + 2 * steps) % count) for sou...]
    ppermute x1, starting transfers between devices: 1.28 us -> 2.86 us  [shifted(): lax.ppermute(value, 'chan', [(source, (source + steps) % count) for sourc...]
    pallas_call x10 -> x11, Pallas kernels: 1.69 us -> 0.21 us  [phase(): pl.pallas_call(functools.partial(phase_kernel, len(kept), len(made), tupl...]
    ppermute x10 -> x12, starting transfers between devices: 12.5 us -> 11.1 us  [swapped(): lax.ppermute(value, axis, [(source, source ^ bit) for source in range(lax...]
  transfers between devices with their start and end apart: 17 -> 19, of which waited for: 9 -> 9; matrix products, arithmetic and copies ran while one was open for 0% -> 0% of each run, Pallas kernels for 12% -> 11%
where the time goes in v5:
time: 61.4 us; the launch traced here: 61.1 us
  starting transfers between devices  24.9 us (41%)
  waiting for transfers between devices  20 us (33%)
  Pallas kernels  15.4 us (25%)
  between operations  0.79 us (1%)
    ppermute x12, starting transfers between devices, swapped(): lax.ppermute(value, axis, [(source, source ^ bit) for source in range(lax...  11.1 us
    ppermute x6, starting transfers between devices, moved(): lax.ppermute(value, 'tm', [(source, (source + 2 * steps) % count) for sou...  10.9 us
    ppermute x12, waiting for transfers between devices, swapped(): lax.ppermute(value, axis, [(source, source ^ bit) for source in range(lax...  10.2 us
    ppermute x6, waiting for transfers between devices, moved(): lax.ppermute(value, 'tm', [(source, (source + 2 * steps) % count) for sou...  9.77 us
    pallas_call x1, Pallas kernels, whiten(): pl.pallas_call(functools.partial(whiten_kernel, scale, step_windows, coun...  6.98 us
    pallas_call x2, Pallas kernels, pair_stack(): pl.pallas_call(functools.partial(pair_kernel, len(own), len(operands)), g...  4.69 us
    pallas_call x2, Pallas kernels, last_stack(): pl.pallas_call(functools.partial(last_kernel, len(own), finish_far), in_s...  3.51 us
    ppermute x1, starting transfers between devices, shifted(): lax.ppermute(value, 'chan', [(source, (source + steps) % count) for sourc...  2.86 us
  transfers between devices with their start and end apart: 19, of which 9 were waited for; matrix products, arithmetic and copies ran while one was open for 0% of the time, Pallas kernels for 11%

profile of v5, /device:TPU:0, one launch (start us, length us, event | category | flops | bytes accessed | tf_op | source)
XLA Modules:
  0.0 61.1 jit_solution(1123910196564312731)
XLA Ops:
  0.6 7.0 %whiten.1 = (bf16[1,704,128]{2,1,0:T(8,128)(2,1)S(1)}, bf16[1,704,128]{2,1,0:T(8,128)(2,1)S(1)}, bf16[1,704,128]{2,1,0:T(8,128)(2,1)S(1)}, bf16[1,704,128]{2,1,0:T(8,128)(2,1)S(1)}, bf16[4,704,128]{2,1,0:T(8,128)(2,1)S(1)}) custom-call(bf16[44,128,1024]{2,1,0:T(8,128)(2,1)} %records_hbm.1), custom_call_target="tpu_custom_call" | custom-call | tf_op jit(solution)/shard_map/whiten/pallas_call | solution.py:78
  8.1 2.6 %collective-permute-start.1 = (bf16[1,704,128]{2,1,0:T(8,128)(2,1)S(1)}, bf16[1,704,128]{2,1,0:T(8,128)(2,1)S(1)}, u32[]{:S(2)}, u32[]{:S(2)}) collective-permute-start(bf16[1,704,128]{2,1,0:T(8,128)(2,1)S(1)} %get-tuple-element.47), channel_id=1, source_target_pairs={{0,2},{1,3},{2,4},{3,5},{4,6},{5,7},{6,0},{7,1},{8,10},{9,11},{10,... | collective-permute-start | bytes 540680 | tf_op jit(solution)/shard_map/ppermute | solution.py:281
  10.8 1.5 %collective-permute-start.2 = (bf16[1,704,128]{2,1,0:T(8,128)(2,1)S(1)}, bf16[1,704,128]{2,1,0:T(8,128)(2,1)S(1)}, u32[]{:S(2)}, u32[]{:S(2)}) collective-permute-start(bf16[1,704,128]{2,1,0:T(8,128)(2,1)S(1)} %get-tuple-element.50.refs_1_), channel_id=1, source_target_pairs={{0,16},{8,24},{16,0},{24,8},{1,17},{9,25},{17,1},{25,9},{2,18},{10... | collective-permute-start | bytes 540680 | tf_op jit(solution)/shard_map/ppermute | solution.py:276
  12.4 1.6 %collective-permute-start.3 = (bf16[1,704,128]{2,1,0:T(8,128)(2,1)S(1)}, bf16[1,704,128]{2,1,0:T(8,128)(2,1)S(1)}, u32[]{:S(2)}, u32[]{:S(2)}) collective-permute-start(bf16[1,704,128]{2,1,0:T(8,128)(2,1)S(1)} %get-tuple-element.53), channel_id=1, source_target_pairs={{0,2},{1,3},{2,4},{3,5},{4,6},{5,7},{6,0},{7,1},{8,10},{9,11},{10,... | collective-permute-start | bytes 540680 | tf_op jit(solution)/shard_map/ppermute | solution.py:281
  14.6 3.6 %collective-permute-done.1.refs_1_ = bf16[1,704,128]{2,1,0:T(8,128)(2,1)S(1)} collective-permute-done((bf16[1,704,128]{2,1,0:T(8,128)(2,1)S(1)}, bf16[1,704,128]{2,1,0:T(8,128)(2,1)S(1)}, u32[]{:S(2)}, u32[]{:S(2)}) %collective-permute-start.1) | collective-permute-done | bytes 180256 | tf_op jit(solution)/shard_map/ppermute | solution.py:281
  18.2 1.7 %collective-permute-start.6 = (bf16[1,704,128]{2,1,0:T(8,128)(2,1)S(1)}, bf16[1,704,128]{2,1,0:T(8,128)(2,1)S(1)}, u32[]{:S(2)}, u32[]{:S(2)}) collective-permute-start(bf16[1,704,128]{2,1,0:T(8,128)(2,1)S(1)} %get-tuple-element.60), channel_id=1, source_target_pairs={{0,8},{8,0},{16,24},{24,16},{1,9},{9,1},{17,25},{25,17},{2,10},{10... | collective-permute-start | bytes 540680 | tf_op jit(solution)/shard_map/ppermute | solution.py:276
  19.9 2.1 %collective-permute-start.5 = (bf16[1,704,128]{2,1,0:T(8,128)(2,1)S(1)}, bf16[1,704,128]{2,1,0:T(8,128)(2,1)S(1)}, u32[]{:S(2)}, u32[]{:S(2)}) collective-permute-start(bf16[1,704,128]{2,1,0:T(8,128)(2,1)S(1)} %get-tuple-element.58), channel_id=1, source_target_pairs={{0,6},{1,7},{2,0},{3,1},{4,2},{5,3},{6,4},{7,5},{8,14},{9,15},{10,... | collective-permute-start | bytes 540680 | tf_op jit(solution)/shard_map/ppermute | solution.py:281
  22.1 1.5 %collective-permute-start.7 = (bf16[1,704,128]{2,1,0:T(8,128)(2,1)S(1)}, bf16[1,704,128]{2,1,0:T(8,128)(2,1)S(1)}, u32[]{:S(2)}, u32[]{:S(2)}) collective-permute-start(bf16[1,704,128]{2,1,0:T(8,128)(2,1)S(1)} %get-tuple-element.63), channel_id=1, source_target_pairs={{0,8},{8,0},{16,24},{24,16},{1,9},{9,1},{17,25},{25,17},{2,10},{10... | collective-permute-start | bytes 540680 | tf_op jit(solution)/shard_map/ppermute | solution.py:276
  23.6 1.6 %collective-permute-start.8 = (bf16[1,704,128]{2,1,0:T(8,128)(2,1)S(1)}, bf16[1,704,128]{2,1,0:T(8,128)(2,1)S(1)}, u32[]{:S(2)}, u32[]{:S(2)}) collective-permute-start(bf16[1,704,128]{2,1,0:T(8,128)(2,1)S(1)} %get-tuple-element.65), channel_id=1, source_target_pairs={{0,6},{1,7},{2,0},{3,1},{4,2},{5,3},{6,4},{7,5},{8,14},{9,15},{10,... | collective-permute-start | bytes 540680 | tf_op jit(solution)/shard_map/ppermute | solution.py:281
  25.2 1.5 %collective-permute-start.9 = (bf16[2,704,128]{2,1,0:T(8,128)(2,1)S(1)}, bf16[2,704,128]{2,1,0:T(8,128)(2,1)S(1)}, u32[]{:S(2)}, u32[]{:S(2)}) collective-permute-start(bf16[2,704,128]{2,1,0:T(8,128)(2,1)S(1)} %get-tuple-element.67.refs_2_.refs_0_), channel_id=1, source_target_pairs={{0,16},{8,24},{16,0},{24,8},{1,17},{9,25},{17,1},{25,9},{2,18},{10... | collective-permute-start | bytes 1081352 | tf_op jit(solution)/shard_map/ppermute | solution.py:276
  26.7 1.6 %collective-permute-done.7.refs_2_ = bf16[1,704,128]{2,1,0:T(8,128)(2,1)S(1)} collective-permute-done((bf16[1,704,128]{2,1,0:T(8,128)(2,1)S(1)}, bf16[1,704,128]{2,1,0:T(8,128)(2,1)S(1)}, u32[]{:S(2)}, u32[]{:S(2)}) %collective-permute-start.7) | collective-permute-done | bytes 180256 | tf_op jit(solution)/shard_map/ppermute | solution.py:276
  28.3 1.3 %collective-permute-done.8.refs_4_ = bf16[1,704,128]{2,1,0:T(8,128)(2,1)S(1)} collective-permute-done((bf16[1,704,128]{2,1,0:T(8,128)(2,1)S(1)}, bf16[1,704,128]{2,1,0:T(8,128)(2,1)S(1)}, u32[]{:S(2)}, u32[]{:S(2)}) %collective-permute-start.8) | collective-permute-done | bytes 180256 | tf_op jit(solution)/shard_map/ppermute | solution.py:281
  29.6 1.6 %collective-permute-start.10 = (bf16[2,704,128]{2,1,0:T(8,128)(2,1)S(1)}, bf16[2,704,128]{2,1,0:T(8,128)(2,1)S(1)}, u32[]{:S(2)}, u32[]{:S(2)}) collective-permute-start(bf16[2,704,128]{2,1,0:T(8,128)(2,1)S(1)} %get-tuple-element.73.refs_2_.refs_1_), channel_id=1, source_target_pairs={{0,16},{8,24},{16,0},{24,8},{1,17},{9,25},{17,1},{25,9},{2,18},{10... | collective-permute-start | bytes 1081352 | tf_op jit(solution)/shard_map/ppermute | solution.py:276
  31.1 2.2 %collective-permute-start.11 = (bf16[1,704,128]{2,1,0:T(8,128)(2,1)S(1)}, bf16[1,704,128]{2,1,0:T(8,128)(2,1)S(1)}, u32[]{:S(2)}, u32[]{:S(2)}) collective-permute-start(bf16[1,704,128]{2,1,0:T(8,128)(2,1)S(1)} %get-tuple-element.75), channel_id=1, source_target_pairs={{0,4},{1,5},{2,6},{3,7},{4,0},{5,1},{6,2},{7,3},{8,12},{9,13},{10,... | collective-permute-start | bytes 540680 | tf_op jit(solution)/shard_map/ppermute | solution.py:281
  34.1 2.5 %collective-permute-done.9.refs_3_.refs_4_ = bf16[2,704,128]{2,1,0:T(8,128)(2,1)S(1)} collective-permute-done((bf16[2,704,128]{2,1,0:T(8,128)(2,1)S(1)}, bf16[2,704,128]{2,1,0:T(8,128)(2,1)S(1)}, u32[]{:S(2)}, u32[]{:S(2)}) %collective-permute-start.9) | collective-permute-done | bytes 360480 | tf_op jit(solution)/shard_map/ppermute | solution.py:276
  37.1 1.8 %pair_stack.2 = (f32[4,2,2,256,128]{4,3,2,1,0:T(8,128)S(1)}, f32[4,256,128]{2,1,0:T(8,128)S(1)}) custom-call(s32[1]{0:T(128)} %bitcast.lower_ref, bf16[4,176,128]{2,1,0:T(8,128)(2,1)S(1)} %copy-done, bf16[1,704,128]{2,1,0:T(8,128)(2,1)S(1)} %get-tuple-element.69.refs_0_, bf16[1,704,128]{2,1,0:T(8,128)(2,1)S(1)} %get-tuple-element.56.refs_2_.refs_1_, ...), custom_call_target="tpu_custom_call" | custom-call | tf_op jit(solution)/shard_map/pair_stack/pallas_call | solution.py:248
  38.9 3.4 %collective-permute-done.10.refs_3_.refs_5_ = bf16[2,704,128]{2,1,0:T(8,128)(2,1)S(1)} collective-permute-done((bf16[2,704,128]{2,1,0:T(8,128)(2,1)S(1)}, bf16[2,704,128]{2,1,0:T(8,128)(2,1)S(1)}, u32[]{:S(2)}, u32[]{:S(2)}) %collective-permute-start.10) | collective-permute-done | bytes 360480 | tf_op jit(solution)/shard_map/ppermute | solution.py:276
  43.0 2.9 %collective-permute-done.11.refs_1_ = bf16[1,704,128]{2,1,0:T(8,128)(2,1)S(1)} collective-permute-done((bf16[1,704,128]{2,1,0:T(8,128)(2,1)S(1)}, bf16[1,704,128]{2,1,0:T(8,128)(2,1)S(1)}, u32[]{:S(2)}, u32[]{:S(2)}) %collective-permute-start.11) | collective-permute-done | bytes 180256 | tf_op jit(solution)/shard_map/ppermute | solution.py:281
  46.4 2.0 %collective-permute-done.12.refs_1_ = bf16[1,704,128]{2,1,0:T(8,128)(2,1)S(1)} collective-permute-done((bf16[1,704,128]{2,1,0:T(8,128)(2,1)S(1)}, bf16[1,704,128]{2,1,0:T(8,128)(2,1)S(1)}, u32[]{:S(2)}, u32[]{:S(2)}) %collective-permute-start.12) | collective-permute-done | bytes 180256 | tf_op jit(solution)/shard_map/ppermute | solution.py:281
  48.9 2.9 %collective-permute-start.15 = (bf16[1,704,128]{2,1,0:T(8,128)(2,1)S(1)}, bf16[1,704,128]{2,1,0:T(8,128)(2,1)S(1)}, u32[]{:S(2)}, u32[]{:S(2)}) collective-permute-start(bf16[1,704,128]{2,1,0:T(8,128)(2,1)S(1)} %collective-permute-done.12.refs_1_), channel_id=1, source_target_pairs={{0,24},{8,0},{16,8},{24,16},{1,25},{9,1},{17,9},{25,17},{2,26},{10... | collective-permute-start | bytes 540680 | tf_op jit(solution)/shard_map/ppermute | solution.py:272
  53.0 2.9 %pair_stack.3 = (f32[4,2,2,256,128]{4,3,2,1,0:T(8,128)S(1)}, f32[4,256,128]{2,1,0:T(8,128)S(1)}) custom-call(s32[1]{0:T(128)} %bitcast.lower_ref, bf16[4,176,128]{2,1,0:T(8,128)(2,1)S(1)} %copy-done, bf16[2,704,128]{2,1,0:T(8,128)(2,1)S(1)} %get-tuple-element.67.refs_2_.refs_0_, ...), custom_call_target="tpu_custom_call", output_to_operand_aliasing={{0}: (8, {}), {1}: (9, {})} | custom-call | tf_op jit(solution)/shard_map/pair_stack/pallas_call | solution.py:248
  56.0 1.9 %last_stack.2 = (f32[4,2,2,256,128]{4,3,2,1,0:T(8,128)}, f32[4,256,128]{2,1,0:T(8,128)}) custom-call(s32[1]{0:T(128)} %bitcast.lower_ref, bf16[4,176,128]{2,1,0:T(8,128)(2,1)S(1)} %copy-done, bf16[1,704,128]{2,1,0:T(8,128)(2,1)S(1)} %get-tuple-element.76.refs_1_.refs_0_, bf16[1,704,128]{2,1,0:T(8,128)(2,1)S(1)} %collective-permute-done.12.refs_1_, ...), custom_call_target="tpu_custom_call" | custom-call | tf_op jit(solution)/shard_map/last_stack/pallas_call | solution.py:218
  57.9 1.6 %collective-permute-done.14.refs_2_ = bf16[1,704,128]{2,1,0:T(8,128)(2,1)S(1)} collective-permute-done((bf16[1,704,128]{2,1,0:T(8,128)(2,1)S(1)}, bf16[1,704,128]{2,1,0:T(8,128)(2,1)S(1)}, u32[]{:S(2)}, u32[]{:S(2)}) %collective-permute-start.14) | collective-permute-done | bytes 180256 | tf_op jit(solution)/shard_map/ppermute | solution.py:276
  59.5 1.6 %last_stack.3 = f32[4,2,2,256,128]{4,3,2,1,0:T(8,128)} custom-call(s32[1]{0:T(128)} %bitcast.lower_ref, bf16[4,176,128]{2,1,0:T(8,128)(2,1)S(1)} %copy-done, bf16[1,704,128]{2,1,0:T(8,128)(2,1)S(1)} %get-tuple-element.76.refs_1_.refs_0_, bf16[1,704,128]{2,1,0:T(8,128)(2,1)S(1)} %collective-permute-done.12.refs_1_, ...), custom_call_target="tpu_custom_call", output_to_operand_aliasing={{}: (7, {})} | custom-call | tf_op jit(solution)/shard_map/last_stack/pallas_call | solution.py:218
  (34 shorter events, 5.5 us)
Async XLA Ops:
  7.6 4.7 %collective-permute-start = (bf16[4,704,128]{2,1,0:T(8,128)(2,1)S(1)}, bf16[4,704,128]{2,1,0:T(8,128)(2,1)S(1)}, u32[]{:S(2)}, u32[]{:S(2)}) collective-permute-start(bf16[4,704,128]{2,1,0:T(8,128)(2,1)S(1)} %get-tuple-element.45), channel_id=1, source_target_pairs={{0,1},{1,0},{2,3},{3,2},{4,5},{5,4},{6,7},{7,6},{8,9},{9,8},{10,11... | collective-permute-start | bytes 2162696 | tf_op jit(solution)/shard_map/ppermute | solution.py:276
  8.1 10.1 %collective-permute-start.1 = (bf16[1,704,128]{2,1,0:T(8,128)(2,1)S(1)}, bf16[1,704,128]{2,1,0:T(8,128)(2,1)S(1)}, u32[]{:S(2)}, u32[]{:S(2)}) collective-permute-start(bf16[1,704,128]{2,1,0:T(8,128)(2,1)S(1)} %get-tuple-element.47), channel_id=1, source_target_pairs={{0,2},{1,3},{2,4},{3,5},{4,6},{5,7},{6,0},{7,1},{8,10},{9,11},{10,... | collective-permute-start | bytes 540680 | tf_op jit(solution)/shard_map/ppermute | solution.py:281
  10.8 7.4 %collective-permute-start.2 = (bf16[1,704,128]{2,1,0:T(8,128)(2,1)S(1)}, bf16[1,704,128]{2,1,0:T(8,128)(2,1)S(1)}, u32[]{:S(2)}, u32[]{:S(2)}) collective-permute-start(bf16[1,704,128]{2,1,0:T(8,128)(2,1)S(1)} %get-tuple-element.50.refs_1_), channel_id=1, source_target_pairs={{0,16},{8,24},{16,0},{24,8},{1,17},{9,25},{17,1},{25,9},{2,18},{10... | collective-permute-start | bytes 540680 | tf_op jit(solution)/shard_map/ppermute | solution.py:276
  12.4 24.7 %copy-start = (bf16[4,176,128]{2,1,0:T(8,128)(2,1)S(1)}, bf16[4,176,128]{2,1,0:T(8,128)(2,1)}, u32[]{:S(2)}) copy-start(bf16[4,176,128]{2,1,0:T(8,128)(2,1)} %constant.11.clone.masks_ref) | copy-start | bytes 540676
  12.4 9.6 %collective-permute-start.3 = (bf16[1,704,128]{2,1,0:T(8,128)(2,1)S(1)}, bf16[1,704,128]{2,1,0:T(8,128)(2,1)S(1)}, u32[]{:S(2)}, u32[]{:S(2)}) collective-permute-start(bf16[1,704,128]{2,1,0:T(8,128)(2,1)S(1)} %get-tuple-element.53), channel_id=1, source_target_pairs={{0,2},{1,3},{2,4},{3,5},{4,6},{5,7},{6,0},{7,1},{8,10},{9,11},{10,... | collective-permute-start | bytes 540680 | tf_op jit(solution)/shard_map/ppermute | solution.py:281
  14.0 8.0 %collective-permute-start.4 = (bf16[1,704,128]{2,1,0:T(8,128)(2,1)S(1)}, bf16[1,704,128]{2,1,0:T(8,128)(2,1)S(1)}, u32[]{:S(2)}, u32[]{:S(2)}) collective-permute-start(bf16[1,704,128]{2,1,0:T(8,128)(2,1)S(1)} %get-tuple-element.56.refs_2_.refs_1_), channel_id=1, source_target_pairs={{0,16},{8,24},{16,0},{24,8},{1,17},{9,25},{17,1},{25,9},{2,18},{10... | collective-permute-start | bytes 540680 | tf_op jit(solution)/shard_map/ppermute | solution.py:276
  18.2 8.5 %collective-permute-start.6 = (bf16[1,704,128]{2,1,0:T(8,128)(2,1)S(1)}, bf16[1,704,128]{2,1,0:T(8,128)(2,1)S(1)}, u32[]{:S(2)}, u32[]{:S(2)}) collective-permute-start(bf16[1,704,128]{2,1,0:T(8,128)(2,1)S(1)} %get-tuple-element.60), channel_id=1, source_target_pairs={{0,8},{8,0},{16,24},{24,16},{1,9},{9,1},{17,25},{25,17},{2,10},{10... | collective-permute-start | bytes 540680 | tf_op jit(solution)/shard_map/ppermute | solution.py:276
  19.9 6.8 %collective-permute-start.5 = (bf16[1,704,128]{2,1,0:T(8,128)(2,1)S(1)}, bf16[1,704,128]{2,1,0:T(8,128)(2,1)S(1)}, u32[]{:S(2)}, u32[]{:S(2)}) collective-permute-start(bf16[1,704,128]{2,1,0:T(8,128)(2,1)S(1)} %get-tuple-element.58), channel_id=1, source_target_pairs={{0,6},{1,7},{2,0},{3,1},{4,2},{5,3},{6,4},{7,5},{8,14},{9,15},{10,... | collective-permute-start | bytes 540680 | tf_op jit(solution)/shard_map/ppermute | solution.py:281
  22.1 6.2 %collective-permute-start.7 = (bf16[1,704,128]{2,1,0:T(8,128)(2,1)S(1)}, bf16[1,704,128]{2,1,0:T(8,128)(2,1)S(1)}, u32[]{:S(2)}, u32[]{:S(2)}) collective-permute-start(bf16[1,704,128]{2,1,0:T(8,128)(2,1)S(1)} %get-tuple-element.63), channel_id=1, source_target_pairs={{0,8},{8,0},{16,24},{24,16},{1,9},{9,1},{17,25},{25,17},{2,10},{10... | collective-permute-start | bytes 540680 | tf_op jit(solution)/shard_map/ppermute | solution.py:276
  23.6 6.0 %collective-permute-start.8 = (bf16[1,704,128]{2,1,0:T(8,128)(2,1)S(1)}, bf16[1,704,128]{2,1,0:T(8,128)(2,1)S(1)}, u32[]{:S(2)}, u32[]{:S(2)}) collective-permute-start(bf16[1,704,128]{2,1,0:T(8,128)(2,1)S(1)} %get-tuple-element.65), channel_id=1, source_target_pairs={{0,6},{1,7},{2,0},{3,1},{4,2},{5,3},{6,4},{7,5},{8,14},{9,15},{10,... | collective-permute-start | bytes 540680 | tf_op jit(solution)/shard_map/ppermute | solution.py:281
  25.2 11.3 %collective-permute-start.9 = (bf16[2,704,128]{2,1,0:T(8,128)(2,1)S(1)}, bf16[2,704,128]{2,1,0:T(8,128)(2,1)S(1)}, u32[]{:S(2)}, u32[]{:S(2)}) collective-permute-start(bf16[2,704,128]{2,1,0:T(8,128)(2,1)S(1)} %get-tuple-element.67.refs_2_.refs_0_), channel_id=1, source_target_pairs={{0,16},{8,24},{16,0},{24,8},{1,17},{9,25},{17,1},{25,9},{2,18},{10... | collective-permute-start | bytes 1081352 | tf_op jit(solution)/shard_map/ppermute | solution.py:276
  29.6 12.8 %collective-permute-start.10 = (bf16[2,704,128]{2,1,0:T(8,128)(2,1)S(1)}, bf16[2,704,128]{2,1,0:T(8,128)(2,1)S(1)}, u32[]{:S(2)}, u32[]{:S(2)}) collective-permute-start(bf16[2,704,128]{2,1,0:T(8,128)(2,1)S(1)} %get-tuple-element.73.refs_2_.refs_1_), channel_id=1, source_target_pairs={{0,16},{8,24},{16,0},{24,8},{1,17},{9,25},{17,1},{25,9},{2,18},{10... | collective-permute-start | bytes 1081352 | tf_op jit(solution)/shard_map/ppermute | solution.py:276
  31.1 14.7 %collective-permute-start.11 = (bf16[1,704,128]{2,1,0:T(8,128)(2,1)S(1)}, bf16[1,704,128]{2,1,0:T(8,128)(2,1)S(1)}, u32[]{:S(2)}, u32[]{:S(2)}) collective-permute-start(bf16[1,704,128]{2,1,0:T(8,128)(2,1)S(1)} %get-tuple-element.75), channel_id=1, source_target_pairs={{0,4},{1,5},{2,6},{3,7},{4,0},{5,1},{6,2},{7,3},{8,12},{9,13},{10,... | collective-permute-start | bytes 540680 | tf_op jit(solution)/shard_map/ppermute | solution.py:281
  33.3 15.1 %collective-permute-start.12 = (bf16[1,704,128]{2,1,0:T(8,128)(2,1)S(1)}, bf16[1,704,128]{2,1,0:T(8,128)(2,1)S(1)}, u32[]{:S(2)}, u32[]{:S(2)}) collective-permute-start(bf16[1,704,128]{2,1,0:T(8,128)(2,1)S(1)} %get-tuple-element.77), channel_id=1, source_target_pairs={{0,4},{1,5},{2,6},{3,7},{4,0},{5,1},{6,2},{7,3},{8,12},{9,13},{10,... | collective-permute-start | bytes 540680 | tf_op jit(solution)/shard_map/ppermute | solution.py:281
  36.6 16.5 %collective-permute-start.16 = (bf16[2,704,128]{2,1,0:T(8,128)(2,1)S(1)}, bf16[2,704,128]{2,1,0:T(8,128)(2,1)S(1)}, u32[]{:S(2)}, u32[]{:S(2)}) collective-permute-start(bf16[2,704,128]{2,1,0:T(8,128)(2,1)S(1)} %get-tuple-element.80), channel_id=1, source_target_pairs={{0,8},{8,0},{16,24},{24,16},{1,9},{9,1},{17,25},{25,17},{2,10},{10... | collective-permute-start | bytes 1081352 | tf_op jit(solution)/shard_map/ppermute | solution.py:276
  42.4 10.7 %collective-permute-start.17 = (bf16[2,704,128]{2,1,0:T(8,128)(2,1)S(1)}, bf16[2,704,128]{2,1,0:T(8,128)(2,1)S(1)}, u32[]{:S(2)}, u32[]{:S(2)}) collective-permute-start(bf16[2,704,128]{2,1,0:T(8,128)(2,1)S(1)} %get-tuple-element.81), channel_id=1, source_target_pairs={{0,8},{8,0},{16,24},{24,16},{1,9},{9,1},{17,25},{25,17},{2,10},{10... | collective-permute-start | bytes 1081352 | tf_op jit(solution)/shard_map/ppermute | solution.py:276
  45.8 7.1 %collective-permute-start.13 = (bf16[1,704,128]{2,1,0:T(8,128)(2,1)S(1)}, bf16[1,704,128]{2,1,0:T(8,128)(2,1)S(1)}, u32[]{:S(2)}, u32[]{:S(2)}) collective-permute-start(bf16[1,704,128]{2,1,0:T(8,128)(2,1)S(1)} %get-tuple-element.76.refs_1_.refs_0_), channel_id=1, source_target_pairs={{0,16},{8,24},{16,0},{24,8},{1,17},{9,25},{17,1},{25,9},{2,18},{10... | collective-permute-start | bytes 540680 | tf_op jit(solution)/shard_map/ppermute | solution.py:276
  48.4 7.6 %collective-permute-start.18 = (bf16[1,704,128]{2,1,0:T(8,128)(2,1)S(1)}, bf16[1,704,128]{2,1,0:T(8,128)(2,1)S(1)}, u32[]{:S(2)}, u32[]{:S(2)}) collective-permute-start(bf16[1,704,128]{2,1,0:T(8,128)(2,1)S(1)} %collective-permute-done.12.refs_1_), channel_id=1, source_target_pairs={{0,16},{8,24},{16,0},{24,8},{1,17},{9,25},{17,1},{25,9},{2,18},{10... | collective-permute-start | bytes 540680 | tf_op jit(solution)/shard_map/ppermute | solution.py:276
  48.9 9.0 %collective-permute-start.15 = (bf16[1,704,128]{2,1,0:T(8,128)(2,1)S(1)}, bf16[1,704,128]{2,1,0:T(8,128)(2,1)S(1)}, u32[]{:S(2)}, u32[]{:S(2)}) collective-permute-start(bf16[1,704,128]{2,1,0:T(8,128)(2,1)S(1)} %collective-permute-done.12.refs_1_), channel_id=1, source_target_pairs={{0,24},{8,0},{16,8},{24,16},{1,25},{9,1},{17,9},{25,17},{2,26},{10... | collective-permute-start | bytes 540680 | tf_op jit(solution)/shard_map/ppermute | solution.py:272
  52.9 6.6 %collective-permute-start.14 = (bf16[1,704,128]{2,1,0:T(8,128)(2,1)S(1)}, bf16[1,704,128]{2,1,0:T(8,128)(2,1)S(1)}, u32[]{:S(2)}, u32[]{:S(2)}) collective-permute-start(bf16[1,704,128]{2,1,0:T(8,128)(2,1)S(1)} %get-tuple-element.79), channel_id=1, source_target_pairs={{0,8},{8,0},{16,24},{24,16},{1,9},{9,1},{17,25},{25,17},{2,10},{10... | collective-permute-start | bytes 540680 | tf_op jit(solution)/shard_map/ppermute | solution.py:276

commit v6 on v5

--- a/solution.py
+++ b/solution.py
@@ -45,21 +45,14 @@
         record_copy(step).wait()
         if step + 2 < steps:
             record_copy(step + 2).start()
-        windows = records_ref[step * step_windows : (step + 1) * step_windows]
-        spectra = lax.dot_general(
-            table_ref[...],
-            windows.reshape(step_windows * channels, samples),
-            (((1,), (1,)), ((), ())),
-            preferred_element_type=jnp.float32,
-        )
-        mean_square = jnp.sum(spectra * spectra, axis=0, keepdims=True) * (1.0 / bins)
-        whitened = spectra * (scale / jnp.sqrt(mean_square + EPSILON))
-        for local in range(step_windows):
-            window = step * step_windows + local
+        for window in range(step * step_windows, (step + 1) * step_windows):
+            spectra = lax.dot_general(
+                table_ref[...], records_ref[window], (((1,), (1,)), ((), ())), preferred_element_type=jnp.float32
+            )
+            mean_square = jnp.sum(spectra * spectra, axis=0, keepdims=True) * (1.0 / bins)
+            whitened = spectra * (scale / jnp.sqrt(mean_square + EPSILON))
             for row in range(0, bins, 8):
-                rows_ref[pl.ds(row * window_count + window, 8, stride=window_count), :] = whitened[
-                    row : row + 8, local * channels : (local + 1) * channels
-                ]
+                rows_ref[pl.ds(row * window_count + window, 8, stride=window_count), :] = whitened[row : row + 8]
     place = 0
     for out_ref, count in zip(out_refs, counts):
         rows = out_ref.shape[1]

time: 61.4 us -> 60.9 us (level)
  no operation moved by 1% of the time
where the time goes in v6:
time: 60.9 us; the launch traced here: 60.5 us
  starting transfers between devices  24.9 us (41%)
  waiting for transfers between devices  20 us (33%)
  Pallas kernels  14.8 us (24%)
  between operations  0.79 us (1%)
    ppermute x12, starting transfers between devices, swapped(): lax.ppermute(value, axis, [(source, source ^ bit) for source in range(lax...  11.1 us
    ppermute x6, starting transfers between devices, moved(): lax.ppermute(value, 'tm', [(source, (source + 2 * steps) % count) for sou...  10.9 us
    ppermute x12, waiting for transfers between devices, swapped(): lax.ppermute(value, axis, [(source, source ^ bit) for source in range(lax...  10.2 us
    ppermute x6, waiting for transfers between devices, moved(): lax.ppermute(value, 'tm', [(source, (source + 2 * steps) % count) for sou...  9.75 us
    pallas_call x1, Pallas kernels, whiten(): pl.pallas_call(functools.partial(whiten_kernel, scale, step_windows, coun...  6.46 us
    pallas_call x2, Pallas kernels, pair_stack(): pl.pallas_call(functools.partial(pair_kernel, len(own), len(operands)), g...  4.68 us
    pallas_call x2, Pallas kernels, last_stack(): pl.pallas_call(functools.partial(last_kernel, len(own), finish_far), in_s...  3.5 us
    ppermute x1, starting transfers between devices, shifted(): lax.ppermute(value, 'chan', [(source, (source + steps) % count) for sourc...  2.87 us
  transfers between devices with their start and end apart: 19, of which 9 were waited for; matrix products, arithmetic and copies ran while one was open for 0% of the time, Pallas kernels for 11%

profile of v6, /device:TPU:0, one launch (start us, length us, event | category | flops | bytes accessed | tf_op | source)
XLA Modules:
  0.0 60.5 jit_solution(15295101959168266830)
XLA Ops:
  0.6 6.5 %whiten.1 = (bf16[1,704,128]{2,1,0:T(8,128)(2,1)S(1)}, bf16[1,704,128]{2,1,0:T(8,128)(2,1)S(1)}, bf16[1,704,128]{2,1,0:T(8,128)(2,1)S(1)}, bf16[1,704,128]{2,1,0:T(8,128)(2,1)S(1)}, bf16[4,704,128]{2,1,0:T(8,128)(2,1)S(1)}) custom-call(bf16[44,128,1024]{2,1,0:T(8,128)(2,1)} %records_hbm.1), custom_call_target="tpu_custom_call" | custom-call | tf_op jit(solution)/shard_map/whiten/pallas_call | solution.py:71
  7.6 2.6 %collective-permute-start.1 = (bf16[1,704,128]{2,1,0:T(8,128)(2,1)S(1)}, bf16[1,704,128]{2,1,0:T(8,128)(2,1)S(1)}, u32[]{:S(2)}, u32[]{:S(2)}) collective-permute-start(bf16[1,704,128]{2,1,0:T(8,128)(2,1)S(1)} %get-tuple-element.47), channel_id=1, source_target_pairs={{0,2},{1,3},{2,4},{3,5},{4,6},{5,7},{6,0},{7,1},{8,10},{9,11},{10,... | collective-permute-start | bytes 540680 | tf_op jit(solution)/shard_map/ppermute | solution.py:274
  10.3 1.5 %collective-permute-start.2 = (bf16[1,704,128]{2,1,0:T(8,128)(2,1)S(1)}, bf16[1,704,128]{2,1,0:T(8,128)(2,1)S(1)}, u32[]{:S(2)}, u32[]{:S(2)}) collective-permute-start(bf16[1,704,128]{2,1,0:T(8,128)(2,1)S(1)} %get-tuple-element.50.refs_1_), channel_id=1, source_target_pairs={{0,16},{8,24},{16,0},{24,8},{1,17},{9,25},{17,1},{25,9},{2,18},{10... | collective-permute-start | bytes 540680 | tf_op jit(solution)/shard_map/ppermute | solution.py:269
  11.9 1.6 %collective-permute-start.3 = (bf16[1,704,128]{2,1,0:T(8,128)(2,1)S(1)}, bf16[1,704,128]{2,1,0:T(8,128)(2,1)S(1)}, u32[]{:S(2)}, u32[]{:S(2)}) collective-permute-start(bf16[1,704,128]{2,1,0:T(8,128)(2,1)S(1)} %get-tuple-element.53), channel_id=1, source_target_pairs={{0,2},{1,3},{2,4},{3,5},{4,6},{5,7},{6,0},{7,1},{8,10},{9,11},{10,... | collective-permute-start | bytes 540680 | tf_op jit(solution)/shard_map/ppermute | solution.py:274
  14.1 3.6 %collective-permute-done.1.refs_1_ = bf16[1,704,128]{2,1,0:T(8,128)(2,1)S(1)} collective-permute-done((bf16[1,704,128]{2,1,0:T(8,128)(2,1)S(1)}, bf16[1,704,128]{2,1,0:T(8,128)(2,1)S(1)}, u32[]{:S(2)}, u32[]{:S(2)}) %collective-permute-start.1) | collective-permute-done | bytes 180256 | tf_op jit(solution)/shard_map/ppermute | solution.py:274
  17.7 1.7 %collective-permute-start.6 = (bf16[1,704,128]{2,1,0:T(8,128)(2,1)S(1)}, bf16[1,704,128]{2,1,0:T(8,128)(2,1)S(1)}, u32[]{:S(2)}, u32[]{:S(2)}) collective-permute-start(bf16[1,704,128]{2,1,0:T(8,128)(2,1)S(1)} %get-tuple-element.60), channel_id=1, source_target_pairs={{0,8},{8,0},{16,24},{24,16},{1,9},{9,1},{17,25},{25,17},{2,10},{10... | collective-permute-start | bytes 540680 | tf_op jit(solution)/shard_map/ppermute | solution.py:269
  19.4 2.1 %collective-permute-start.5 = (bf16[1,704,128]{2,1,0:T(8,128)(2,1)S(1)}, bf16[1,704,128]{2,1,0:T(8,128)(2,1)S(1)}, u32[]{:S(2)}, u32[]{:S(2)}) collective-permute-start(bf16[1,704,128]{2,1,0:T(8,128)(2,1)S(1)} %get-tuple-element.58), channel_id=1, source_target_pairs={{0,6},{1,7},{2,0},{3,1},{4,2},{5,3},{6,4},{7,5},{8,14},{9,15},{10,... | collective-permute-start | bytes 540680 | tf_op jit(solution)/shard_map/ppermute | solution.py:274
  21.5 1.5 %collective-permute-start.7 = (bf16[1,704,128]{2,1,0:T(8,128)(2,1)S(1)}, bf16[1,704,128]{2,1,0:T(8,128)(2,1)S(1)}, u32[]{:S(2)}, u32[]{:S(2)}) collective-permute-start(bf16[1,704,128]{2,1,0:T(8,128)(2,1)S(1)} %get-tuple-element.63), channel_id=1, source_target_pairs={{0,8},{8,0},{16,24},{24,16},{1,9},{9,1},{17,25},{25,17},{2,10},{10... | collective-permute-start | bytes 540680 | tf_op jit(solution)/shard_map/ppermute | solution.py:269
  23.1 1.6 %collective-permute-start.8 = (bf16[1,704,128]{2,1,0:T(8,128)(2,1)S(1)}, bf16[1,704,128]{2,1,0:T(8,128)(2,1)S(1)}, u32[]{:S(2)}, u32[]{:S(2)}) collective-permute-start(bf16[1,704,128]{2,1,0:T(8,128)(2,1)S(1)} %get-tuple-element.65), channel_id=1, source_target_pairs={{0,6},{1,7},{2,0},{3,1},{4,2},{5,3},{6,4},{7,5},{8,14},{9,15},{10,... | collective-permute-start | bytes 540680 | tf_op jit(solution)/shard_map/ppermute | solution.py:274
  24.7 1.5 %collective-permute-start.9 = (bf16[2,704,128]{2,1,0:T(8,128)(2,1)S(1)}, bf16[2,704,128]{2,1,0:T(8,128)(2,1)S(1)}, u32[]{:S(2)}, u32[]{:S(2)}) collective-permute-start(bf16[2,704,128]{2,1,0:T(8,128)(2,1)S(1)} %get-tuple-element.67.refs_2_.refs_0_), channel_id=1, source_target_pairs={{0,16},{8,24},{16,0},{24,8},{1,17},{9,25},{17,1},{25,9},{2,18},{10... | collective-permute-start | bytes 1081352 | tf_op jit(solution)/shard_map/ppermute | solution.py:269
  26.2 1.6 %collective-permute-done.7.refs_2_ = bf16[1,704,128]{2,1,0:T(8,128)(2,1)S(1)} collective-permute-done((bf16[1,704,128]{2,1,0:T(8,128)(2,1)S(1)}, bf16[1,704,128]{2,1,0:T(8,128)(2,1)S(1)}, u32[]{:S(2)}, u32[]{:S(2)}) %collective-permute-start.7) | collective-permute-done | bytes 180256 | tf_op jit(solution)/shard_map/ppermute | solution.py:269
  27.8 1.3 %collective-permute-done.8.refs_4_ = bf16[1,704,128]{2,1,0:T(8,128)(2,1)S(1)} collective-permute-done((bf16[1,704,128]{2,1,0:T(8,128)(2,1)S(1)}, bf16[1,704,128]{2,1,0:T(8,128)(2,1)S(1)}, u32[]{:S(2)}, u32[]{:S(2)}) %collective-permute-start.8) | collective-permute-done | bytes 180256 | tf_op jit(solution)/shard_map/ppermute | solution.py:274
  29.0 1.6 %collective-permute-start.10 = (bf16[2,704,128]{2,1,0:T(8,128)(2,1)S(1)}, bf16[2,704,128]{2,1,0:T(8,128)(2,1)S(1)}, u32[]{:S(2)}, u32[]{:S(2)}) collective-permute-start(bf16[2,704,128]{2,1,0:T(8,128)(2,1)S(1)} %get-tuple-element.73.refs_2_.refs_1_), channel_id=1, source_target_pairs={{0,16},{8,24},{16,0},{24,8},{1,17},{9,25},{17,1},{25,9},{2,18},{10... | collective-permute-start | bytes 1081352 | tf_op jit(solution)/shard_map/ppermute | solution.py:269
  30.6 2.2 %collective-permute-start.11 = (bf16[1,704,128]{2,1,0:T(8,128)(2,1)S(1)}, bf16[1,704,128]{2,1,0:T(8,128)(2,1)S(1)}, u32[]{:S(2)}, u32[]{:S(2)}) collective-permute-start(bf16[1,704,128]{2,1,0:T(8,128)(2,1)S(1)} %get-tuple-element.75), channel_id=1, source_target_pairs={{0,4},{1,5},{2,6},{3,7},{4,0},{5,1},{6,2},{7,3},{8,12},{9,13},{10,... | collective-permute-start | bytes 540680 | tf_op jit(solution)/shard_map/ppermute | solution.py:274
  33.5 2.5 %collective-permute-done.9.refs_3_.refs_4_ = bf16[2,704,128]{2,1,0:T(8,128)(2,1)S(1)} collective-permute-done((bf16[2,704,128]{2,1,0:T(8,128)(2,1)S(1)}, bf16[2,704,128]{2,1,0:T(8,128)(2,1)S(1)}, u32[]{:S(2)}, u32[]{:S(2)}) %collective-permute-start.9) | collective-permute-done | bytes 360480 | tf_op jit(solution)/shard_map/ppermute | solution.py:269
  36.6 1.8 %pair_stack.2 = (f32[4,2,2,256,128]{4,3,2,1,0:T(8,128)S(1)}, f32[4,256,128]{2,1,0:T(8,128)S(1)}) custom-call(s32[1]{0:T(128)} %bitcast.lower_ref, bf16[4,176,128]{2,1,0:T(8,128)(2,1)S(1)} %copy-done, bf16[1,704,128]{2,1,0:T(8,128)(2,1)S(1)} %get-tuple-element.69.refs_0_, bf16[1,704,128]{2,1,0:T(8,128)(2,1)S(1)} %get-tuple-element.56.refs_2_.refs_1_, ...), custom_call_target="tpu_custom_call" | custom-call | tf_op jit(solution)/shard_map/pair_stack/pallas_call | solution.py:241
  38.4 3.4 %collective-permute-done.10.refs_3_.refs_5_ = bf16[2,704,128]{2,1,0:T(8,128)(2,1)S(1)} collective-permute-done((bf16[2,704,128]{2,1,0:T(8,128)(2,1)S(1)}, bf16[2,704,128]{2,1,0:T(8,128)(2,1)S(1)}, u32[]{:S(2)}, u32[]{:S(2)}) %collective-permute-start.10) | collective-permute-done | bytes 360480 | tf_op jit(solution)/shard_map/ppermute | solution.py:269
  42.4 2.9 %collective-permute-done.11.refs_1_ = bf16[1,704,128]{2,1,0:T(8,128)(2,1)S(1)} collective-permute-done((bf16[1,704,128]{2,1,0:T(8,128)(2,1)S(1)}, bf16[1,704,128]{2,1,0:T(8,128)(2,1)S(1)}, u32[]{:S(2)}, u32[]{:S(2)}) %collective-permute-start.11) | collective-permute-done | bytes 180256 | tf_op jit(solution)/shard_map/ppermute | solution.py:274
  45.8 2.0 %collective-permute-done.12.refs_1_ = bf16[1,704,128]{2,1,0:T(8,128)(2,1)S(1)} collective-permute-done((bf16[1,704,128]{2,1,0:T(8,128)(2,1)S(1)}, bf16[1,704,128]{2,1,0:T(8,128)(2,1)S(1)}, u32[]{:S(2)}, u32[]{:S(2)}) %collective-permute-start.12) | collective-permute-done | bytes 180256 | tf_op jit(solution)/shard_map/ppermute | solution.py:274
  48.4 2.9 %collective-permute-start.15 = (bf16[1,704,128]{2,1,0:T(8,128)(2,1)S(1)}, bf16[1,704,128]{2,1,0:T(8,128)(2,1)S(1)}, u32[]{:S(2)}, u32[]{:S(2)}) collective-permute-start(bf16[1,704,128]{2,1,0:T(8,128)(2,1)S(1)} %collective-permute-done.12.refs_1_), channel_id=1, source_target_pairs={{0,24},{8,0},{16,8},{24,16},{1,25},{9,1},{17,9},{25,17},{2,26},{10... | collective-permute-start | bytes 540680 | tf_op jit(solution)/shard_map/ppermute | solution.py:265
  52.5 2.9 %pair_stack.3 = (f32[4,2,2,256,128]{4,3,2,1,0:T(8,128)S(1)}, f32[4,256,128]{2,1,0:T(8,128)S(1)}) custom-call(s32[1]{0:T(128)} %bitcast.lower_ref, bf16[4,176,128]{2,1,0:T(8,128)(2,1)S(1)} %copy-done, bf16[2,704,128]{2,1,0:T(8,128)(2,1)S(1)} %get-tuple-element.67.refs_2_.refs_0_, ...), custom_call_target="tpu_custom_call", output_to_operand_aliasing={{0}: (8, {}), {1}: (9, {})} | custom-call | tf_op jit(solution)/shard_map/pair_stack/pallas_call | solution.py:241
  55.4 1.9 %last_stack.2 = (f32[4,2,2,256,128]{4,3,2,1,0:T(8,128)}, f32[4,256,128]{2,1,0:T(8,128)}) custom-call(s32[1]{0:T(128)} %bitcast.lower_ref, bf16[4,176,128]{2,1,0:T(8,128)(2,1)S(1)} %copy-done, bf16[1,704,128]{2,1,0:T(8,128)(2,1)S(1)} %get-tuple-element.76.refs_1_.refs_0_, bf16[1,704,128]{2,1,0:T(8,128)(2,1)S(1)} %collective-permute-done.12.refs_1_, ...), custom_call_target="tpu_custom_call" | custom-call | tf_op jit(solution)/shard_map/last_stack/pallas_call | solution.py:211
  57.4 1.6 %collective-permute-done.14.refs_2_ = bf16[1,704,128]{2,1,0:T(8,128)(2,1)S(1)} collective-permute-done((bf16[1,704,128]{2,1,0:T(8,128)(2,1)S(1)}, bf16[1,704,128]{2,1,0:T(8,128)(2,1)S(1)}, u32[]{:S(2)}, u32[]{:S(2)}) %collective-permute-start.14) | collective-permute-done | bytes 180256 | tf_op jit(solution)/shard_map/ppermute | solution.py:269
  59.0 1.6 %last_stack.3 = f32[4,2,2,256,128]{4,3,2,1,0:T(8,128)} custom-call(s32[1]{0:T(128)} %bitcast.lower_ref, bf16[4,176,128]{2,1,0:T(8,128)(2,1)S(1)} %copy-done, bf16[1,704,128]{2,1,0:T(8,128)(2,1)S(1)} %get-tuple-element.76.refs_1_.refs_0_, bf16[1,704,128]{2,1,0:T(8,128)(2,1)S(1)} %collective-permute-done.12.refs_1_, ...), custom_call_target="tpu_custom_call", output_to_operand_aliasing={{}: (7, {})} | custom-call | tf_op jit(solution)/shard_map/last_stack/pallas_call | solution.py:211
  (34 shorter events, 5.5 us)
Async XLA Ops:
  7.1 4.7 %collective-permute-start = (bf16[4,704,128]{2,1,0:T(8,128)(2,1)S(1)}, bf16[4,704,128]{2,1,0:T(8,128)(2,1)S(1)}, u32[]{:S(2)}, u32[]{:S(2)}) collective-permute-start(bf16[4,704,128]{2,1,0:T(8,128)(2,1)S(1)} %get-tuple-element.45), channel_id=1, source_target_pairs={{0,1},{1,0},{2,3},{3,2},{4,5},{5,4},{6,7},{7,6},{8,9},{9,8},{10,11... | collective-permute-start | bytes 2162696 | tf_op jit(solution)/shard_map/ppermute | solution.py:269
  7.6 10.1 %collective-permute-start.1 = (bf16[1,704,128]{2,1,0:T(8,128)(2,1)S(1)}, bf16[1,704,128]{2,1,0:T(8,128)(2,1)S(1)}, u32[]{:S(2)}, u32[]{:S(2)}) collective-permute-start(bf16[1,704,128]{2,1,0:T(8,128)(2,1)S(1)} %get-tuple-element.47), channel_id=1, source_target_pairs={{0,2},{1,3},{2,4},{3,5},{4,6},{5,7},{6,0},{7,1},{8,10},{9,11},{10,... | collective-permute-start | bytes 540680 | tf_op jit(solution)/shard_map/ppermute | solution.py:274
  10.3 7.4 %collective-permute-start.2 = (bf16[1,704,128]{2,1,0:T(8,128)(2,1)S(1)}, bf16[1,704,128]{2,1,0:T(8,128)(2,1)S(1)}, u32[]{:S(2)}, u32[]{:S(2)}) collective-permute-start(bf16[1,704,128]{2,1,0:T(8,128)(2,1)S(1)} %get-tuple-element.50.refs_1_), channel_id=1, source_target_pairs={{0,16},{8,24},{16,0},{24,8},{1,17},{9,25},{17,1},{25,9},{2,18},{10... | collective-permute-start | bytes 540680 | tf_op jit(solution)/shard_map/ppermute | solution.py:269
  11.9 24.7 %copy-start = (bf16[4,176,128]{2,1,0:T(8,128)(2,1)S(1)}, bf16[4,176,128]{2,1,0:T(8,128)(2,1)}, u32[]{:S(2)}) copy-start(bf16[4,176,128]{2,1,0:T(8,128)(2,1)} %constant.11.clone.masks_ref) | copy-start | bytes 540676
  11.9 9.6 %collective-permute-start.3 = (bf16[1,704,128]{2,1,0:T(8,128)(2,1)S(1)}, bf16[1,704,128]{2,1,0:T(8,128)(2,1)S(1)}, u32[]{:S(2)}, u32[]{:S(2)}) collective-permute-start(bf16[1,704,128]{2,1,0:T(8,128)(2,1)S(1)} %get-tuple-element.53), channel_id=1, source_target_pairs={{0,2},{1,3},{2,4},{3,5},{4,6},{5,7},{6,0},{7,1},{8,10},{9,11},{10,... | collective-permute-start | bytes 540680 | tf_op jit(solution)/shard_map/ppermute | solution.py:274
  13.5 8.0 %collective-permute-start.4 = (bf16[1,704,128]{2,1,0:T(8,128)(2,1)S(1)}, bf16[1,704,128]{2,1,0:T(8,128)(2,1)S(1)}, u32[]{:S(2)}, u32[]{:S(2)}) collective-permute-start(bf16[1,704,128]{2,1,0:T(8,128)(2,1)S(1)} %get-tuple-element.56.refs_2_.refs_1_), channel_id=1, source_target_pairs={{0,16},{8,24},{16,0},{24,8},{1,17},{9,25},{17,1},{25,9},{2,18},{10... | collective-permute-start | bytes 540680 | tf_op jit(solution)/shard_map/ppermute | solution.py:269
  17.7 8.5 %collective-permute-start.6 = (bf16[1,704,128]{2,1,0:T(8,128)(2,1)S(1)}, bf16[1,704,128]{2,1,0:T(8,128)(2,1)S(1)}, u32[]{:S(2)}, u32[]{:S(2)}) collective-permute-start(bf16[1,704,128]{2,1,0:T(8,128)(2,1)S(1)} %get-tuple-element.60), channel_id=1, source_target_pairs={{0,8},{8,0},{16,24},{24,16},{1,9},{9,1},{17,25},{25,17},{2,10},{10... | collective-permute-start | bytes 540680 | tf_op jit(solution)/shard_map/ppermute | solution.py:269
  19.4 6.8 %collective-permute-start.5 = (bf16[1,704,128]{2,1,0:T(8,128)(2,1)S(1)}, bf16[1,704,128]{2,1,0:T(8,128)(2,1)S(1)}, u32[]{:S(2)}, u32[]{:S(2)}) collective-permute-start(bf16[1,704,128]{2,1,0:T(8,128)(2,1)S(1)} %get-tuple-element.58), channel_id=1, source_target_pairs={{0,6},{1,7},{2,0},{3,1},{4,2},{5,3},{6,4},{7,5},{8,14},{9,15},{10,... | collective-permute-start | bytes 540680 | tf_op jit(solution)/shard_map/ppermute | solution.py:274
  21.5 6.2 %collective-permute-start.7 = (bf16[1,704,128]{2,1,0:T(8,128)(2,1)S(1)}, bf16[1,704,128]{2,1,0:T(8,128)(2,1)S(1)}, u32[]{:S(2)}, u32[]{:S(2)}) collective-permute-start(bf16[1,704,128]{2,1,0:T(8,128)(2,1)S(1)} %get-tuple-element.63), channel_id=1, source_target_pairs={{0,8},{8,0},{16,24},{24,16},{1,9},{9,1},{17,25},{25,17},{2,10},{10... | collective-permute-start | bytes 540680 | tf_op jit(solution)/shard_map/ppermute | solution.py:269
  23.1 6.0 %collective-permute-start.8 = (bf16[1,704,128]{2,1,0:T(8,128)(2,1)S(1)}, bf16[1,704,128]{2,1,0:T(8,128)(2,1)S(1)}, u32[]{:S(2)}, u32[]{:S(2)}) collective-permute-start(bf16[1,704,128]{2,1,0:T(8,128)(2,1)S(1)} %get-tuple-element.65), channel_id=1, source_target_pairs={{0,6},{1,7},{2,0},{3,1},{4,2},{5,3},{6,4},{7,5},{8,14},{9,15},{10,... | collective-permute-start | bytes 540680 | tf_op jit(solution)/shard_map/ppermute | solution.py:274
  24.7 11.3 %collective-permute-start.9 = (bf16[2,704,128]{2,1,0:T(8,128)(2,1)S(1)}, bf16[2,704,128]{2,1,0:T(8,128)(2,1)S(1)}, u32[]{:S(2)}, u32[]{:S(2)}) collective-permute-start(bf16[2,704,128]{2,1,0:T(8,128)(2,1)S(1)} %get-tuple-element.67.refs_2_.refs_0_), channel_id=1, source_target_pairs={{0,16},{8,24},{16,0},{24,8},{1,17},{9,25},{17,1},{25,9},{2,18},{10... | collective-permute-start | bytes 1081352 | tf_op jit(solution)/shard_map/ppermute | solution.py:269
  29.0 12.8 %collective-permute-start.10 = (bf16[2,704,128]{2,1,0:T(8,128)(2,1)S(1)}, bf16[2,704,128]{2,1,0:T(8,128)(2,1)S(1)}, u32[]{:S(2)}, u32[]{:S(2)}) collective-permute-start(bf16[2,704,128]{2,1,0:T(8,128)(2,1)S(1)} %get-tuple-element.73.refs_2_.refs_1_), channel_id=1, source_target_pairs={{0,16},{8,24},{16,0},{24,8},{1,17},{9,25},{17,1},{25,9},{2,18},{10... | collective-permute-start | bytes 1081352 | tf_op jit(solution)/shard_map/ppermute | solution.py:269
  30.6 14.7 %collective-permute-start.11 = (bf16[1,704,128]{2,1,0:T(8,128)(2,1)S(1)}, bf16[1,704,128]{2,1,0:T(8,128)(2,1)S(1)}, u32[]{:S(2)}, u32[]{:S(2)}) collective-permute-start(bf16[1,704,128]{2,1,0:T(8,128)(2,1)S(1)} %get-tuple-element.75), channel_id=1, source_target_pairs={{0,4},{1,5},{2,6},{3,7},{4,0},{5,1},{6,2},{7,3},{8,12},{9,13},{10,... | collective-permute-start | bytes 540680 | tf_op jit(solution)/shard_map/ppermute | solution.py:274
  32.8 15.1 %collective-permute-start.12 = (bf16[1,704,128]{2,1,0:T(8,128)(2,1)S(1)}, bf16[1,704,128]{2,1,0:T(8,128)(2,1)S(1)}, u32[]{:S(2)}, u32[]{:S(2)}) collective-permute-start(bf16[1,704,128]{2,1,0:T(8,128)(2,1)S(1)} %get-tuple-element.77), channel_id=1, source_target_pairs={{0,4},{1,5},{2,6},{3,7},{4,0},{5,1},{6,2},{7,3},{8,12},{9,13},{10,... | collective-permute-start | bytes 540680 | tf_op jit(solution)/shard_map/ppermute | solution.py:274
  36.1 16.4 %collective-permute-start.16 = (bf16[2,704,128]{2,1,0:T(8,128)(2,1)S(1)}, bf16[2,704,128]{2,1,0:T(8,128)(2,1)S(1)}, u32[]{:S(2)}, u32[]{:S(2)}) collective-permute-start(bf16[2,704,128]{2,1,0:T(8,128)(2,1)S(1)} %get-tuple-element.80), channel_id=1, source_target_pairs={{0,8},{8,0},{16,24},{24,16},{1,9},{9,1},{17,25},{25,17},{2,10},{10... | collective-permute-start | bytes 1081352 | tf_op jit(solution)/shard_map/ppermute | solution.py:269
  41.8 10.7 %collective-permute-start.17 = (bf16[2,704,128]{2,1,0:T(8,128)(2,1)S(1)}, bf16[2,704,128]{2,1,0:T(8,128)(2,1)S(1)}, u32[]{:S(2)}, u32[]{:S(2)}) collective-permute-start(bf16[2,704,128]{2,1,0:T(8,128)(2,1)S(1)} %get-tuple-element.81), channel_id=1, source_target_pairs={{0,8},{8,0},{16,24},{24,16},{1,9},{9,1},{17,25},{25,17},{2,10},{10... | collective-permute-start | bytes 1081352 | tf_op jit(solution)/shard_map/ppermute | solution.py:269
  45.3 7.1 %collective-permute-start.13 = (bf16[1,704,128]{2,1,0:T(8,128)(2,1)S(1)}, bf16[1,704,128]{2,1,0:T(8,128)(2,1)S(1)}, u32[]{:S(2)}, u32[]{:S(2)}) collective-permute-start(bf16[1,704,128]{2,1,0:T(8,128)(2,1)S(1)} %get-tuple-element.76.refs_1_.refs_0_), channel_id=1, source_target_pairs={{0,16},{8,24},{16,0},{24,8},{1,17},{9,25},{17,1},{25,9},{2,18},{10... | collective-permute-start | bytes 540680 | tf_op jit(solution)/shard_map/ppermute | solution.py:269
  47.8 7.6 %collective-permute-start.18 = (bf16[1,704,128]{2,1,0:T(8,128)(2,1)S(1)}, bf16[1,704,128]{2,1,0:T(8,128)(2,1)S(1)}, u32[]{:S(2)}, u32[]{:S(2)}) collective-permute-start(bf16[1,704,128]{2,1,0:T(8,128)(2,1)S(1)} %collective-permute-done.12.refs_1_), channel_id=1, source_target_pairs={{0,16},{8,24},{16,0},{24,8},{1,17},{9,25},{17,1},{25,9},{2,18},{10... | collective-permute-start | bytes 540680 | tf_op jit(solution)/shard_map/ppermute | solution.py:269
  48.4 9.0 %collective-permute-start.15 = (bf16[1,704,128]{2,1,0:T(8,128)(2,1)S(1)}, bf16[1,704,128]{2,1,0:T(8,128)(2,1)S(1)}, u32[]{:S(2)}, u32[]{:S(2)}) collective-permute-start(bf16[1,704,128]{2,1,0:T(8,128)(2,1)S(1)} %collective-permute-done.12.refs_1_), channel_id=1, source_target_pairs={{0,24},{8,0},{16,8},{24,16},{1,25},{9,1},{17,9},{25,17},{2,26},{10... | collective-permute-start | bytes 540680 | tf_op jit(solution)/shard_map/ppermute | solution.py:265
  52.4 6.6 %collective-permute-start.14 = (bf16[1,704,128]{2,1,0:T(8,128)(2,1)S(1)}, bf16[1,704,128]{2,1,0:T(8,128)(2,1)S(1)}, u32[]{:S(2)}, u32[]{:S(2)}) collective-permute-start(bf16[1,704,128]{2,1,0:T(8,128)(2,1)S(1)} %get-tuple-element.79), channel_id=1, source_target_pairs={{0,8},{8,0},{16,24},{24,16},{1,9},{9,1},{17,25},{25,17},{2,10},{10... | collective-permute-start | bytes 540680 | tf_op jit(solution)/shard_map/ppermute | solution.py:269
